TPU v7x, 512 devices: a whole 4x4x16 slice. The times are simulated.
512 devices in a mesh: depth: 8 (over z_lo), row: 8 (over x, core), col: 8 (over z_hi, y).
Axes of the slice: x: 4, y: 4, z: 16 (z_hi: 2, z_lo: 8; z = z_hi * 8 + z_lo), core: 2. Of those that a mesh axis runs over, the one named last changes fastest.
Arguments:
- inputs: bfloat16 [512, 12288], P(('depth', 'row'), 'col'), may hold values from -6 to 6
- pre_act: bfloat16 [512, 24576], P('col', ('depth', 'row')), may hold values from -8 to 8
- out_grad: bfloat16 [512, 12288], P(('depth', 'row'), 'col'), may hold values from -4 to 4
- w_in: bfloat16 [12288, 24576], P('col', ('depth', 'row')), may hold values from -0.0546875 to 0.0546875
- w_out: bfloat16 [24576, 12288], P(('depth', 'row'), 'col'), may hold values from -0.0390625 to 0.0390625
Outputs:
- grad_inputs: bfloat16 [512, 12288], P(('depth', 'row'), 'col')
- grad_w_in: bfloat16 [12288, 24576], P('col', ('depth', 'row'))
- grad_w_out: bfloat16 [24576, 12288], P(('depth', 'row'), 'col')
All inputs are finite; a program needn't handle non-finite values.
Results may differ from a plain program's by a relative error of at most 0.0049.
Values may be sent and summed in bfloat16 or wider, within the bound.
No kernel may reach another device: no remote copies, remote signals or barrier semaphores. Data moves between devices by JAX's collectives and lax.ppermute only.
A program may use at most 64 MiB of HBM per device.

v0:
```python
import jax
import jax.numpy as jnp
from jax import lax
from jax.sharding import PartitionSpec as P

gelu_coeff = 0.7978845608028654
cubic_coeff = 0.044715


def gelu_parts(pre_act):
    pre_float = pre_act.astype(jnp.float32)
    inner_value = gelu_coeff * (pre_float + cubic_coeff * pre_float * pre_float * pre_float)
    tanh_value = jnp.tanh(inner_value)
    activation = 0.5 * pre_float * (1.0 + tanh_value)
    derivative = 0.5 * (1.0 + tanh_value) + 0.5 * pre_float * (
        1.0 - tanh_value * tanh_value
    ) * gelu_coeff * (1.0 + 3.0 * cubic_coeff * pre_float * pre_float)
    return (activation, derivative)


def on_device(inputs, pre_act, out_grad, w_in, w_out):
    grad_rows, input_rows = (
        lax.all_gather(out_grad, ("depth", "row"), axis=0, tiled=True),
        lax.all_gather(inputs, ("depth", "row"), axis=0, tiled=True),
    )
    hidden_grad = lax.psum_scatter(
        jnp.dot(grad_rows, w_out.T, preferred_element_type=jnp.float32),
        "col",
        scatter_dimension=0,
        tiled=True,
    )
    activation, derivative = gelu_parts(pre_act)
    act_local = activation.astype(jnp.bfloat16)
    delta_local = (hidden_grad * derivative).astype(jnp.bfloat16)
    act_rows, delta_rows = (
        lax.all_gather(act_local, "col", axis=0, tiled=True),
        lax.all_gather(delta_local, "col", axis=0, tiled=True),
    )
    grad_w_out = jnp.dot(act_rows.T, grad_rows, preferred_element_type=jnp.float32).astype(
        jnp.bfloat16
    )
    grad_w_in = jnp.dot(input_rows.T, delta_rows, preferred_element_type=jnp.float32).astype(
        jnp.bfloat16
    )
    grad_inputs = lax.psum_scatter(
        jnp.dot(delta_rows, w_in.T, preferred_element_type=jnp.float32),
        ("depth", "row"),
        scatter_dimension=0,
        tiled=True,
    )
    return (grad_inputs.astype(jnp.bfloat16), grad_w_in, grad_w_out)


def solution(mesh):
    in_specs = (
        P(("depth", "row"), "col"),
        P("col", ("depth", "row")),
        P(("depth", "row"), "col"),
        P("col", ("depth", "row")),
        P(("depth", "row"), "col"),
    )
    out_specs = (P(("depth", "row"), "col"), P("col", ("depth", "row")), P(("depth", "row"), "col"))
    return jax.shard_map(
        on_device, mesh=mesh, in_specs=in_specs, out_specs=out_specs, check_vma=False
    )
```

profile of v0, /device:TPU:24, one launch (start us, length us, event | category | flops | bytes accessed | tf_op | source)
XLA Modules:
  0.0 812.8 jit_solution(11608779097794322926)
XLA Ops:
  7.2 0.0 copy-start
  7.2 0.0 all-gather.3.cloned.1.call-start
  7.2 0.7 all-gather.3.cloned.1.call-update
  7.9 0.0 copy-start.1
  7.9 0.0 reduce-scatter.3.cloned.1.call-start
  8.0 126.8 %all-gather.3.cloned.1.call-done = bf16[512,1536]{1,0:T(8,128)(2,1)} async-done(((bf16[8,1536]{1,0:T(8,128)(2,1)}), bf16[512,1536]{1,0:T(8,128)(2,1)}) %all-gather.3.cloned.1.call-update) | async-done | bytes 1572880 | tf_op jit(solution)/shard_map/all_gather | solution.py:23
  134.8 3.6 fusion.12
  138.4 0.0 reduce-scatter.3.cloned.1.call-update
  138.4 0.0 all-gather.5.cloned.1.call-start
  138.5 0.7 all-gather.5.cloned.1.call-update
  139.1 0.0 reduce-scatter.5.cloned.1.call-start
  139.2 111.8 %reduce-scatter.3.cloned.1.call-done = f32[64,384]{1,0:T(8,128)} async-done(((f32[512,384]{1,0:T(8,128)}), f32[64,384]{1,0:T(8,128)}) %reduce-scatter.3.cloned.1.call-update) | async-done | bytes 98320 | tf_op jit(solution)/shard_map/reduce_scatter | solution.py:26
  251.0 0.0 copy-done.1
  251.0 1.0 fusion.8
  251.9 64.1 %all_gather.13 = bf16[512,384]{1,0:T(8,128)(2,1)S(1)} all-gather(bf16[64,384]{1,0:T(8,128)(2,1)S(1)} %get-tuple-element.7), channel_id=1, replica_groups=mesh['depth'=8,'row'=8,'col'=8] {'col'}, dimensions={0}, use_global_device_ids=true | all-gather | bytes 442368 | tf_op jit(solution)/shard_map/all_gather | solution.py:37
  316.0 0.0 copy-done
  316.0 2.6 fusion.13
  318.7 0.0 reduce-scatter.5.cloned.1.call-update
  318.7 46.3 %all-gather.5.cloned.1.call-done = bf16[512,1536]{1,0:T(8,128)(2,1)} async-done(((bf16[8,1536]{1,0:T(8,128)(2,1)}), bf16[512,1536]{1,0:T(8,128)(2,1)}) %all-gather.5.cloned.1.call-update) | async-done | bytes 1572880 | tf_op jit(solution)/shard_map/all_gather | solution.py:24
  365.0 2.2 fusion
  367.3 1.4 copy.8
  368.7 63.8 %all_gather.15 = bf16[512,384]{1,0:T(8,128)(2,1)S(1)} all-gather(bf16[64,384]{1,0:T(8,128)(2,1)S(1)} %get-tuple-element.6), channel_id=1, replica_groups=mesh['depth'=8,'row'=8,'col'=8] {'col'}, dimensions={0}, use_global_device_ids=true | all-gather | bytes 442368 | tf_op jit(solution)/shard_map/all_gather | solution.py:36
  432.5 3.2 convolution_convert_fusion
  435.7 369.1 %reduce-scatter.5.cloned.1.call-done = f32[8,1536]{1,0:T(8,128)} async-done(((f32[512,1536]{1,0:T(8,128)}), f32[8,1536]{1,0:T(8,128)}) %reduce-scatter.5.cloned.1.call-update) | async-done | bytes 49168 | tf_op jit(solution)/shard_map/reduce_scatter | solution.py:45
  804.8 1.4 convert_element_type.23
Async XLA Ops:
  7.2 308.9 %copy-start = (bf16[1536,384]{1,0:T(8,128)(2,1)S(1)}, bf16[1536,384]{1,0:T(8,128)(2,1)}, u32[]{:S(2)}) copy-start(bf16[1536,384]{1,0:T(8,128)(2,1)} %param.8) | copy-start | bytes 3538948
  7.2 127.6 %all-gather.3.cloned.1.call-start = ((), (), s32[]{:S(2)}) async-start(), calls=%async_computation.2 | async-start | bytes 1597440 | tf_op jit(solution)/shard_map/all_gather | solution.py:23
  7.9 243.0 %copy-start.1 = (bf16[64,384]{1,0:T(8,128)(2,1)S(1)}, bf16[64,384]{1,0:T(8,128)(2,1)}, u32[]{:S(2)}) copy-start(bf16[64,384]{1,0:T(8,128)(2,1)} %param.6) | copy-start | bytes 147460
  7.9 243.0 %reduce-scatter.3.cloned.1.call-start = ((), (), s32[]{:S(2)}) async-start(), calls=%async_computation.3 | async-start | bytes 884736 | tf_op jit(solution)/shard_map/reduce_scatter | solution.py:26
  138.4 226.6 %all-gather.5.cloned.1.call-start = ((), (), s32[]{:S(2)}) async-start(), calls=%async_computation.5 | async-start | bytes 1597440 | tf_op jit(solution)/shard_map/all_gather | solution.py:24
  139.1 665.7 %reduce-scatter.5.cloned.1.call-start = ((), (), s32[]{:S(2)}) async-start(), calls=%async_computation.4 | async-start | bytes 3194880 | tf_op jit(solution)/shard_map/reduce_scatter | solution.py:45
Sparse Core Ops, SparseCore 0:
  10.2 124.5 all-gather.2
  139.8 111.0 reduce-scatter.2
  253.1 111.8 all-gather.4
  367.7 437.0 reduce-scatter.4
where the time goes:
time: 813 us
  waiting for transfers between devices  655 us (81%)
  blocking collectives  128 us (16%)
  between operations  13.8 us (2%)
  matrix products  11.7 us (1%)
    reduce_scatter x1, waiting for transfers between devices, on_device(): lax.psum_scatter(jnp.dot(delta_rows, w_in.T, preferred_element_type=jnp.f...  369 us
    all_gather x1, waiting for transfers between devices, on_device(): lax.all_gather(out_grad, ('depth', 'row'), axis=0, tiled=True)  127 us
    reduce_scatter x1, waiting for transfers between devices, on_device(): lax.psum_scatter(jnp.dot(grad_rows, w_out.T, preferred_element_type=jnp.f...  112 us
    all_gather x1, blocking collectives, on_device(): lax.all_gather(delta_local, 'col', axis=0, tiled=True)  64.1 us
    all_gather x1, blocking collectives, on_device(): lax.all_gather(act_local, 'col', axis=0, tiled=True)  63.8 us
    all_gather x1, waiting for transfers between devices, on_device(): lax.all_gather(inputs, ('depth', 'row'), axis=0, tiled=True)  46.3 us
  transfers between devices with their start and end apart: 4, of which 4 were waited for; matrix products, arithmetic and copies ran while one was open for 1% of the time, Pallas kernels for 0%

commit v1 on v0

v1 whole, which is shorter than its diff:
```python
import jax
import jax.numpy as jnp
from jax import lax
from jax.sharding import Mesh, PartitionSpec as P

gelu_coeff = 0.7978845608028654
cubic_coeff = 0.044715
bf16 = jnp.bfloat16
f32 = jnp.float32


def gelu_parts(pre_act):
    pre_float = pre_act.astype(jnp.float32)
    inner_value = gelu_coeff * (pre_float + cubic_coeff * pre_float * pre_float * pre_float)
    tanh_value = jnp.tanh(inner_value)
    activation = 0.5 * pre_float * (1.0 + tanh_value)
    derivative = 0.5 * (1.0 + tanh_value) + 0.5 * pre_float * (
        1.0 - tanh_value * tanh_value
    ) * gelu_coeff * (1.0 + 3.0 * cubic_coeff * pre_float * pre_float)
    return (activation, derivative)


def spread(value, axis, size):
    copies = jnp.broadcast_to(value[None], (size,) + value.shape)
    return lax.all_to_all(copies, axis, 0, 0)


def swap(value, axis):
    return lax.ppermute(value, axis, [(0, 1), (1, 0)])


def dot_rows(rows, weights):
    return lax.dot_general(rows, weights, (((1,), (1,)), ((), ())), preferred_element_type=f32)


def dot_tokens(left, right):
    return lax.dot_general(left, right, (((0,), (0,)), ((), ())), preferred_element_type=f32)


def on_device(inputs, pre_act, out_grad, w_in, w_out):
    core = lax.axis_index("c")
    half = lax.axis_index("h")
    D = out_grad.shape[1]
    F = w_out.shape[0]

    both = spread(jnp.stack([out_grad, inputs]), "z", 8)
    grad_z = both[:, 0].reshape(64, D)
    input_z = both[:, 1].reshape(64, D)
    input_rows = lax.all_gather(input_z, ("x", "c"), axis=0, tiled=True)
    grad_own = spread(grad_z, "x", 4).reshape(256, D)
    grad_sib = swap(grad_own, "c")

    part_own = dot_rows(grad_own, w_out).reshape(4, 2, 4, 8, F)
    part_sib = dot_rows(grad_sib, w_out).reshape(4, 2, 4, 8, F)
    parts = jnp.stack([part_own, part_sib], axis=3).transpose(2, 1, 0, 3, 4, 5).astype(bf16)
    parts = lax.all_to_all(parts.reshape(4, 128, F), "y", 0, 0)
    share = jnp.sum(parts.astype(f32), axis=0)

    pre_parts = pre_act.reshape(4, 2, 8, F)
    pre_rel = jnp.where(core == 0, pre_parts, pre_parts[:, ::-1]).reshape(64, F)
    other = swap(jnp.concatenate([share.astype(bf16), pre_rel]), "h")
    hidden_grad = share + other[:128].astype(f32)
    pre_other = other[128:]
    pre_all = jnp.concatenate(
        [jnp.where(half == 0, pre_rel, pre_other), jnp.where(half == 0, pre_other, pre_rel)]
    )
    activation, derivative = gelu_parts(pre_all)
    delta = (hidden_grad * derivative).astype(bf16)
    act = activation.astype(bf16)

    cols = spread(jnp.stack([delta, act]), "y", 4)
    cols = cols.reshape(4, 2, 2, 4, 2, 8, F).transpose(1, 4, 3, 2, 0, 5, 6)
    delta_rel = cols[0].reshape(2, 256, F)
    act_rel = cols[1].reshape(2, 256, F)

    to_sib = dot_rows(delta_rel[1], w_in).astype(bf16)
    from_sib = swap(to_sib, "c")
    own = dot_rows(delta_rel[0], w_in) + from_sib.astype(f32)
    by_x = lax.all_to_all(own.astype(bf16).reshape(4, 64, D), "x", 0, 0)
    own = jnp.sum(by_x.astype(f32), axis=0)
    by_z = lax.all_to_all(own.astype(bf16).reshape(8, 8, D), "z", 0, 0)
    grad_inputs = jnp.sum(by_z.astype(f32), axis=0).astype(bf16)

    grad_w_out = dot_tokens(act_rel[0], grad_own) + dot_tokens(act_rel[1], grad_sib)
    delta_abs = jnp.where(core == 0, delta_rel, delta_rel[::-1])
    delta_abs = delta_abs.reshape(2, 4, 64, F).transpose(1, 0, 2, 3).reshape(512, F)
    grad_w_in = dot_tokens(input_rows, delta_abs)
    return (grad_inputs, grad_w_in.astype(bf16), grad_w_out.astype(bf16))


def solution(mesh):
    fine = Mesh(mesh.devices.reshape(8, 4, 2, 2, 4), ("z", "x", "c", "h", "y"))
    rows, cols = ("z", "x", "c"), ("h", "y")
    in_specs = (P(rows, cols), P(cols, rows), P(rows, cols), P(cols, rows), P(rows, cols))
    out_specs = (P(rows, cols), P(cols, rows), P(rows, cols))
    return jax.shard_map(
        on_device, mesh=fine, in_specs=in_specs, out_specs=out_specs, check_vma=False
    )
```

time: 813 us -> 175 us (0.22)
  the two profiles are of different devices: /device:TPU:24 before, /device:TPU:8 now
where the time goes in v1:
time: 175 us; the launch traced here: 174 us
  waiting for transfers between devices  54.7 us (31%)
  blocking collectives  49.1 us (28%)
  starting transfers between devices  35.3 us (20%)
  between operations  14.3 us (8%)
  matrix products  8.77 us (5%)
  other arithmetic  6.14 us (4%)
  local copies, waits for them, and re-layouts  5.69 us (3%)
    all_to_all x2, blocking collectives, spread(): return lax.all_to_all(copies, axis, 0, 0)  49.1 us
    ppermute x3, waiting for transfers between devices, swap(): return lax.ppermute(value, axis, [(0, 1), (1, 0)])  19 us
    all_to_all x1, waiting for transfers between devices, on_device(): by_x = lax.all_to_all(own.astype(bf16).reshape(4, 64, D), 'x', 0, 0)  14.1 us
    ppermute x3, starting transfers between devices, swap(): return lax.ppermute(value, axis, [(0, 1), (1, 0)])  12 us
    all_to_all x1, starting transfers between devices, on_device(): by_z = lax.all_to_all(own.astype(bf16).reshape(8, 8, D), 'z', 0, 0)  9.23 us
    all_to_all x1, waiting for transfers between devices, spread(): return lax.all_to_all(copies, axis, 0, 0)  7.31 us
    all_to_all x1, waiting for transfers between devices, on_device(): parts = lax.all_to_all(parts.reshape(4, 128, F), 'y', 0, 0)  6.9 us
    all_to_all x1, waiting for transfers between devices, on_device(): by_z = lax.all_to_all(own.astype(bf16).reshape(8, 8, D), 'z', 0, 0)  6.77 us
  transfers between devices with their start and end apart: 8, of which 7 were waited for; matrix products, arithmetic and copies ran while one was open for 8% of the time, Pallas kernels for 0%

profile of v1, /device:TPU:8, one launch (start us, length us, event | category | flops | bytes accessed | tf_op | source)
XLA Modules:
  0.0 174.1 jit_solution(10640207752521652952)
XLA Ops:
  7.2 0.9 pad_maximum_fusion.2
  8.1 35.4 %all_to_all.30 = bf16[8,2,8,1536]{3,2,1,0:T(8,128)(2,1)S(1)} all-to-all(bf16[8,2,8,1536]{3,2,1,0:T(8,128)(2,1)S(1)} %broadcast_in_dim.8), channel_id=1, replica_groups=mesh['z'=8,'x'=4,'c'=2,'h'=2,'y'=4] {'z'}, dimensions={0} | all-to-all | bytes 786432 | tf_op jit(solution)/shard_map/all_to_all | solution.py:25
  43.5 0.7 slice_bitcast_fusion
  44.3 13.7 %all_to_all.31 = bf16[4,64,1536]{2,1,0:T(8,128)(2,1)S(1)} all-to-all(bf16[4,64,1536]{2,1,0:T(8,128)(2,1)S(1)} %broadcast_in_dim.10), channel_id=1, replica_groups=mesh['z'=8,'x'=4,'c'=2,'h'=2,'y'=4] {'x'}, dimensions={0} | all-to-all | bytes 1572864 | tf_op jit(solution)/shard_map/all_to_all | solution.py:25
  58.0 1.9 %collective-permute-start = (bf16[256,1536]{1,0:T(8,128)(2,1)S(1)}, bf16[256,1536]{1,0:T(8,128)(2,1)S(1)}, u32[]{:S(2)}, u32[]{:S(2)}) collective-permute-start(bf16[256,1536]{1,0:T(8,128)(2,1)S(1)} %bitcast.60), channel_id=1, source_target_pairs={{0,8},{8,0},{1,9},{9,1},{2,10},{10,2},{3,11},{11,3},{4,12},{12,4},... | collective-permute-start | bytes 2359304 | tf_op jit(solution)/shard_map/ppermute | solution.py:29
  59.9 0.6 fusion.6
  60.5 1.6 collective-permute-done
  63.0 0.8 copy.24
  63.8 4.9 %all-to-all-start.2 = ((bf16[4,128,384]{2,1,0:T(8,128)(2,1)}), bf16[4,128,384]{2,1,0:T(8,128)(2,1)S(1)}, u32[]{:S(2)}, u32[]{:S(2)}) async-start(bf16[4,128,384]{2,1,0:T(8,128)(2,1)} %bitcast.10), calls=%async_computation.2 | async-start | bytes 786432 | tf_op jit(solution)/shard_map/all_to_all | solution.py:56
  68.8 6.9 %all-to-all-done.2 = bf16[4,128,384]{2,1,0:T(8,128)(2,1)S(1)} async-done(((bf16[4,128,384]{2,1,0:T(8,128)(2,1)}), bf16[4,128,384]{2,1,0:T(8,128)(2,1)S(1)}, u32[]{:S(2)}, u32[]{:S(2)}) %all-to-all-start.2) | async-done | bytes 393248 | tf_op jit(solution)/shard_map/all_to_all | solution.py:56
  75.8 8.2 %collective-permute-start.1 = (bf16[192,384]{1,0:T(8,128)(2,1)S(1)}, bf16[192,384]{1,0:T(8,128)(2,1)S(1)}, u32[]{:S(2)}, u32[]{:S(2)}) collective-permute-start(bf16[192,384]{1,0:T(8,128)(2,1)S(1)} %pad_maximum_fusion.1), channel_id=1, source_target_pairs={{0,4},{4,0},{1,5},{5,1},{2,6},{6,2},{3,7},{7,3},{8,12},{12,8},{9,1... | collective-permute-start | bytes 442376 | tf_op jit(solution)/shard_map/ppermute | solution.py:29
  84.0 15.1 %collective-permute-done.1 = bf16[192,384]{1,0:T(8,128)(2,1)S(1)} collective-permute-done((bf16[192,384]{1,0:T(8,128)(2,1)S(1)}, bf16[192,384]{1,0:T(8,128)(2,1)S(1)}, u32[]{:S(2)}, u32[]{:S(2)}) %collective-permute-start.1) | collective-permute-done | bytes 147488 | tf_op jit(solution)/shard_map/ppermute | solution.py:29
  99.4 1.0 broadcast_in_dim.22
  100.3 4.9 %all-to-all-start.3 = ((bf16[4,2,128,384]{3,2,1,0:T(8,128)(2,1)}), bf16[4,2,128,384]{3,2,1,0:T(8,128)(2,1)S(1)}, u32[]{:S(2)}, u32[]{:S(2)}) async-start(bf16[4,2,128,384]{3,2,1,0:T(8,128)(2,1)} %broadcast_in_dim.22), calls=%async_computation.3 | async-start | bytes 1572864 | tf_op jit(solution)/shard_map/all_to_all | solution.py:25
  105.3 0.7 all-gather.2.cloned.1.call-update
  106.0 7.3 %all-to-all-done.3 = bf16[4,2,128,384]{3,2,1,0:T(8,128)(2,1)S(1)} async-done(((bf16[4,2,128,384]{3,2,1,0:T(8,128)(2,1)}), bf16[4,2,128,384]{3,2,1,0:T(8,128)(2,1)S(1)}, u32[]{:S(2)}, u32[]{:S(2)}) %all-to-all-start.3) | async-done | bytes 786464 | tf_op jit(solution)/shard_map/all_to_all | solution.py:25
  113.3 0.8 fusion.24
  114.1 0.6 convolution_convert_fusion.1
  114.8 1.9 %collective-permute-start.2 = (bf16[256,1536]{1,0:T(8,128)(2,1)S(1)}, bf16[256,1536]{1,0:T(8,128)(2,1)S(1)}, u32[]{:S(2)}, u32[]{:S(2)}) collective-permute-start(bf16[256,1536]{1,0:T(8,128)(2,1)S(1)} %convolution_convert_fusion.1), channel_id=1, source_target_pairs={{0,8},{8,0},{1,9},{9,1},{2,10},{10,2},{3,11},{11,3},{4,12},{12,4},... | collective-permute-start | bytes 2359304 | tf_op jit(solution)/shard_map/ppermute | solution.py:29
  116.7 2.2 %collective-permute-done.2 = bf16[256,1536]{1,0:T(8,128)(2,1)S(1)} collective-permute-done((bf16[256,1536]{1,0:T(8,128)(2,1)S(1)}, bf16[256,1536]{1,0:T(8,128)(2,1)S(1)}, u32[]{:S(2)}, u32[]{:S(2)}) %collective-permute-start.2) | collective-permute-done | bytes 786464 | tf_op jit(solution)/shard_map/ppermute | solution.py:29
  118.9 1.5 add_convert_fusion
  120.4 4.2 %all-to-all-start.4 = ((bf16[4,64,1536]{2,1,0:T(8,128)(2,1)}), bf16[4,64,1536]{2,1,0:T(8,128)(2,1)}, u32[]{:S(2)}, u32[]{:S(2)}) async-start(bf16[4,64,1536]{2,1,0:T(8,128)(2,1)} %bitcast.21), calls=%async_computation.4 | async-start | bytes 1572864 | tf_op jit(solution)/shard_map/all_to_all | solution.py:79
  124.7 0.8 copy.27
  126.4 14.1 %all-to-all-done.4 = bf16[4,64,1536]{2,1,0:T(8,128)(2,1)} async-done(((bf16[4,64,1536]{2,1,0:T(8,128)(2,1)}), bf16[4,64,1536]{2,1,0:T(8,128)(2,1)}, u32[]{:S(2)}, u32[]{:S(2)}) %all-to-all-start.4) | async-done | bytes 786464 | tf_op jit(solution)/shard_map/all_to_all | solution.py:79
  140.5 2.0 %reduce_sum.34 = bf16[64,1536]{1,0:T(8,128)(2,1)} reduce(bf16[4,64,1536]{2,1,0:T(8,128)(2,1)} %all-to-all-done.4, bf16[]{:T(256)} %constant.26.clone.1), dimensions={0}, to_apply=%region_1.2 | reduce | flops 294912 | bytes 983042 | tf_op jit(solution)/shard_map/reduce_sum | solution.py:80
  142.5 9.2 %all-to-all-start.5 = ((bf16[8,8,1536]{2,1,0:T(8,128)(2,1)}), bf16[8,8,1536]{2,1,0:T(8,128)(2,1)}, u32[]{:S(2)}, u32[]{:S(2)}) async-start(bf16[8,8,1536]{2,1,0:T(8,128)(2,1)} %bitcast.66), calls=%async_computation.5 | async-start | bytes 393216 | tf_op jit(solution)/shard_map/all_to_all | solution.py:81
  151.7 1.3 reverse_select_fusion
  153.0 0.8 copy.28
  153.8 1.5 fusion
  155.4 3.5 %convolution_convert_fusion = bf16[1536,384]{1,0:T(8,128)(2,1)} fusion(bf16[512,1536]{1,0:T(8,128)(2,1)} %all-gather.2.cloned.1.call-done, bf16[512,384]{1,0:T(8,128)(2,1)} %bitcast.73), kind=kOutput, calls=%fused_computation.2 | convolution fusion | flops 604569600 | bytes 3145728 | tf_op jit(solution)/shard_map/dot_general | solution.py:37
  158.9 6.8 %all-to-all-done.5 = bf16[8,8,1536]{2,1,0:T(8,128)(2,1)} async-done(((bf16[8,8,1536]{2,1,0:T(8,128)(2,1)}), bf16[8,8,1536]{2,1,0:T(8,128)(2,1)}, u32[]{:S(2)}, u32[]{:S(2)}) %all-to-all-start.5) | async-done | bytes 196640 | tf_op jit(solution)/shard_map/all_to_all | solution.py:81
  165.6 1.6 reduce_sum.35
  (36 shorter events, 2.4 us)
Async XLA Ops:
  7.2 107.0 %copy-start = (bf16[1536,384]{1,0:T(8,128)(2,1)S(1)}, bf16[1536,384]{1,0:T(8,128)(2,1)}, u32[]{:S(2)}) copy-start(bf16[1536,384]{1,0:T(8,128)(2,1)} %param.8) | copy-start | bytes 3538948
  44.2 15.7 %copy-start.7 = (bf16[384,1536]{1,0:T(8,128)(2,1)S(1)}, bf16[384,1536]{1,0:T(8,128)(2,1)}, u32[]{:S(2)}) copy-start(bf16[384,1536]{1,0:T(8,128)(2,1)} %param.9) | copy-start | bytes 3538948
  58.0 4.8 %copy-start.1 = (bf16[4,64,1536]{2,1,0:T(8,128)(2,1)}, bf16[4,64,1536]{2,1,0:T(8,128)(2,1)S(1)}, u32[]{:S(2)}) copy-start(bf16[4,64,1536]{2,1,0:T(8,128)(2,1)S(1)} %all_to_all.31) | copy-start | bytes 2359300
  58.0 4.2 %collective-permute-start = (bf16[256,1536]{1,0:T(8,128)(2,1)S(1)}, bf16[256,1536]{1,0:T(8,128)(2,1)S(1)}, u32[]{:S(2)}, u32[]{:S(2)}) collective-permute-start(bf16[256,1536]{1,0:T(8,128)(2,1)S(1)} %bitcast.60), channel_id=1, source_target_pairs={{0,8},{8,0},{1,9},{9,1},{2,10},{10,2},{3,11},{11,3},{4,12},{12,4},... | collective-permute-start | bytes 2359304 | tf_op jit(solution)/shard_map/ppermute | solution.py:29
  62.1 0.9 copy-start.4
  62.7 6.0 %copy-start.6 = (bf16[64,384]{1,0:T(8,128)(2,1)S(1)}, bf16[64,384]{1,0:T(8,128)(2,1)}, u32[]{:S(2)}) copy-start(bf16[64,384]{1,0:T(8,128)(2,1)} %param.6) | copy-start | bytes 147460
  63.8 11.8 %all-to-all-start.2 = ((bf16[4,128,384]{2,1,0:T(8,128)(2,1)}), bf16[4,128,384]{2,1,0:T(8,128)(2,1)S(1)}, u32[]{:S(2)}, u32[]{:S(2)}) async-start(bf16[4,128,384]{2,1,0:T(8,128)(2,1)} %bitcast.10), calls=%async_computation.2 | async-start | bytes 786432 | tf_op jit(solution)/shard_map/all_to_all | solution.py:56
  75.8 23.3 %collective-permute-start.1 = (bf16[192,384]{1,0:T(8,128)(2,1)S(1)}, bf16[192,384]{1,0:T(8,128)(2,1)S(1)}, u32[]{:S(2)}, u32[]{:S(2)}) collective-permute-start(bf16[192,384]{1,0:T(8,128)(2,1)S(1)} %pad_maximum_fusion.1), channel_id=1, source_target_pairs={{0,4},{4,0},{1,5},{5,1},{2,6},{6,2},{3,7},{7,3},{8,12},{12,8},{9,1... | collective-permute-start | bytes 442376 | tf_op jit(solution)/shard_map/ppermute | solution.py:29
  100.3 13.0 %all-to-all-start.3 = ((bf16[4,2,128,384]{3,2,1,0:T(8,128)(2,1)}), bf16[4,2,128,384]{3,2,1,0:T(8,128)(2,1)S(1)}, u32[]{:S(2)}, u32[]{:S(2)}) async-start(bf16[4,2,128,384]{3,2,1,0:T(8,128)(2,1)} %broadcast_in_dim.22), calls=%async_computation.3 | async-start | bytes 1572864 | tf_op jit(solution)/shard_map/all_to_all | solution.py:25
  105.3 50.1 %all-gather.2.cloned.1.call-start = ((), (), s32[]{:S(2)}) async-start(), calls=%async_computation.6 | async-start | bytes 1769472 | tf_op jit(solution)/shard_map/all_gather | solution.py:49
  114.8 4.2 %collective-permute-start.2 = (bf16[256,1536]{1,0:T(8,128)(2,1)S(1)}, bf16[256,1536]{1,0:T(8,128)(2,1)S(1)}, u32[]{:S(2)}, u32[]{:S(2)}) collective-permute-start(bf16[256,1536]{1,0:T(8,128)(2,1)S(1)} %convolution_convert_fusion.1), channel_id=1, source_target_pairs={{0,8},{8,0},{1,9},{9,1},{2,10},{10,2},{3,11},{11,3},{4,12},{12,4},... | collective-permute-start | bytes 2359304 | tf_op jit(solution)/shard_map/ppermute | solution.py:29
  120.4 20.1 %all-to-all-start.4 = ((bf16[4,64,1536]{2,1,0:T(8,128)(2,1)}), bf16[4,64,1536]{2,1,0:T(8,128)(2,1)}, u32[]{:S(2)}, u32[]{:S(2)}) async-start(bf16[4,64,1536]{2,1,0:T(8,128)(2,1)} %bitcast.21), calls=%async_computation.4 | async-start | bytes 1572864 | tf_op jit(solution)/shard_map/all_to_all | solution.py:79
  124.6 1.3 copy-start.2
  142.5 23.2 %all-to-all-start.5 = ((bf16[8,8,1536]{2,1,0:T(8,128)(2,1)}), bf16[8,8,1536]{2,1,0:T(8,128)(2,1)}, u32[]{:S(2)}, u32[]{:S(2)}) async-start(bf16[8,8,1536]{2,1,0:T(8,128)(2,1)} %bitcast.66), calls=%async_computation.5 | async-start | bytes 393216 | tf_op jit(solution)/shard_map/all_to_all | solution.py:81
  151.7 2.1 %copy-start.3 = (bf16[1,1,4,2,4,8,384]{6,5,1,2,3,0,4:T(8,128)(2,1)S(1)}, bf16[1,1,4,2,4,8,384]{6,5,1,2,3,0,4:T(8,128)(2,1)}, u32[]{:S(2)}) copy-start(bf16[1,1,4,2,4,8,384]{6,5,1,2,3,0,4:T(8,128)(2,1)} %get-tuple-element.3) | copy-start | bytes 589828
  151.7 2.1 %copy-start.5 = (bf16[256,1536]{1,0:T(8,128)(2,1)S(1)}, bf16[256,1536]{1,0:T(8,128)(2,1)}, u32[]{:S(2)}) copy-start(bf16[256,1536]{1,0:T(8,128)(2,1)} %copy-done.4) | copy-start | bytes 2359300
Sparse Core Ops, SparseCore 0:
  108.2 29.1 all-gather.1

commit v2 on v1

v2 whole, which is shorter than its diff:
```python
import jax
import jax.numpy as jnp
from jax import lax
from jax.sharding import Mesh, PartitionSpec as P

gelu_coeff = 0.7978845608028654
cubic_coeff = 0.044715
bf16 = jnp.bfloat16
f32 = jnp.float32


def gelu_parts(pre_act):
    pre_float = pre_act.astype(jnp.float32)
    inner_value = gelu_coeff * (pre_float + cubic_coeff * pre_float * pre_float * pre_float)
    tanh_value = jnp.tanh(inner_value)
    activation = 0.5 * pre_float * (1.0 + tanh_value)
    derivative = 0.5 * (1.0 + tanh_value) + 0.5 * pre_float * (
        1.0 - tanh_value * tanh_value
    ) * gelu_coeff * (1.0 + 3.0 * cubic_coeff * pre_float * pre_float)
    return (activation, derivative)


def spread(value, axis, size):
    copies = jnp.broadcast_to(value[None], (size,) + value.shape)
    return lax.all_to_all(copies, axis, 0, 0)


def swap(value, axis):
    return lax.ppermute(value, axis, [(0, 1), (1, 0)])


def after(value, other):
    return lax.optimization_barrier((value, other))[0]


def turn(value, axis, step):
    size = lax.axis_size(axis)
    return lax.ppermute(value, axis, [((i + step) % size, i) for i in range(size)])


def flip(value, axis, bit):
    size = lax.axis_size(axis)
    return lax.ppermute(value, axis, [(i, i ^ bit) for i in range(size)])


def join(value, other, axis, bit, at):
    upper = (lax.axis_index(axis) & bit) != 0
    return jnp.stack([jnp.where(upper, other, value), jnp.where(upper, value, other)], axis=at)


def dot_rows(rows, weights):
    return lax.dot_general(rows, weights, (((1,), (1,)), ((), ())), preferred_element_type=f32)


def dot_tokens(left, right):
    return lax.dot_general(left, right, (((0,), (0,)), ((), ())), preferred_element_type=f32)


def on_device(inputs, pre_act, out_grad, w_in, w_out):
    core = lax.axis_index("c")
    half = lax.axis_index("h")
    D = out_grad.shape[1]
    F = w_out.shape[0]

    place = lax.axis_index("x")
    copies = jnp.broadcast_to(out_grad[None], (8,) + out_grad.shape)
    grad_z = lax.all_to_all(copies, "z", 0, 0).reshape(64, D)
    other = after(flip(inputs, "z", 4), grad_z)
    block = join(inputs, other, "z", 4, 0)
    pre_parts = pre_act.reshape(4, 2, 8, F)
    pre_parts = jnp.where((place & 1) != 0, pre_parts.reshape(2, 2, 2, 8, F)[:, ::-1].reshape(4, 2, 8, F), pre_parts)
    pre_parts = jnp.where((place & 2) != 0, pre_parts.reshape(2, 2, 2, 8, F)[::-1].reshape(4, 2, 8, F), pre_parts)
    w_out_sib = swap(w_out, "c")
    pre_mine = jnp.where(core == 0, pre_parts[:, 0], pre_parts[:, 1])
    pre_give = jnp.where(core == 0, pre_parts[:, 1], pre_parts[:, 0])
    pre_rel = jnp.stack([pre_mine, swap(pre_give, "c")]).reshape(64, F)
    grad_own = jnp.concatenate([grad_z] + [flip(grad_z, "x", k) for k in (1, 2, 3)])
    other = after(flip(block, "z", 2), grad_own)
    block = join(block, other, "z", 2, 1)
    grad_sib = swap(grad_own, "c")
    w_in_sib = swap(after(w_in, grad_own), "c")
    parts = jnp.stack([dot_rows(grad_own, w_out), dot_rows(grad_own, w_out_sib)])
    parts = parts.reshape(2, 4, 2, 4, 8, F).transpose(3, 0, 2, 1, 4, 5).astype(bf16)
    parts = parts.reshape(4, 128, F)
    summed = lax.all_to_all(parts, "y", 0, 0)
    share = jnp.sum(summed.astype(f32), axis=0)
    other = after(flip(after(block, parts), "z", 1), share)
    block = join(block, other, "z", 1, 2).reshape(64, D)
    other = swap(jnp.concatenate([share.astype(bf16), pre_rel]), "h")
    hidden_grad = share + other[:128].astype(f32)
    pre_other = other[128:]
    pre_rel, pre_other = pre_rel.reshape(2, 1, 32, F), pre_other.reshape(2, 1, 32, F)
    pre_all = jnp.concatenate([jnp.where(half == 0, pre_rel, pre_other), jnp.where(half == 0, pre_other, pre_rel)], axis=1).reshape(128, F)
    activation, derivative = gelu_parts(pre_all)
    delta = (hidden_grad * derivative).astype(bf16)
    act = activation.astype(bf16)
    other = after(flip(after(block, share), "x", 1), delta)
    block = jnp.concatenate([block, other])
    cols = spread(jnp.stack([delta, act]), "y", 4)
    other = after(flip(after(block, delta), "x", 2), cols)
    block = jnp.concatenate([block, other])
    cols = cols.reshape(4, 2, 2, 2, 4, 8, F).transpose(1, 2, 4, 3, 0, 5, 6).reshape(2, 2, 256, F)
    own = dot_rows(cols[0, 0], w_in) + dot_rows(cols[0, 1], w_in_sib)
    far = swap(cols[:, 1].reshape(512, F), "c").reshape(2, 256, F)
    delta_rel = jnp.stack([cols[0, 0], far[0]])
    act_rel = jnp.stack([cols[1, 0], far[1]])
    own = own.reshape(4, 64, D)
    send = own.astype(bf16)
    block_sib = swap(after(block, send), "c")
    own = own[0] + sum(flip(send[k], "x", k).astype(f32) for k in (1, 2, 3))
    by_z = lax.all_to_all(own.astype(bf16).reshape(8, 8, D), "z", 0, 0)
    grad_inputs = jnp.sum(by_z.astype(f32), axis=0).astype(bf16)
    grad_w_out = dot_tokens(act_rel[0], grad_own) + dot_tokens(act_rel[1], grad_sib)
    grad_w_in = dot_tokens(block, delta_rel[0]) + dot_tokens(block_sib, delta_rel[1])
    return (grad_inputs, grad_w_in.astype(bf16), grad_w_out.astype(bf16))

def solution(mesh):
    fine = Mesh(mesh.devices.reshape(8, 4, 2, 2, 4), ("z", "x", "c", "h", "y"))
    rows, cols = ("z", "x", "c"), ("h", "y")
    in_specs = (P(rows, cols), P(cols, rows), P(rows, cols), P(cols, rows), P(rows, cols))
    out_specs = (P(rows, cols), P(cols, rows), P(rows, cols))
    return jax.shard_map(
        on_device, mesh=fine, in_specs=in_specs, out_specs=out_specs, check_vma=False
    )
```

time: 175 us -> 151 us (0.86)
  starting transfers between devices: 35.3 us -> 93.6 us
  blocking collectives: 49.1 us -> 0 us
  waiting for transfers between devices: 54.7 us -> 29.9 us
  between operations: 14.3 us -> 1.21 us
  matrix products: 8.77 us -> 12.6 us
    all_to_all x2 -> x0, blocking collectives: 49.1 us -> none  [spread(): return lax.all_to_all(copies, axis, 0, 0)]
    ppermute x0 -> x11, starting transfers between devices: none -> 43.1 us  [flip(): return lax.ppermute(value, axis, [(i, i ^ bit) for i in range(size)])]
    all_to_all x2, waiting for transfers between devices: 21 us -> 3.87 us  [the longest x1 3.86 us: on_device(): summed = lax.all_to_all(parts, 'y', 0, 0)]
    ppermute x3 -> x7, starting transfers between devices: 12 us -> 20.7 us  [swap(): return lax.ppermute(value, axis, [(0, 1), (1, 0)])]
    all_to_all x2, starting transfers between devices: 9.1 us -> 17.4 us  [the longest x1 12.5 us: on_device(): grad_z = lax.all_to_all(copies, 'z', 0, 0).reshape(64, D)]
    all_to_all x1, waiting for transfers between devices: 7.31 us -> 0.01 us  [spread(): return lax.all_to_all(copies, axis, 0, 0)]
    ppermute x3 -> x7, waiting for transfers between devices: 19 us -> 14 us  [swap(): return lax.ppermute(value, axis, [(0, 1), (1, 0)])]
    ppermute x0 -> x11, waiting for transfers between devices: none -> 4.07 us  [flip(): return lax.ppermute(value, axis, [(i, i ^ bit) for i in range(size)])]
  transfers between devices with their start and end apart: 8 -> 22, of which waited for: 7 -> 5; matrix products, arithmetic and copies ran while one was open for 8% -> 15% of each run, Pallas kernels for 0% -> 0%
where the time goes in v2:
time: 151 us; the launch traced here: 150 us
  starting transfers between devices  93.6 us (62%)
  waiting for transfers between devices  29.9 us (20%)
  matrix products  12.6 us (8%)
  other arithmetic  7.3 us (5%)
  local copies, waits for them, and re-layouts  5.08 us (3%)
    ppermute x11, starting transfers between devices, flip(): return lax.ppermute(value, axis, [(i, i ^ bit) for i in range(size)])  43.1 us
    ppermute x7, starting transfers between devices, swap(): return lax.ppermute(value, axis, [(0, 1), (1, 0)])  20.7 us
    ppermute x7, waiting for transfers between devices, swap(): return lax.ppermute(value, axis, [(0, 1), (1, 0)])  14 us
    all_to_all x1, starting transfers between devices, on_device(): grad_z = lax.all_to_all(copies, 'z', 0, 0).reshape(64, D)  12.5 us
    all_to_all x1, waiting for transfers between devices, on_device(): by_z = lax.all_to_all(own.astype(bf16).reshape(8, 8, D), 'z', 0, 0)  8.02 us
    dot_general x4, matrix products, dot_tokens(): lax.dot_general(left, right, (((0,), (0,)), ((), ())), preferred_element_...  7.72 us
    all_to_all x1, starting transfers between devices, on_device(): by_z = lax.all_to_all(own.astype(bf16).reshape(8, 8, D), 'z', 0, 0)  7.43 us
    all_to_all x1, starting transfers between devices, spread(): return lax.all_to_all(copies, axis, 0, 0)  4.92 us
  transfers between devices with their start and end apart: 22, of which 5 were waited for; matrix products, arithmetic and copies ran while one was open for 15% of the time, Pallas kernels for 0%

profile of v2, /device:TPU:8, one launch (start us, length us, event | category | flops | bytes accessed | tf_op | source)
XLA Modules:
  0.0 149.8 jit_solution(17747930225894104327)
XLA Ops:
  2.2 12.5 %all-to-all-start = ((bf16[8,8,1536]{2,1,0:T(8,128)(2,1)}), bf16[8,8,1536]{2,1,0:T(8,128)(2,1)S(1)}, u32[]{:S(2)}, u32[]{:S(2)}) async-start(bf16[8,8,1536]{2,1,0:T(8,128)(2,1)} %broadcast_in_dim.4), calls=%async_computation | async-start | bytes 393216 | tf_op jit(solution)/shard_map/all_to_all | solution.py:67
  17.2 1.9 %collective-permute-start.4 = (bf16[4,8,384]{2,1,0:T(8,128)(2,1)S(1)}, bf16[4,8,384]{2,1,0:T(8,128)(2,1)S(1)}, u32[]{:S(2)}, u32[]{:S(2)}) collective-permute-start(bf16[4,8,384]{2,1,0:T(8,128)(2,1)S(1)} %fusion.24), channel_id=1, source_target_pairs={{0,8},{8,0},{1,9},{9,1},{2,10},{10,2},{3,11},{11,3},{4,12},{12,4},... | collective-permute-start | bytes 73736 | tf_op jit(solution)/shard_map/ppermute | solution.py:29
  19.2 2.4 %collective-permute-start.3 = (bf16[384,1536]{1,0:T(8,128)(2,1)}, bf16[384,1536]{1,0:T(8,128)(2,1)S(1)}, u32[]{:S(2)}, u32[]{:S(2)}) collective-permute-start(bf16[384,1536]{1,0:T(8,128)(2,1)} %param.9), channel_id=1, source_target_pairs={{0,8},{8,0},{1,9},{9,1},{2,10},{10,2},{3,11},{11,3},{4,12},{12,4},... | collective-permute-start | bytes 3538952 | tf_op jit(solution)/shard_map/ppermute | solution.py:29
  21.6 7.8 %collective-permute-start.10 = (bf16[8,1536]{1,0:T(8,128)(2,1)}, bf16[8,1536]{1,0:T(8,128)(2,1)S(1)}, u32[]{:S(2)}, u32[]{:S(2)}) collective-permute-start(bf16[8,1536]{1,0:T(8,128)(2,1)} %param.5), channel_id=1, source_target_pairs={{0,256},{64,320},{128,384},{192,448},{256,0},{320,64},{384,128},{4... | collective-permute-start | bytes 73736 | tf_op jit(solution)/shard_map/ppermute | solution.py:43
  29.5 3.9 %collective-permute-start.2 = (bf16[64,1536]{1,0:T(8,128)(2,1)S(1)}, bf16[64,1536]{1,0:T(8,128)(2,1)S(1)}, u32[]{:S(2)}, u32[]{:S(2)}) collective-permute-start(bf16[64,1536]{1,0:T(8,128)(2,1)S(1)} %bitcast.111), channel_id=1, source_target_pairs={{0,48},{16,32},{32,16},{48,0},{1,49},{17,33},{33,17},{49,1},{2,50}... | collective-permute-start | bytes 589832 | tf_op jit(solution)/shard_map/ppermute | solution.py:43
  33.4 3.0 %collective-permute-start.1 = (bf16[64,1536]{1,0:T(8,128)(2,1)S(1)}, bf16[64,1536]{1,0:T(8,128)(2,1)S(1)}, u32[]{:S(2)}, u32[]{:S(2)}) collective-permute-start(bf16[64,1536]{1,0:T(8,128)(2,1)S(1)} %bitcast.112), channel_id=1, source_target_pairs={{0,32},{16,48},{32,0},{48,16},{1,33},{17,49},{33,1},{49,17},{2,34}... | collective-permute-start | bytes 589832 | tf_op jit(solution)/shard_map/ppermute | solution.py:43
  36.4 3.0 %collective-permute-start = (bf16[64,1536]{1,0:T(8,128)(2,1)S(1)}, bf16[64,1536]{1,0:T(8,128)(2,1)S(1)}, u32[]{:S(2)}, u32[]{:S(2)}) collective-permute-start(bf16[64,1536]{1,0:T(8,128)(2,1)S(1)} %bitcast.113), channel_id=1, source_target_pairs={{0,16},{16,0},{32,48},{48,32},{1,17},{17,1},{33,49},{49,33},{2,18}... | collective-permute-start | bytes 589832 | tf_op jit(solution)/shard_map/ppermute | solution.py:43
  40.1 4.3 %collective-permute-start.11 = (bf16[2,8,1536]{2,1,0:T(8,128)(2,1)S(1)}, bf16[2,8,1536]{2,1,0:T(8,128)(2,1)S(1)}, u32[]{:S(2)}, u32[]{:S(2)}) collective-permute-start(bf16[2,8,1536]{2,1,0:T(8,128)(2,1)S(1)} %pad_maximum_fusion.10), channel_id=1, source_target_pairs={{0,128},{64,192},{128,0},{192,64},{256,384},{320,448},{384,256},{4... | collective-permute-start | bytes 147464 | tf_op jit(solution)/shard_map/ppermute | solution.py:43
  46.8 1.9 %collective-permute-start.6 = (bf16[1536,384]{1,0:T(8,128)(2,1)}, bf16[1536,384]{1,0:T(8,128)(2,1)}, u32[]{:S(2)}, u32[]{:S(2)}) collective-permute-start(bf16[1536,384]{1,0:T(8,128)(2,1)} %param.8), channel_id=1, source_target_pairs={{0,8},{8,0},{1,9},{9,1},{2,10},{10,2},{3,11},{11,3},{4,12},{12,4},... | collective-permute-start | bytes 3538952 | tf_op jit(solution)/shard_map/ppermute | solution.py:29
  50.9 4.9 %all-to-all-start.1 = ((bf16[4,128,384]{2,1,0:T(8,128)(2,1)}), bf16[4,128,384]{2,1,0:T(8,128)(2,1)S(1)}, u32[]{:S(2)}, u32[]{:S(2)}) async-start(bf16[4,128,384]{2,1,0:T(8,128)(2,1)} %bitcast.4), calls=%async_computation.1 | async-start | bytes 786432 | tf_op jit(solution)/shard_map/all_to_all | solution.py:85
  55.8 3.4 %collective-permute-start.12 = (bf16[2,2,8,1536]{3,2,1,0:T(8,128)(2,1)S(1)}, bf16[2,2,8,1536]{3,2,1,0:T(8,128)(2,1)S(1)}, u32[]{:S(2)}, u32[]{:S(2)}) collective-permute-start(bf16[2,2,8,1536]{3,2,1,0:T(8,128)(2,1)S(1)} %pad_maximum_fusion.7), channel_id=1, source_target_pairs={{0,64},{64,0},{128,192},{192,128},{256,320},{320,256},{384,448},{4... | collective-permute-start | bytes 294920 | tf_op jit(solution)/shard_map/ppermute | solution.py:43
  59.2 3.9 %all-to-all-done.1 = bf16[4,128,384]{2,1,0:T(8,128)(2,1)S(1)} async-done(((bf16[4,128,384]{2,1,0:T(8,128)(2,1)}), bf16[4,128,384]{2,1,0:T(8,128)(2,1)S(1)}, u32[]{:S(2)}, u32[]{:S(2)}) %all-to-all-start.1) | async-done | bytes 393248 | tf_op jit(solution)/shard_map/all_to_all | solution.py:85
  63.2 8.2 %collective-permute-start.5 = (bf16[192,384]{1,0:T(8,128)(2,1)S(1)}, bf16[192,384]{1,0:T(8,128)(2,1)S(1)}, u32[]{:S(2)}, u32[]{:S(2)}) collective-permute-start(bf16[192,384]{1,0:T(8,128)(2,1)S(1)} %pad_maximum_fusion.6), channel_id=1, source_target_pairs={{0,4},{4,0},{1,5},{5,1},{2,6},{6,2},{3,7},{7,3},{8,12},{12,8},{9,1... | collective-permute-start | bytes 442376 | tf_op jit(solution)/shard_map/ppermute | solution.py:29
  71.4 14.0 %collective-permute-done.5 = bf16[192,384]{1,0:T(8,128)(2,1)S(1)} collective-permute-done((bf16[192,384]{1,0:T(8,128)(2,1)S(1)}, bf16[192,384]{1,0:T(8,128)(2,1)S(1)}, u32[]{:S(2)}, u32[]{:S(2)}) %collective-permute-start.5) | collective-permute-done | bytes 147488 | tf_op jit(solution)/shard_map/ppermute | solution.py:29
  86.7 4.9 %all-to-all-start.2 = ((bf16[4,2,128,384]{3,2,1,0:T(8,128)(2,1)}), bf16[4,2,128,384]{3,2,1,0:T(8,128)(2,1)S(1)}, u32[]{:S(2)}, u32[]{:S(2)}) async-start(bf16[4,2,128,384]{3,2,1,0:T(8,128)(2,1)} %broadcast_in_dim.5), calls=%async_computation.2 | async-start | bytes 1572864 | tf_op jit(solution)/shard_map/all_to_all | solution.py:25
  91.6 3.1 %collective-permute-start.13 = (bf16[64,1536]{1,0:T(8,128)(2,1)S(1)}, bf16[64,1536]{1,0:T(8,128)(2,1)S(1)}, u32[]{:S(2)}, u32[]{:S(2)}) collective-permute-start(bf16[64,1536]{1,0:T(8,128)(2,1)S(1)} %bitcast.107), channel_id=1, source_target_pairs={{0,16},{16,0},{32,48},{48,32},{1,17},{17,1},{33,49},{49,33},{2,18}... | collective-permute-start | bytes 589832 | tf_op jit(solution)/shard_map/ppermute | solution.py:43
  94.8 1.9 %collective-permute-start.17 = (bf16[256,1536]{1,0:T(8,128)(2,1)}, bf16[256,1536]{1,0:T(8,128)(2,1)}, u32[]{:S(2)}, u32[]{:S(2)}) collective-permute-start(bf16[256,1536]{1,0:T(8,128)(2,1)} %pad_maximum_fusion), channel_id=1, source_target_pairs={{0,8},{8,0},{1,9},{9,1},{2,10},{10,2},{3,11},{11,3},{4,12},{12,4},... | collective-permute-start | bytes 2359304 | tf_op jit(solution)/shard_map/ppermute | solution.py:29
  96.7 2.6 %collective-permute-done.13 = bf16[64,1536]{1,0:T(8,128)(2,1)S(1)} collective-permute-done((bf16[64,1536]{1,0:T(8,128)(2,1)S(1)}, bf16[64,1536]{1,0:T(8,128)(2,1)S(1)}, u32[]{:S(2)}, u32[]{:S(2)}) %collective-permute-start.13) | collective-permute-done | bytes 196640 | tf_op jit(solution)/shard_map/ppermute | solution.py:43
  99.3 4.9 %collective-permute-start.14 = (bf16[128,1536]{1,0:T(8,128)(2,1)S(1)}, bf16[128,1536]{1,0:T(8,128)(2,1)S(1)}, u32[]{:S(2)}, u32[]{:S(2)}) collective-permute-start(bf16[128,1536]{1,0:T(8,128)(2,1)S(1)} %pad_maximum_fusion.3), channel_id=1, source_target_pairs={{0,32},{16,48},{32,0},{48,16},{1,33},{17,49},{33,1},{49,17},{2,34}... | collective-permute-start | bytes 1179656 | tf_op jit(solution)/shard_map/ppermute | solution.py:43
  105.1 1.9 %fusion.22 = f32[256,1536]{1,0:T(8,128)S(1)} fusion(bf16[1536,384]{1,0:T(8,128)(2,1)} %param.8, bf16[2,2,256,384]{3,2,1,0:T(8,128)(2,1)S(1)} %bitcast.102), kind=kOutput, calls=%fused_computation.42 | convolution fusion | flops 301989888 | bytes 2949120 | tf_op jit(solution)/shard_map/dot_general | solution.py:52
  107.0 1.9 %fusion.28 = (bf16[256,1536]{1,0:T(8,128)(2,1)S(1)}, f32[256,1536]{1,0:T(8,128)S(1)}) fusion(f32[256,1536]{1,0:T(8,128)S(1)} %fusion.22, bf16[1536,384]{1,0:T(8,128)(2,1)} %collective-permute-done.6, bf16[2,2,256,384]{3,2,1,0:T(8,128)(2,1)S(1)} %bitcast.103), kind=kOutput, calls=%fused_computation.66 | convolution fusion | flops 302776320 | bytes 5308416 | tf_op jit(solution)/shard_map/dot_general | solution.py:52
  108.9 2.9 %collective-permute-start.9 = (bf16[64,1536]{1,0:T(8,128)(2,1)S(1)}, bf16[64,1536]{1,0:T(8,128)(2,1)S(1)}, u32[]{:S(2)}, u32[]{:S(2)}) collective-permute-start(bf16[64,1536]{1,0:T(8,128)(2,1)S(1)} %get-tuple-element.22), channel_id=1, source_target_pairs={{0,48},{16,32},{32,16},{48,0},{1,49},{17,33},{33,17},{49,1},{2,50}... | collective-permute-start | bytes 589832 | tf_op jit(solution)/shard_map/ppermute | solution.py:43
  111.8 2.9 %collective-permute-start.8 = (bf16[64,1536]{1,0:T(8,128)(2,1)S(1)}, bf16[64,1536]{1,0:T(8,128)(2,1)S(1)}, u32[]{:S(2)}, u32[]{:S(2)}) collective-permute-start(bf16[64,1536]{1,0:T(8,128)(2,1)S(1)} %get-tuple-element.23), channel_id=1, source_target_pairs={{0,32},{16,48},{32,0},{48,16},{1,33},{17,49},{33,1},{49,17},{2,34}... | collective-permute-start | bytes 589832 | tf_op jit(solution)/shard_map/ppermute | solution.py:43
  114.7 4.1 %collective-permute-start.7 = (bf16[64,1536]{1,0:T(8,128)(2,1)S(1)}, bf16[64,1536]{1,0:T(8,128)(2,1)S(1)}, u32[]{:S(2)}, u32[]{:S(2)}) collective-permute-start(bf16[64,1536]{1,0:T(8,128)(2,1)S(1)} %get-tuple-element.21), channel_id=1, source_target_pairs={{0,16},{16,0},{32,48},{48,32},{1,17},{17,1},{33,49},{49,33},{2,18}... | collective-permute-start | bytes 589832 | tf_op jit(solution)/shard_map/ppermute | solution.py:43
  119.8 1.9 %collective-permute-start.15 = (bf16[256,1536]{1,0:T(8,128)(2,1)}, bf16[256,1536]{1,0:T(8,128)(2,1)}, u32[]{:S(2)}, u32[]{:S(2)}) collective-permute-start(bf16[256,1536]{1,0:T(8,128)(2,1)} %pad_maximum_fusion.1), channel_id=1, source_target_pairs={{0,8},{8,0},{1,9},{9,1},{2,10},{10,2},{3,11},{11,3},{4,12},{12,4},... | collective-permute-start | bytes 2359304 | tf_op jit(solution)/shard_map/ppermute | solution.py:29
  121.7 1.6 %fusion.21 = f32[1536,384]{1,0:T(8,128)S(1)} fusion(bf16[2,2,256,384]{3,2,1,0:T(8,128)(2,1)S(1)} %bitcast.104, bf16[128,1536]{1,0:T(8,128)(2,1)} %copy-done.1, bf16[64,1536]{1,0:T(8,128)(2,1)} %copy-done, bf16[64,1536]{1,0:T(8,128)(2,1)S(1)} %bitcast.110), kind=kOutput, calls=%fused_computation.41 | convolution fusion | flops 304349184 | bytes 3342336 | tf_op jit(solution)/shard_map/dot_general | solution.py:56
  123.4 2.4 %collective-permute-start.16 = (bf16[512,384]{1,0:T(8,128)(2,1)}, bf16[512,384]{1,0:T(8,128)(2,1)}, u32[]{:S(2)}, u32[]{:S(2)}) collective-permute-start(bf16[512,384]{1,0:T(8,128)(2,1)} %bitcast.40), channel_id=1, source_target_pairs={{0,8},{8,0},{1,9},{9,1},{2,10},{10,2},{3,11},{11,3},{4,12},{12,4},... | collective-permute-start | bytes 1179656 | tf_op jit(solution)/shard_map/ppermute | solution.py:29
  126.6 7.4 %all-to-all-start.3 = ((bf16[8,8,1536]{2,1,0:T(8,128)(2,1)}), bf16[8,8,1536]{2,1,0:T(8,128)(2,1)}, u32[]{:S(2)}, u32[]{:S(2)}) async-start(bf16[8,8,1536]{2,1,0:T(8,128)(2,1)} %fusion.15), calls=%async_computation.3 | async-start | bytes 393216 | tf_op jit(solution)/shard_map/all_to_all | solution.py:111
  134.1 1.8 %fusion.16 = f32[384,1536]{1,0:T(8,128)S(1)} fusion(bf16[256,1536]{1,0:T(8,128)(2,1)} %collective-permute-done.17, bf16[512,384]{1,0:T(8,128)(2,1)} %collective-permute-done.16), kind=kOutput, calls=%fused_computation.30 | convolution fusion | flops 301989888 | bytes 3342336 | tf_op jit(solution)/shard_map/dot_general | solution.py:56
  137.4 2.8 %fusion = bf16[1536,384]{1,0:T(8,128)(2,1)} fusion(f32[1536,384]{1,0:T(8,128)S(1)} %fusion.21, bf16[256,1536]{1,0:T(8,128)(2,1)} %collective-permute-done.15, bf16[512,384]{1,0:T(8,128)(2,1)} %collective-permute-done.16), kind=kOutput, calls=%fused_computation.2 | convolution fusion | flops 303169536 | bytes 4521984 | tf_op jit(solution)/shard_map/dot_general | solution.py:56
  140.2 8.0 %all-to-all-done.3 = bf16[8,8,1536]{2,1,0:T(8,128)(2,1)} async-done(((bf16[8,8,1536]{2,1,0:T(8,128)(2,1)}), bf16[8,8,1536]{2,1,0:T(8,128)(2,1)}, u32[]{:S(2)}, u32[]{:S(2)}) %all-to-all-start.3) | async-done | bytes 196640 | tf_op jit(solution)/shard_map/all_to_all | solution.py:111
  148.2 1.6 %reduce_sum.22 = bf16[8,1536]{1,0:T(8,128)(2,1)} reduce(bf16[8,8,1536]{2,1,0:T(8,128)(2,1)} %all-to-all-done.3, bf16[]{:T(256)} %constant.37.clone.1), dimensions={0}, to_apply=%region_1.2 | reduce | flops 86016 | bytes 221186 | tf_op jit(solution)/shard_map/reduce_sum | solution.py:112
  (72 shorter events, 15.0 us)
Async XLA Ops:
  0.6 48.1 %copy-start.8 = (bf16[384,1536]{1,0:T(8,128)(2,1)S(1)}, bf16[384,1536]{1,0:T(8,128)(2,1)}, u32[]{:S(2)}) copy-start(bf16[384,1536]{1,0:T(8,128)(2,1)} %param.9) | copy-start | bytes 3538948
  2.2 27.3 %all-to-all-start = ((bf16[8,8,1536]{2,1,0:T(8,128)(2,1)}), bf16[8,8,1536]{2,1,0:T(8,128)(2,1)S(1)}, u32[]{:S(2)}, u32[]{:S(2)}) async-start(bf16[8,8,1536]{2,1,0:T(8,128)(2,1)} %broadcast_in_dim.4), calls=%async_computation | async-start | bytes 393216 | tf_op jit(solution)/shard_map/all_to_all | solution.py:67
  17.2 12.2 %collective-permute-start.4 = (bf16[4,8,384]{2,1,0:T(8,128)(2,1)S(1)}, bf16[4,8,384]{2,1,0:T(8,128)(2,1)S(1)}, u32[]{:S(2)}, u32[]{:S(2)}) collective-permute-start(bf16[4,8,384]{2,1,0:T(8,128)(2,1)S(1)} %fusion.24), channel_id=1, source_target_pairs={{0,8},{8,0},{1,9},{9,1},{2,10},{10,2},{3,11},{11,3},{4,12},{12,4},... | collective-permute-start | bytes 73736 | tf_op jit(solution)/shard_map/ppermute | solution.py:29
  19.2 30.2 %collective-permute-start.3 = (bf16[384,1536]{1,0:T(8,128)(2,1)}, bf16[384,1536]{1,0:T(8,128)(2,1)S(1)}, u32[]{:S(2)}, u32[]{:S(2)}) collective-permute-start(bf16[384,1536]{1,0:T(8,128)(2,1)} %param.9), channel_id=1, source_target_pairs={{0,8},{8,0},{1,9},{9,1},{2,10},{10,2},{3,11},{11,3},{4,12},{12,4},... | collective-permute-start | bytes 3538952 | tf_op jit(solution)/shard_map/ppermute | solution.py:29
  21.6 17.8 %collective-permute-start.10 = (bf16[8,1536]{1,0:T(8,128)(2,1)}, bf16[8,1536]{1,0:T(8,128)(2,1)S(1)}, u32[]{:S(2)}, u32[]{:S(2)}) collective-permute-start(bf16[8,1536]{1,0:T(8,128)(2,1)} %param.5), channel_id=1, source_target_pairs={{0,256},{64,320},{128,384},{192,448},{256,0},{320,64},{384,128},{4... | collective-permute-start | bytes 73736 | tf_op jit(solution)/shard_map/ppermute | solution.py:43
  29.5 14.9 %collective-permute-start.2 = (bf16[64,1536]{1,0:T(8,128)(2,1)S(1)}, bf16[64,1536]{1,0:T(8,128)(2,1)S(1)}, u32[]{:S(2)}, u32[]{:S(2)}) collective-permute-start(bf16[64,1536]{1,0:T(8,128)(2,1)S(1)} %bitcast.111), channel_id=1, source_target_pairs={{0,48},{16,32},{32,16},{48,0},{1,49},{17,33},{33,17},{49,1},{2,50}... | collective-permute-start | bytes 589832 | tf_op jit(solution)/shard_map/ppermute | solution.py:43
  33.4 11.0 %collective-permute-start.1 = (bf16[64,1536]{1,0:T(8,128)(2,1)S(1)}, bf16[64,1536]{1,0:T(8,128)(2,1)S(1)}, u32[]{:S(2)}, u32[]{:S(2)}) collective-permute-start(bf16[64,1536]{1,0:T(8,128)(2,1)S(1)} %bitcast.112), channel_id=1, source_target_pairs={{0,32},{16,48},{32,0},{48,16},{1,33},{17,49},{33,1},{49,17},{2,34}... | collective-permute-start | bytes 589832 | tf_op jit(solution)/shard_map/ppermute | solution.py:43
  36.4 9.5 %collective-permute-start = (bf16[64,1536]{1,0:T(8,128)(2,1)S(1)}, bf16[64,1536]{1,0:T(8,128)(2,1)S(1)}, u32[]{:S(2)}, u32[]{:S(2)}) collective-permute-start(bf16[64,1536]{1,0:T(8,128)(2,1)S(1)} %bitcast.113), channel_id=1, source_target_pairs={{0,16},{16,0},{32,48},{48,32},{1,17},{17,1},{33,49},{49,33},{2,18}... | collective-permute-start | bytes 589832 | tf_op jit(solution)/shard_map/ppermute | solution.py:43
  40.1 8.6 %collective-permute-start.11 = (bf16[2,8,1536]{2,1,0:T(8,128)(2,1)S(1)}, bf16[2,8,1536]{2,1,0:T(8,128)(2,1)S(1)}, u32[]{:S(2)}, u32[]{:S(2)}) collective-permute-start(bf16[2,8,1536]{2,1,0:T(8,128)(2,1)S(1)} %pad_maximum_fusion.10), channel_id=1, source_target_pairs={{0,128},{64,192},{128,0},{192,64},{256,384},{320,448},{384,256},{4... | collective-permute-start | bytes 147464 | tf_op jit(solution)/shard_map/ppermute | solution.py:43
  44.4 5.0 %copy-start.2 = (bf16[64,1536]{1,0:T(8,128)(2,1)}, bf16[64,1536]{1,0:T(8,128)(2,1)S(1)}, u32[]{:S(2)}) copy-start(bf16[64,1536]{1,0:T(8,128)(2,1)S(1)} %collective-permute-done.2) | copy-start | bytes 589828
  44.4 5.0 %copy-start.4 = (bf16[64,1536]{1,0:T(8,128)(2,1)}, bf16[64,1536]{1,0:T(8,128)(2,1)S(1)}, u32[]{:S(2)}) copy-start(bf16[64,1536]{1,0:T(8,128)(2,1)S(1)} %collective-permute-done.1) | copy-start | bytes 589828
  45.9 3.5 %copy-start.6 = (bf16[64,1536]{1,0:T(8,128)(2,1)}, bf16[64,1536]{1,0:T(8,128)(2,1)S(1)}, u32[]{:S(2)}) copy-start(bf16[64,1536]{1,0:T(8,128)(2,1)S(1)} %collective-permute-done) | copy-start | bytes 589828
  46.8 60.1 %collective-permute-start.6 = (bf16[1536,384]{1,0:T(8,128)(2,1)}, bf16[1536,384]{1,0:T(8,128)(2,1)}, u32[]{:S(2)}, u32[]{:S(2)}) collective-permute-start(bf16[1536,384]{1,0:T(8,128)(2,1)} %param.8), channel_id=1, source_target_pairs={{0,8},{8,0},{1,9},{9,1},{2,10},{10,2},{3,11},{11,3},{4,12},{12,4},... | collective-permute-start | bytes 3538952 | tf_op jit(solution)/shard_map/ppermute | solution.py:29
  50.9 12.2 %all-to-all-start.1 = ((bf16[4,128,384]{2,1,0:T(8,128)(2,1)}), bf16[4,128,384]{2,1,0:T(8,128)(2,1)S(1)}, u32[]{:S(2)}, u32[]{:S(2)}) async-start(bf16[4,128,384]{2,1,0:T(8,128)(2,1)} %bitcast.4), calls=%async_computation.1 | async-start | bytes 786432 | tf_op jit(solution)/shard_map/all_to_all | solution.py:85
  55.8 15.6 %collective-permute-start.12 = (bf16[2,2,8,1536]{3,2,1,0:T(8,128)(2,1)S(1)}, bf16[2,2,8,1536]{3,2,1,0:T(8,128)(2,1)S(1)}, u32[]{:S(2)}, u32[]{:S(2)}) collective-permute-start(bf16[2,2,8,1536]{3,2,1,0:T(8,128)(2,1)S(1)} %pad_maximum_fusion.7), channel_id=1, source_target_pairs={{0,64},{64,0},{128,192},{192,128},{256,320},{320,256},{384,448},{4... | collective-permute-start | bytes 294920 | tf_op jit(solution)/shard_map/ppermute | solution.py:43
  63.2 22.2 %collective-permute-start.5 = (bf16[192,384]{1,0:T(8,128)(2,1)S(1)}, bf16[192,384]{1,0:T(8,128)(2,1)S(1)}, u32[]{:S(2)}, u32[]{:S(2)}) collective-permute-start(bf16[192,384]{1,0:T(8,128)(2,1)S(1)} %pad_maximum_fusion.6), channel_id=1, source_target_pairs={{0,4},{4,0},{1,5},{5,1},{2,6},{6,2},{3,7},{7,3},{8,12},{12,8},{9,1... | collective-permute-start | bytes 442376 | tf_op jit(solution)/shard_map/ppermute | solution.py:29
  86.7 17.5 %all-to-all-start.2 = ((bf16[4,2,128,384]{3,2,1,0:T(8,128)(2,1)}), bf16[4,2,128,384]{3,2,1,0:T(8,128)(2,1)S(1)}, u32[]{:S(2)}, u32[]{:S(2)}) async-start(bf16[4,2,128,384]{3,2,1,0:T(8,128)(2,1)} %broadcast_in_dim.5), calls=%async_computation.2 | async-start | bytes 1572864 | tf_op jit(solution)/shard_map/all_to_all | solution.py:25
  91.6 7.7 %collective-permute-start.13 = (bf16[64,1536]{1,0:T(8,128)(2,1)S(1)}, bf16[64,1536]{1,0:T(8,128)(2,1)S(1)}, u32[]{:S(2)}, u32[]{:S(2)}) collective-permute-start(bf16[64,1536]{1,0:T(8,128)(2,1)S(1)} %bitcast.107), channel_id=1, source_target_pairs={{0,16},{16,0},{32,48},{48,32},{1,17},{17,1},{33,49},{49,33},{2,18}... | collective-permute-start | bytes 589832 | tf_op jit(solution)/shard_map/ppermute | solution.py:43
  94.8 39.3 %collective-permute-start.17 = (bf16[256,1536]{1,0:T(8,128)(2,1)}, bf16[256,1536]{1,0:T(8,128)(2,1)}, u32[]{:S(2)}, u32[]{:S(2)}) collective-permute-start(bf16[256,1536]{1,0:T(8,128)(2,1)} %pad_maximum_fusion), channel_id=1, source_target_pairs={{0,8},{8,0},{1,9},{9,1},{2,10},{10,2},{3,11},{11,3},{4,12},{12,4},... | collective-permute-start | bytes 2359304 | tf_op jit(solution)/shard_map/ppermute | solution.py:29
  99.3 19.5 %copy-start = (bf16[64,1536]{1,0:T(8,128)(2,1)}, bf16[64,1536]{1,0:T(8,128)(2,1)S(1)}, u32[]{:S(2)}) copy-start(bf16[64,1536]{1,0:T(8,128)(2,1)S(1)} %collective-permute-done.13) | copy-start | bytes 589828
  99.3 19.5 %collective-permute-start.14 = (bf16[128,1536]{1,0:T(8,128)(2,1)S(1)}, bf16[128,1536]{1,0:T(8,128)(2,1)S(1)}, u32[]{:S(2)}, u32[]{:S(2)}) collective-permute-start(bf16[128,1536]{1,0:T(8,128)(2,1)S(1)} %pad_maximum_fusion.3), channel_id=1, source_target_pairs={{0,32},{16,48},{32,0},{48,16},{1,33},{17,49},{33,1},{49,17},{2,34}... | collective-permute-start | bytes 1179656 | tf_op jit(solution)/shard_map/ppermute | solution.py:43
  108.9 14.4 %collective-permute-start.9 = (bf16[64,1536]{1,0:T(8,128)(2,1)S(1)}, bf16[64,1536]{1,0:T(8,128)(2,1)S(1)}, u32[]{:S(2)}, u32[]{:S(2)}) collective-permute-start(bf16[64,1536]{1,0:T(8,128)(2,1)S(1)} %get-tuple-element.22), channel_id=1, source_target_pairs={{0,48},{16,32},{32,16},{48,0},{1,49},{17,33},{33,17},{49,1},{2,50}... | collective-permute-start | bytes 589832 | tf_op jit(solution)/shard_map/ppermute | solution.py:43
  111.8 14.0 %collective-permute-start.8 = (bf16[64,1536]{1,0:T(8,128)(2,1)S(1)}, bf16[64,1536]{1,0:T(8,128)(2,1)S(1)}, u32[]{:S(2)}, u32[]{:S(2)}) collective-permute-start(bf16[64,1536]{1,0:T(8,128)(2,1)S(1)} %get-tuple-element.23), channel_id=1, source_target_pairs={{0,32},{16,48},{32,0},{48,16},{1,33},{17,49},{33,1},{49,17},{2,34}... | collective-permute-start | bytes 589832 | tf_op jit(solution)/shard_map/ppermute | solution.py:43
  114.7 11.1 %collective-permute-start.7 = (bf16[64,1536]{1,0:T(8,128)(2,1)S(1)}, bf16[64,1536]{1,0:T(8,128)(2,1)S(1)}, u32[]{:S(2)}, u32[]{:S(2)}) collective-permute-start(bf16[64,1536]{1,0:T(8,128)(2,1)S(1)} %get-tuple-element.21), channel_id=1, source_target_pairs={{0,16},{16,0},{32,48},{48,32},{1,17},{17,1},{33,49},{49,33},{2,18}... | collective-permute-start | bytes 589832 | tf_op jit(solution)/shard_map/ppermute | solution.py:43
  118.8 1.0 copy-start.1
  119.8 17.6 %collective-permute-start.15 = (bf16[256,1536]{1,0:T(8,128)(2,1)}, bf16[256,1536]{1,0:T(8,128)(2,1)}, u32[]{:S(2)}, u32[]{:S(2)}) collective-permute-start(bf16[256,1536]{1,0:T(8,128)(2,1)} %pad_maximum_fusion.1), channel_id=1, source_target_pairs={{0,8},{8,0},{1,9},{9,1},{2,10},{10,2},{3,11},{11,3},{4,12},{12,4},... | collective-permute-start | bytes 2359304 | tf_op jit(solution)/shard_map/ppermute | solution.py:29
  123.4 10.7 %collective-permute-start.16 = (bf16[512,384]{1,0:T(8,128)(2,1)}, bf16[512,384]{1,0:T(8,128)(2,1)}, u32[]{:S(2)}, u32[]{:S(2)}) collective-permute-start(bf16[512,384]{1,0:T(8,128)(2,1)} %bitcast.40), channel_id=1, source_target_pairs={{0,8},{8,0},{1,9},{9,1},{2,10},{10,2},{3,11},{11,3},{4,12},{12,4},... | collective-permute-start | bytes 1179656 | tf_op jit(solution)/shard_map/ppermute | solution.py:29
  126.6 21.6 %all-to-all-start.3 = ((bf16[8,8,1536]{2,1,0:T(8,128)(2,1)}), bf16[8,8,1536]{2,1,0:T(8,128)(2,1)}, u32[]{:S(2)}, u32[]{:S(2)}) async-start(bf16[8,8,1536]{2,1,0:T(8,128)(2,1)} %fusion.15), calls=%async_computation.3 | async-start | bytes 393216 | tf_op jit(solution)/shard_map/all_to_all | solution.py:111
  134.0 1.8 %copy-start.3 = (bf16[64,1536]{1,0:T(8,128)(2,1)S(1)}, bf16[64,1536]{1,0:T(8,128)(2,1)}, u32[]{:S(2)}) copy-start(bf16[64,1536]{1,0:T(8,128)(2,1)} %copy-done.2) | copy-start | bytes 589828
  134.0 1.8 %copy-start.5 = (bf16[64,1536]{1,0:T(8,128)(2,1)S(1)}, bf16[64,1536]{1,0:T(8,128)(2,1)}, u32[]{:S(2)}) copy-start(bf16[64,1536]{1,0:T(8,128)(2,1)} %copy-done.4) | copy-start | bytes 589828
  134.0 1.8 %copy-start.7 = (bf16[64,1536]{1,0:T(8,128)(2,1)S(1)}, bf16[64,1536]{1,0:T(8,128)(2,1)}, u32[]{:S(2)}) copy-start(bf16[64,1536]{1,0:T(8,128)(2,1)} %copy-done.6) | copy-start | bytes 589828

commit v3 on v2

--- a/solution.py
+++ b/solution.py
@@ -1,6 +1,8 @@
 import jax
 import jax.numpy as jnp
 from jax import lax
+from jax.experimental import pallas as pl
+from jax.experimental.pallas import tpu as pltpu
 from jax.sharding import Mesh, PartitionSpec as P
 
 gelu_coeff = 0.7978845608028654
@@ -54,6 +56,68 @@
 
 def dot_tokens(left, right):
     return lax.dot_general(left, right, (((0,), (0,)), ((), ())), preferred_element_type=f32)
+
+
+def blocks_of_8(value, order):
+    return jnp.concatenate([value[8 * k : 8 * k + 8] for k in order])
+
+
+def call(kernel, out_shape, flops, *operands):
+    size = sum(a.size * a.dtype.itemsize for a in (*operands, *out_shape))
+    return pl.pallas_call(
+        kernel,
+        out_shape=out_shape,
+        in_specs=[pl.BlockSpec(memory_space=pltpu.VMEM)] * len(operands),
+        out_specs=[pl.BlockSpec(memory_space=pltpu.VMEM)] * len(out_shape),
+        compiler_params=pltpu.CompilerParams(vmem_limit_bytes=40 * 1024 * 1024),
+        cost_estimate=pl.CostEstimate(flops=flops, bytes_accessed=size, transcendentals=0),
+    )(*operands)
+
+
+def hidden_kernel(x0, x1, x2, x3, w_own, w_sib, parts):
+    rows = jnp.concatenate([x0[...], x1[...], x2[...], x3[...]])
+    for f, w in enumerate((w_own, w_sib)):
+        product = dot_rows(rows, w[...])
+        for y in range(4):
+            order = [x * 8 + h * 4 + y for h in range(2) for x in range(4)]
+            parts[y, f * 64 : f * 64 + 64, :] = blocks_of_8(product, order).astype(bf16)
+
+
+def input_kernel(cols, w_own, w_sib, own, s1, s2, s3, far):
+    near_rows = jnp.concatenate([cols[y, 0, 0:64, :] for y in range(4)])
+    far_rows = jnp.concatenate([cols[y, 0, 64:128, :] for y in range(4)])
+    width = w_own.shape[0]
+    step = 512
+    for at in range(0, width, step):
+        product = dot_rows(near_rows, w_own[at : at + step, :]) + dot_rows(far_rows, w_sib[at : at + step, :])
+        for x, out in enumerate((own, s1, s2, s3)):
+            order = [y * 8 + h * 4 + x for h in range(2) for y in range(4)]
+            out[:, at : at + step] = blocks_of_8(product, order).astype(out.dtype)
+    for kind in range(2):
+        far[kind] = jnp.concatenate([cols[y, kind, 64:128, :] for y in range(4)])
+
+
+def by_place(near, far):
+    order = [y * 8 + h * 4 + x for x in range(4) for h in range(2) for y in range(4)]
+    return [blocks_of_8(v.astype(f32), order).astype(bf16) for v in (near, far)]
+
+
+def grad_out_kernel(cols, far, grad_own, grad_sib, out):
+    near, other = by_place(jnp.concatenate([cols[y, 1, 0:64, :] for y in range(4)]), far[1])
+    step = 512
+    for at in range(0, grad_own.shape[1], step):
+        out[:, at : at + step] = (
+            dot_tokens(near, grad_own[:, at : at + step]) + dot_tokens(other, grad_sib[:, at : at + step])
+        ).astype(bf16)
+
+
+def grad_in_kernel(cols, far, block_own, block_sib, out):
+    near, other = by_place(jnp.concatenate([cols[y, 0, 0:64, :] for y in range(4)]), far[0])
+    step = 256
+    for at in range(0, block_own.shape[1], step):
+        out[at : at + step, :] = (
+            dot_tokens(block_own[:, at : at + step], near) + dot_tokens(block_sib[:, at : at + step], other)
+        ).astype(bf16)
 
 
 def on_device(inputs, pre_act, out_grad, w_in, w_out):
@@ -74,17 +138,16 @@
     pre_mine = jnp.where(core == 0, pre_parts[:, 0], pre_parts[:, 1])
     pre_give = jnp.where(core == 0, pre_parts[:, 1], pre_parts[:, 0])
     pre_rel = jnp.stack([pre_mine, swap(pre_give, "c")]).reshape(64, F)
-    grad_own = jnp.concatenate([grad_z] + [flip(grad_z, "x", k) for k in (1, 2, 3)])
-    other = after(flip(block, "z", 2), grad_own)
+    grad_x = [grad_z] + [flip(grad_z, "x", k) for k in (1, 2, 3)]
+    other = after(flip(block, "z", 2), grad_x[3])
     block = join(block, other, "z", 2, 1)
-    grad_sib = swap(grad_own, "c")
-    w_in_sib = swap(after(w_in, grad_own), "c")
-    parts = jnp.stack([dot_rows(grad_own, w_out), dot_rows(grad_own, w_out_sib)])
-    parts = parts.reshape(2, 4, 2, 4, 8, F).transpose(3, 0, 2, 1, 4, 5).astype(bf16)
-    parts = parts.reshape(4, 128, F)
+    (parts,) = call(
+        hidden_kernel, [jax.ShapeDtypeStruct((4, 128, F), bf16)], 2 * 512 * D * F, *grad_x, w_out, w_out_sib
+    )
     summed = lax.all_to_all(parts, "y", 0, 0)
     share = jnp.sum(summed.astype(f32), axis=0)
     other = after(flip(after(block, parts), "z", 1), share)
+    w_in_sib = after(swap(after(w_in, parts), "c"), share)
     block = join(block, other, "z", 1, 2).reshape(64, D)
     other = swap(jnp.concatenate([share.astype(bf16), pre_rel]), "h")
     hidden_grad = share + other[:128].astype(f32)
@@ -94,25 +157,40 @@
     activation, derivative = gelu_parts(pre_all)
     delta = (hidden_grad * derivative).astype(bf16)
     act = activation.astype(bf16)
-    other = after(flip(after(block, share), "x", 1), delta)
+    other = flip(after(block, share), "x", 1)
+    delta, act, other = lax.optimization_barrier((delta, act, other))
     block = jnp.concatenate([block, other])
+    grad_own = jnp.concatenate(grad_x)
+    grad_sib = swap(after(grad_own, delta), "c")
     cols = spread(jnp.stack([delta, act]), "y", 4)
-    other = after(flip(after(block, delta), "x", 2), cols)
+    other = flip(after(block, delta), "x", 2)
+    cols = cols.reshape(4, 2, 128, F)
+    piece = jax.ShapeDtypeStruct((64, D), bf16)
+    own, send_1, send_2, send_3, far = call(
+        input_kernel,
+        [jax.ShapeDtypeStruct((64, D), f32), piece, piece, piece, jax.ShapeDtypeStruct((2, 256, F), bf16)],
+        2 * 512 * D * F,
+        cols,
+        w_in,
+        w_in_sib,
+    )
+    other = after(other, own)
     block = jnp.concatenate([block, other])
-    cols = cols.reshape(4, 2, 2, 2, 4, 8, F).transpose(1, 2, 4, 3, 0, 5, 6).reshape(2, 2, 256, F)
-    own = dot_rows(cols[0, 0], w_in) + dot_rows(cols[0, 1], w_in_sib)
-    far = swap(cols[:, 1].reshape(512, F), "c").reshape(2, 256, F)
-    delta_rel = jnp.stack([cols[0, 0], far[0]])
-    act_rel = jnp.stack([cols[1, 0], far[1]])
-    own = own.reshape(4, 64, D)
-    send = own.astype(bf16)
-    block_sib = swap(after(block, send), "c")
-    own = own[0] + sum(flip(send[k], "x", k).astype(f32) for k in (1, 2, 3))
+    far = swap(far, "c")
+    sums = [flip(v, "x", k).astype(f32) for k, v in ((1, send_1), (2, send_2), (3, send_3))]
+    own, far = lax.optimization_barrier((own + sums[0] + sums[1] + sums[2], far))
+    block_sib = swap(after(block, own), "c")
     by_z = lax.all_to_all(own.astype(bf16).reshape(8, 8, D), "z", 0, 0)
+    (grad_w_out,) = call(
+        grad_out_kernel, [jax.ShapeDtypeStruct((F, D), bf16)], 2 * 512 * D * F, cols, far, grad_own, grad_sib
+    )
+    (grad_w_in,) = call(
+        grad_in_kernel, [jax.ShapeDtypeStruct((D, F), bf16)], 2 * 512 * D * F, cols, far, block, block_sib
+    )
+    by_z = after(by_z, grad_w_in)
     grad_inputs = jnp.sum(by_z.astype(f32), axis=0).astype(bf16)
-    grad_w_out = dot_tokens(act_rel[0], grad_own) + dot_tokens(act_rel[1], grad_sib)
-    grad_w_in = dot_tokens(block, delta_rel[0]) + dot_tokens(block_sib, delta_rel[1])
-    return (grad_inputs, grad_w_in.astype(bf16), grad_w_out.astype(bf16))
+    return (grad_inputs, grad_w_in, grad_w_out)
+
 
 def solution(mesh):
     fine = Mesh(mesh.devices.reshape(8, 4, 2, 2, 4), ("z", "x", "c", "h", "y"))

time: 151 us -> 148 us (0.980)
  the two profiles are of different devices: /device:TPU:8 before, /device:TPU:32 now
where the time goes in v3:
time: 148 us; the launch traced here: 146 us
  starting transfers between devices  86.3 us (58%)
  waiting for transfers between devices  38.1 us (26%)
  Pallas kernels  9.04 us (6%)
  other arithmetic  8.38 us (6%)
  local copies, waits for them, and re-layouts  3.39 us (2%)
    ppermute x11, starting transfers between devices, flip(): return lax.ppermute(value, axis, [(i, i ^ bit) for i in range(size)])  40.1 us
    ppermute x7, starting transfers between devices, swap(): return lax.ppermute(value, axis, [(0, 1), (1, 0)])  20.3 us
    ppermute x7, waiting for transfers between devices, swap(): return lax.ppermute(value, axis, [(0, 1), (1, 0)])  13.3 us
    all_to_all x1, starting transfers between devices, on_device(): grad_z = lax.all_to_all(copies, 'z', 0, 0).reshape(64, D)  12.6 us
    all_to_all x1, waiting for transfers between devices, on_device(): by_z = lax.all_to_all(own.astype(bf16).reshape(8, 8, D), 'z', 0, 0)  9.37 us
    pallas_call x4, Pallas kernels, call(): pl.pallas_call(kernel, out_shape=out_shape, in_specs=[pl.BlockSpec(memory...  9.04 us
    all_to_all x1, waiting for transfers between devices, spread(): return lax.all_to_all(copies, axis, 0, 0)  6.62 us
    ppermute x11, waiting for transfers between devices, flip(): return lax.ppermute(value, axis, [(i, i ^ bit) for i in range(size)])  5.8 us
  transfers between devices with their start and end apart: 22, of which 8 were waited for; matrix products, arithmetic and copies ran while one was open for 6% of the time, Pallas kernels for 5%

profile of v3, /device:TPU:32, one launch (start us, length us, event | category | flops | bytes accessed | tf_op | source)
XLA Modules:
  0.0 146.4 jit_solution(11297890970921664216)
XLA Ops:
  2.2 12.6 %all-to-all-start = ((bf16[8,8,1536]{2,1,0:T(8,128)(2,1)}), bf16[8,8,1536]{2,1,0:T(8,128)(2,1)S(1)}, u32[]{:S(2)}, u32[]{:S(2)}) async-start(bf16[8,8,1536]{2,1,0:T(8,128)(2,1)} %broadcast_in_dim.4), calls=%async_computation | async-start | bytes 393216 | tf_op jit(solution)/shard_map/all_to_all | solution.py:131
  14.8 1.9 %collective-permute-start.3 = (bf16[384,1536]{1,0:T(8,128)(2,1)}, bf16[384,1536]{1,0:T(8,128)(2,1)S(1)}, u32[]{:S(2)}, u32[]{:S(2)}) collective-permute-start(bf16[384,1536]{1,0:T(8,128)(2,1)} %w_own.2), channel_id=1, source_target_pairs={{0,8},{8,0},{1,9},{9,1},{2,10},{10,2},{3,11},{11,3},{4,12},{12,4},... | collective-permute-start | bytes 3538952 | tf_op jit(solution)/shard_map/ppermute | solution.py:31
  19.3 2.4 %collective-permute-start.4 = (bf16[4,8,384]{2,1,0:T(8,128)(2,1)S(1)}, bf16[4,8,384]{2,1,0:T(8,128)(2,1)S(1)}, u32[]{:S(2)}, u32[]{:S(2)}) collective-permute-start(bf16[4,8,384]{2,1,0:T(8,128)(2,1)S(1)} %fusion.8), channel_id=1, source_target_pairs={{0,8},{8,0},{1,9},{9,1},{2,10},{10,2},{3,11},{11,3},{4,12},{12,4},... | collective-permute-start | bytes 73736 | tf_op jit(solution)/shard_map/ppermute | solution.py:31
  21.7 7.3 %collective-permute-start.6 = (bf16[8,1536]{1,0:T(8,128)(2,1)S(1)}, bf16[8,1536]{1,0:T(8,128)(2,1)S(1)}, u32[]{:S(2)}, u32[]{:S(2)}) collective-permute-start(bf16[8,1536]{1,0:T(8,128)(2,1)S(1)} %copy-done.13), channel_id=1, source_target_pairs={{0,256},{64,320},{128,384},{192,448},{256,0},{320,64},{384,128},{4... | collective-permute-start | bytes 73736 | tf_op jit(solution)/shard_map/ppermute | solution.py:45
  29.6 2.6 %collective-permute-start = (bf16[64,1536]{1,0:T(8,128)(2,1)S(1)}, bf16[64,1536]{1,0:T(8,128)(2,1)S(1)}, u32[]{:S(2)}, u32[]{:S(2)}) collective-permute-start(bf16[64,1536]{1,0:T(8,128)(2,1)S(1)} %bitcast.71), channel_id=1, source_target_pairs={{0,16},{16,0},{32,48},{48,32},{1,17},{17,1},{33,49},{49,33},{2,18}... | collective-permute-start | bytes 589832 | tf_op jit(solution)/shard_map/ppermute | solution.py:45
  32.2 4.6 %collective-permute-start.1 = (bf16[64,1536]{1,0:T(8,128)(2,1)S(1)}, bf16[64,1536]{1,0:T(8,128)(2,1)S(1)}, u32[]{:S(2)}, u32[]{:S(2)}) collective-permute-start(bf16[64,1536]{1,0:T(8,128)(2,1)S(1)} %bitcast.72), channel_id=1, source_target_pairs={{0,32},{16,48},{32,0},{48,16},{1,33},{17,49},{33,1},{49,17},{2,34}... | collective-permute-start | bytes 589832 | tf_op jit(solution)/shard_map/ppermute | solution.py:45
  36.9 3.2 %collective-permute-start.2 = (bf16[64,1536]{1,0:T(8,128)(2,1)S(1)}, bf16[64,1536]{1,0:T(8,128)(2,1)S(1)}, u32[]{:S(2)}, u32[]{:S(2)}) collective-permute-start(bf16[64,1536]{1,0:T(8,128)(2,1)S(1)} %bitcast.73), channel_id=1, source_target_pairs={{0,48},{16,32},{32,16},{48,0},{1,49},{17,33},{33,17},{49,1},{2,50}... | collective-permute-start | bytes 589832 | tf_op jit(solution)/shard_map/ppermute | solution.py:45
  40.1 4.3 %collective-permute-start.7 = (bf16[2,8,1536]{2,1,0:T(8,128)(2,1)S(1)}, bf16[2,8,1536]{2,1,0:T(8,128)(2,1)S(1)}, u32[]{:S(2)}, u32[]{:S(2)}) collective-permute-start(bf16[2,8,1536]{2,1,0:T(8,128)(2,1)S(1)} %pad_maximum_fusion.9), channel_id=1, source_target_pairs={{0,128},{64,192},{128,0},{192,64},{256,384},{320,448},{384,256},{4... | collective-permute-start | bytes 147464 | tf_op jit(solution)/shard_map/ppermute | solution.py:45
  45.0 2.0 %collective-permute-done.7 = bf16[2,8,1536]{2,1,0:T(8,128)(2,1)S(1)} collective-permute-done((bf16[2,8,1536]{2,1,0:T(8,128)(2,1)S(1)}, bf16[2,8,1536]{2,1,0:T(8,128)(2,1)S(1)}, u32[]{:S(2)}, u32[]{:S(2)}) %collective-permute-start.7) | collective-permute-done | bytes 49184 | tf_op jit(solution)/shard_map/ppermute | solution.py:45
  47.9 1.7 %shard_map.76 = bf16[4,128,384]{2,1,0:T(8,128)(2,1)} custom-call(bf16[64,1536]{1,0:T(8,128)(2,1)S(1)} %bitcast.74, bf16[64,1536]{1,0:T(8,128)(2,1)S(1)} %collective-permute-done.x1, bf16[64,1536]{1,0:T(8,128)(2,1)S(1)} %collective-permute-done.1.x2, bf16[64,1536]{1,0:T(8,128)(2,1)S(1)} %collective-permute-done.2.x3, bf16[384,1536]{1,0:T(8,128)(2,1)S(1)} %copy-done, ...), custom_call_target="tpu_custom_call" | custom-call | flops 603979776 | bytes 3538944 | tf_op jit(solution)/shard_map/pallas_call | solution.py:67
  49.7 4.6 %all-to-all-start.1 = ((bf16[4,128,384]{2,1,0:T(8,128)(2,1)}), bf16[4,128,384]{2,1,0:T(8,128)(2,1)S(1)}, u32[]{:S(2)}, u32[]{:S(2)}) async-start(bf16[4,128,384]{2,1,0:T(8,128)(2,1)} %shard_map.76), calls=%async_computation.1 | async-start | bytes 786432 | tf_op jit(solution)/shard_map/all_to_all | solution.py:147
  55.1 2.5 %collective-permute-start.8 = (bf16[2,2,8,1536]{3,2,0,1:T(8,128)(2,1)S(1)}, bf16[2,2,8,1536]{3,2,0,1:T(8,128)(2,1)S(1)}, u32[]{:S(2)}, u32[]{:S(2)}) collective-permute-start(bf16[2,2,8,1536]{3,2,0,1:T(8,128)(2,1)S(1)} %pad_maximum_fusion.6), channel_id=1, source_target_pairs={{0,64},{64,0},{128,192},{192,128},{256,320},{320,256},{384,448},{4... | collective-permute-start | bytes 294920 | tf_op jit(solution)/shard_map/ppermute | solution.py:45
  57.6 1.9 %collective-permute-start.10 = (bf16[1536,384]{1,0:T(8,128)(2,1)S(1)}, bf16[1536,384]{1,0:T(8,128)(2,1)}, u32[]{:S(2)}, u32[]{:S(2)}) collective-permute-start(bf16[1536,384]{1,0:T(8,128)(2,1)S(1)} %copy-done.1), channel_id=1, source_target_pairs={{0,8},{8,0},{1,9},{9,1},{2,10},{10,2},{3,11},{11,3},{4,12},{12,4},... | collective-permute-start | bytes 3538952 | tf_op jit(solution)/shard_map/ppermute | solution.py:31
  59.6 3.0 %all-to-all-done.1 = bf16[4,128,384]{2,1,0:T(8,128)(2,1)S(1)} async-done(((bf16[4,128,384]{2,1,0:T(8,128)(2,1)}), bf16[4,128,384]{2,1,0:T(8,128)(2,1)S(1)}, u32[]{:S(2)}, u32[]{:S(2)}) %all-to-all-start.1) | async-done | bytes 393248 | tf_op jit(solution)/shard_map/all_to_all | solution.py:147
  62.6 8.2 %collective-permute-start.5 = (bf16[192,384]{1,0:T(8,128)(2,1)S(1)}, bf16[192,384]{1,0:T(8,128)(2,1)S(1)}, u32[]{:S(2)}, u32[]{:S(2)}) collective-permute-start(bf16[192,384]{1,0:T(8,128)(2,1)S(1)} %pad_maximum_fusion.5), channel_id=1, source_target_pairs={{0,4},{4,0},{1,5},{5,1},{2,6},{6,2},{3,7},{7,3},{8,12},{12,8},{9,1... | collective-permute-start | bytes 442376 | tf_op jit(solution)/shard_map/ppermute | solution.py:31
  71.0 2.7 %collective-permute-start.9 = (bf16[64,1536]{1,0:T(8,128)(2,1)S(1)}, bf16[64,1536]{1,0:T(8,128)(2,1)S(1)}, u32[]{:S(2)}, u32[]{:S(2)}) collective-permute-start(bf16[64,1536]{1,0:T(8,128)(2,1)S(1)} %bitcast.76), channel_id=1, source_target_pairs={{0,16},{16,0},{32,48},{48,32},{1,17},{17,1},{33,49},{49,33},{2,18}... | collective-permute-start | bytes 589832 | tf_op jit(solution)/shard_map/ppermute | solution.py:45
  73.7 13.3 %collective-permute-done.5 = bf16[192,384]{1,0:T(8,128)(2,1)S(1)} collective-permute-done((bf16[192,384]{1,0:T(8,128)(2,1)S(1)}, bf16[192,384]{1,0:T(8,128)(2,1)S(1)}, u32[]{:S(2)}, u32[]{:S(2)}) %collective-permute-start.5) | collective-permute-done | bytes 147488 | tf_op jit(solution)/shard_map/ppermute | solution.py:31
  88.3 3.6 %all-to-all-start.2 = ((bf16[4,2,128,384]{3,2,1,0:T(8,128)(2,1)}), bf16[4,2,128,384]{3,2,1,0:T(8,128)(2,1)S(1)}, u32[]{:S(2)}, u32[]{:S(2)}) async-start(bf16[4,2,128,384]{3,2,1,0:T(8,128)(2,1)} %broadcast_in_dim.5), calls=%async_computation.2 | async-start | bytes 1572864 | tf_op jit(solution)/shard_map/all_to_all | solution.py:27
  92.6 3.1 %collective-permute-start.15 = (bf16[128,1536]{1,0:T(8,128)(2,1)}, bf16[128,1536]{1,0:T(8,128)(2,1)}, u32[]{:S(2)}, u32[]{:S(2)}) collective-permute-start(bf16[128,1536]{1,0:T(8,128)(2,1)} %pad_maximum_fusion.2), channel_id=1, source_target_pairs={{0,32},{16,48},{32,0},{48,16},{1,33},{17,49},{33,1},{49,17},{2,34}... | collective-permute-start | bytes 1179656 | tf_op jit(solution)/shard_map/ppermute | solution.py:45
  95.8 2.1 %collective-permute-start.17 = (bf16[256,1536]{1,0:T(8,128)(2,1)S(1)}, bf16[256,1536]{1,0:T(8,128)(2,1)}, u32[]{:S(2)}, u32[]{:S(2)}) collective-permute-start(bf16[256,1536]{1,0:T(8,128)(2,1)S(1)} %pad_maximum_fusion.1.grad_own), channel_id=1, source_target_pairs={{0,8},{8,0},{1,9},{9,1},{2,10},{10,2},{3,11},{11,3},{4,12},{12,4},... | collective-permute-start | bytes 2359304 | tf_op jit(solution)/shard_map/ppermute | solution.py:31
  97.9 6.6 %all-to-all-done.2.cols = bf16[4,2,128,384]{3,2,1,0:T(8,128)(2,1)S(1)} async-done(((bf16[4,2,128,384]{3,2,1,0:T(8,128)(2,1)}), bf16[4,2,128,384]{3,2,1,0:T(8,128)(2,1)S(1)}, u32[]{:S(2)}, u32[]{:S(2)}) %all-to-all-start.2) | async-done | bytes 786464 | tf_op jit(solution)/shard_map/all_to_all | solution.py:27
  104.5 2.3 %shard_map.77 = (f32[64,1536]{1,0:T(8,128)S(1)}, bf16[64,1536]{1,0:T(8,128)(2,1)S(1)}, bf16[64,1536]{1,0:T(8,128)(2,1)S(1)}, bf16[64,1536]{1,0:T(8,128)(2,1)S(1)}, bf16[2,256,384]{2,1,0:T(8,128)(2,1)S(1)}) custom-call(bf16[4,2,128,384]{3,2,1,0:T(8,128)(2,1)S(1)} %all-to-all-done.2.cols, bf16[1536,384]{1,0:T(8,128)(2,1)S(1)} %copy-done.1, ...), custom_call_target="tpu_custom_call" | custom-call | flops 603979776 | bytes 4521984 | tf_op jit(solution)/shard_map/pallas_call | solution.py:67
  106.8 3.1 %collective-permute-start.13 = (bf16[64,1536]{1,0:T(8,128)(2,1)S(1)}, bf16[64,1536]{1,0:T(8,128)(2,1)S(1)}, u32[]{:S(2)}, u32[]{:S(2)}) collective-permute-start(bf16[64,1536]{1,0:T(8,128)(2,1)S(1)} %get-tuple-element.37), channel_id=1, source_target_pairs={{0,48},{16,32},{32,16},{48,0},{1,49},{17,33},{33,17},{49,1},{2,50}... | collective-permute-start | bytes 589832 | tf_op jit(solution)/shard_map/ppermute | solution.py:45
  110.0 3.6 %collective-permute-start.12 = (bf16[64,1536]{1,0:T(8,128)(2,1)S(1)}, bf16[64,1536]{1,0:T(8,128)(2,1)S(1)}, u32[]{:S(2)}, u32[]{:S(2)}) collective-permute-start(bf16[64,1536]{1,0:T(8,128)(2,1)S(1)} %get-tuple-element.36), channel_id=1, source_target_pairs={{0,32},{16,48},{32,0},{48,16},{1,33},{17,49},{33,1},{49,17},{2,34}... | collective-permute-start | bytes 589832 | tf_op jit(solution)/shard_map/ppermute | solution.py:45
  113.6 3.1 %collective-permute-start.11 = (bf16[64,1536]{1,0:T(8,128)(2,1)S(1)}, bf16[64,1536]{1,0:T(8,128)(2,1)S(1)}, u32[]{:S(2)}, u32[]{:S(2)}) collective-permute-start(bf16[64,1536]{1,0:T(8,128)(2,1)S(1)} %get-tuple-element.35), channel_id=1, source_target_pairs={{0,16},{16,0},{32,48},{48,32},{1,17},{17,1},{33,49},{49,33},{2,18}... | collective-permute-start | bytes 589832 | tf_op jit(solution)/shard_map/ppermute | solution.py:45
  116.7 1.9 %collective-permute-start.14 = (bf16[2,256,384]{2,1,0:T(8,128)(2,1)S(1)}, bf16[2,256,384]{2,1,0:T(8,128)(2,1)S(1)}, u32[]{:S(2)}, u32[]{:S(2)}) collective-permute-start(bf16[2,256,384]{2,1,0:T(8,128)(2,1)S(1)} %get-tuple-element.38), channel_id=1, source_target_pairs={{0,8},{8,0},{1,9},{9,1},{2,10},{10,2},{3,11},{11,3},{4,12},{12,4},... | collective-permute-start | bytes 1179656 | tf_op jit(solution)/shard_map/ppermute | solution.py:31
  123.4 1.9 %collective-permute-start.16 = (bf16[256,1536]{1,0:T(8,128)(2,1)S(1)}, bf16[256,1536]{1,0:T(8,128)(2,1)S(1)}, u32[]{:S(2)}, u32[]{:S(2)}) collective-permute-start(bf16[256,1536]{1,0:T(8,128)(2,1)S(1)} %pad_maximum_fusion.block_own), channel_id=1, source_target_pairs={{0,8},{8,0},{1,9},{9,1},{2,10},{10,2},{3,11},{11,3},{4,12},{12,4},... | collective-permute-start | bytes 2359304 | tf_op jit(solution)/shard_map/ppermute | solution.py:31
  125.3 5.1 %all-to-all-start.3 = ((bf16[8,8,1536]{2,1,0:T(8,128)(2,1)}), bf16[8,8,1536]{2,1,0:T(8,128)(2,1)}, u32[]{:S(2)}, u32[]{:S(2)}) async-start(bf16[8,8,1536]{2,1,0:T(8,128)(2,1)} %bitcast.79), calls=%async_computation.3 | async-start | bytes 393216 | tf_op jit(solution)/shard_map/all_to_all | solution.py:183
  130.4 3.0 %shard_map.79 = bf16[384,1536]{1,0:T(8,128)(2,1)} custom-call(bf16[4,2,128,384]{3,2,1,0:T(8,128)(2,1)S(1)} %all-to-all-done.2.cols, bf16[2,256,384]{2,1,0:T(8,128)(2,1)S(1)} %collective-permute-done.14.far, bf16[256,1536]{1,0:T(8,128)(2,1)S(1)} %pad_maximum_fusion.1.grad_own, bf16[256,1536]{1,0:T(8,128)(2,1)} %collective-permute-done.17.grad_sib), custom_call_target="tpu_custom_call" | custom-call | flops 603979776 | bytes 3932160 | tf_op jit(solution)/shard_map/pallas_call | solution.py:67
  133.4 2.0 %shard_map.78 = bf16[1536,384]{1,0:T(8,128)(2,1)} custom-call(bf16[4,2,128,384]{3,2,1,0:T(8,128)(2,1)S(1)} %all-to-all-done.2.cols, bf16[2,256,384]{2,1,0:T(8,128)(2,1)S(1)} %collective-permute-done.14.far, bf16[256,1536]{1,0:T(8,128)(2,1)S(1)} %pad_maximum_fusion.block_own, bf16[256,1536]{1,0:T(8,128)(2,1)S(1)} %collective-permute-done.16.block_sib), custom_call_target="tpu_custom_call" | custom-call | flops 603979776 | bytes 3932160 | tf_op jit(solution)/shard_map/pallas_call | solution.py:67
  135.4 9.4 %all-to-all-done.3 = bf16[8,8,1536]{2,1,0:T(8,128)(2,1)} async-done(((bf16[8,8,1536]{2,1,0:T(8,128)(2,1)}), bf16[8,8,1536]{2,1,0:T(8,128)(2,1)}, u32[]{:S(2)}, u32[]{:S(2)}) %all-to-all-start.3) | async-done | bytes 196640 | tf_op jit(solution)/shard_map/all_to_all | solution.py:183
  144.8 1.6 %reduce_sum.22 = bf16[8,1536]{1,0:T(8,128)(2,1)} reduce(bf16[8,8,1536]{2,1,0:T(8,128)(2,1)} %all-to-all-done.3, bf16[]{:T(256)} %constant.40.clone.1), dimensions={0}, to_apply=%region_1.2 | reduce | flops 86016 | bytes 221186 | tf_op jit(solution)/shard_map/reduce_sum | solution.py:191
  (74 shorter events, 14.0 us)
Async XLA Ops:
  0.6 47.3 %copy-start = (bf16[384,1536]{1,0:T(8,128)(2,1)S(1)}, bf16[384,1536]{1,0:T(8,128)(2,1)}, u32[]{:S(2)}) copy-start(bf16[384,1536]{1,0:T(8,128)(2,1)} %w_own.2) | copy-start | bytes 3538948
  0.6 21.1 %copy-start.13 = (bf16[8,1536]{1,0:T(8,128)(2,1)S(1)}, bf16[8,1536]{1,0:T(8,128)(2,1)}, u32[]{:S(2)}) copy-start(bf16[8,1536]{1,0:T(8,128)(2,1)} %param.5) | copy-start | bytes 73732
  2.2 27.4 %all-to-all-start = ((bf16[8,8,1536]{2,1,0:T(8,128)(2,1)}), bf16[8,8,1536]{2,1,0:T(8,128)(2,1)S(1)}, u32[]{:S(2)}, u32[]{:S(2)}) async-start(bf16[8,8,1536]{2,1,0:T(8,128)(2,1)} %broadcast_in_dim.4), calls=%async_computation | async-start | bytes 393216 | tf_op jit(solution)/shard_map/all_to_all | solution.py:131
  14.8 33.1 %collective-permute-start.3 = (bf16[384,1536]{1,0:T(8,128)(2,1)}, bf16[384,1536]{1,0:T(8,128)(2,1)S(1)}, u32[]{:S(2)}, u32[]{:S(2)}) collective-permute-start(bf16[384,1536]{1,0:T(8,128)(2,1)} %w_own.2), channel_id=1, source_target_pairs={{0,8},{8,0},{1,9},{9,1},{2,10},{10,2},{3,11},{11,3},{4,12},{12,4},... | collective-permute-start | bytes 3538952 | tf_op jit(solution)/shard_map/ppermute | solution.py:31
  19.3 20.8 %collective-permute-start.4 = (bf16[4,8,384]{2,1,0:T(8,128)(2,1)S(1)}, bf16[4,8,384]{2,1,0:T(8,128)(2,1)S(1)}, u32[]{:S(2)}, u32[]{:S(2)}) collective-permute-start(bf16[4,8,384]{2,1,0:T(8,128)(2,1)S(1)} %fusion.8), channel_id=1, source_target_pairs={{0,8},{8,0},{1,9},{9,1},{2,10},{10,2},{3,11},{11,3},{4,12},{12,4},... | collective-permute-start | bytes 73736 | tf_op jit(solution)/shard_map/ppermute | solution.py:31
  21.7 15.2 %collective-permute-start.6 = (bf16[8,1536]{1,0:T(8,128)(2,1)S(1)}, bf16[8,1536]{1,0:T(8,128)(2,1)S(1)}, u32[]{:S(2)}, u32[]{:S(2)}) collective-permute-start(bf16[8,1536]{1,0:T(8,128)(2,1)S(1)} %copy-done.13), channel_id=1, source_target_pairs={{0,256},{64,320},{128,384},{192,448},{256,0},{320,64},{384,128},{4... | collective-permute-start | bytes 73736 | tf_op jit(solution)/shard_map/ppermute | solution.py:45
  29.6 18.3 %collective-permute-start = (bf16[64,1536]{1,0:T(8,128)(2,1)S(1)}, bf16[64,1536]{1,0:T(8,128)(2,1)S(1)}, u32[]{:S(2)}, u32[]{:S(2)}) collective-permute-start(bf16[64,1536]{1,0:T(8,128)(2,1)S(1)} %bitcast.71), channel_id=1, source_target_pairs={{0,16},{16,0},{32,48},{48,32},{1,17},{17,1},{33,49},{49,33},{2,18}... | collective-permute-start | bytes 589832 | tf_op jit(solution)/shard_map/ppermute | solution.py:45
  32.2 15.7 %collective-permute-start.1 = (bf16[64,1536]{1,0:T(8,128)(2,1)S(1)}, bf16[64,1536]{1,0:T(8,128)(2,1)S(1)}, u32[]{:S(2)}, u32[]{:S(2)}) collective-permute-start(bf16[64,1536]{1,0:T(8,128)(2,1)S(1)} %bitcast.72), channel_id=1, source_target_pairs={{0,32},{16,48},{32,0},{48,16},{1,33},{17,49},{33,1},{49,17},{2,34}... | collective-permute-start | bytes 589832 | tf_op jit(solution)/shard_map/ppermute | solution.py:45
  36.9 11.0 %collective-permute-start.2 = (bf16[64,1536]{1,0:T(8,128)(2,1)S(1)}, bf16[64,1536]{1,0:T(8,128)(2,1)S(1)}, u32[]{:S(2)}, u32[]{:S(2)}) collective-permute-start(bf16[64,1536]{1,0:T(8,128)(2,1)S(1)} %bitcast.73), channel_id=1, source_target_pairs={{0,48},{16,32},{32,16},{48,0},{1,49},{17,33},{33,17},{49,1},{2,50}... | collective-permute-start | bytes 589832 | tf_op jit(solution)/shard_map/ppermute | solution.py:45
  40.1 9.6 %copy-start.6 = (bf16[1,8,1536]{2,1,0:T(8,128)(2,1)}, bf16[1,8,1536]{2,1,0:T(8,128)(2,1)S(1)}, u32[]{:S(2)}) copy-start(bf16[1,8,1536]{2,1,0:T(8,128)(2,1)S(1)} %get-tuple-element.55) | copy-start | bytes 73732
  40.1 9.6 %copy-start.7 = (bf16[1,8,1536]{2,1,0:T(8,128)(2,1)}, bf16[1,8,1536]{2,1,0:T(8,128)(2,1)S(1)}, u32[]{:S(2)}) copy-start(bf16[1,8,1536]{2,1,0:T(8,128)(2,1)S(1)} %get-tuple-element.56) | copy-start | bytes 73732
  40.1 6.9 %collective-permute-start.7 = (bf16[2,8,1536]{2,1,0:T(8,128)(2,1)S(1)}, bf16[2,8,1536]{2,1,0:T(8,128)(2,1)S(1)}, u32[]{:S(2)}, u32[]{:S(2)}) collective-permute-start(bf16[2,8,1536]{2,1,0:T(8,128)(2,1)S(1)} %pad_maximum_fusion.9), channel_id=1, source_target_pairs={{0,128},{64,192},{128,0},{192,64},{256,384},{320,448},{384,256},{4... | collective-permute-start | bytes 147464 | tf_op jit(solution)/shard_map/ppermute | solution.py:45
  49.6 13.0 %copy-start.8 = (bf16[2,4,8,384]{3,2,1,0:T(8,128)(2,1)S(1)}, bf16[2,4,8,384]{3,2,1,0:T(8,128)(2,1)}, u32[]{:S(2)}) copy-start(bf16[2,4,8,384]{3,2,1,0:T(8,128)(2,1)} %pad_maximum_fusion.7) | copy-start | bytes 147460
  49.7 12.9 %all-to-all-start.1 = ((bf16[4,128,384]{2,1,0:T(8,128)(2,1)}), bf16[4,128,384]{2,1,0:T(8,128)(2,1)S(1)}, u32[]{:S(2)}, u32[]{:S(2)}) async-start(bf16[4,128,384]{2,1,0:T(8,128)(2,1)} %shard_map.76), calls=%async_computation.1 | async-start | bytes 786432 | tf_op jit(solution)/shard_map/all_to_all | solution.py:147
  55.1 31.9 %copy-start.10 = (bf16[4,8,384]{2,1,0:T(8,128)(2,1)S(1)}, bf16[4,8,384]{2,1,0:T(8,128)(2,1)}, u32[]{:S(2)}) copy-start(bf16[4,8,384]{2,1,0:T(8,128)(2,1)} %copy-done.9) | copy-start | bytes 73732
  55.1 31.9 %copy-start.11 = (bf16[1,1,32,384]{3,2,0,1:T(8,128)(2,1)S(1)}, bf16[1,1,32,384]{3,2,0,1:T(8,128)(2,1)}, u32[]{:S(2)}) copy-start(bf16[1,1,32,384]{3,2,0,1:T(8,128)(2,1)} %get-tuple-element.57) | copy-start | bytes 73732
  55.1 15.7 %collective-permute-start.8 = (bf16[2,2,8,1536]{3,2,0,1:T(8,128)(2,1)S(1)}, bf16[2,2,8,1536]{3,2,0,1:T(8,128)(2,1)S(1)}, u32[]{:S(2)}, u32[]{:S(2)}) collective-permute-start(bf16[2,2,8,1536]{3,2,0,1:T(8,128)(2,1)S(1)} %pad_maximum_fusion.6), channel_id=1, source_target_pairs={{0,64},{64,0},{128,192},{192,128},{256,320},{320,256},{384,448},{4... | collective-permute-start | bytes 294920 | tf_op jit(solution)/shard_map/ppermute | solution.py:45
  57.6 40.2 %collective-permute-start.10 = (bf16[1536,384]{1,0:T(8,128)(2,1)S(1)}, bf16[1536,384]{1,0:T(8,128)(2,1)}, u32[]{:S(2)}, u32[]{:S(2)}) collective-permute-start(bf16[1536,384]{1,0:T(8,128)(2,1)S(1)} %copy-done.1), channel_id=1, source_target_pairs={{0,8},{8,0},{1,9},{9,1},{2,10},{10,2},{3,11},{11,3},{4,12},{12,4},... | collective-permute-start | bytes 3538952 | tf_op jit(solution)/shard_map/ppermute | solution.py:31
  62.6 24.4 %collective-permute-start.5 = (bf16[192,384]{1,0:T(8,128)(2,1)S(1)}, bf16[192,384]{1,0:T(8,128)(2,1)S(1)}, u32[]{:S(2)}, u32[]{:S(2)}) collective-permute-start(bf16[192,384]{1,0:T(8,128)(2,1)S(1)} %pad_maximum_fusion.5), channel_id=1, source_target_pairs={{0,4},{4,0},{1,5},{5,1},{2,6},{6,2},{3,7},{7,3},{8,12},{12,8},{9,1... | collective-permute-start | bytes 442376 | tf_op jit(solution)/shard_map/ppermute | solution.py:31
  71.0 20.9 %copy-start.2 = (bf16[2,2,2,8,1536]{4,3,2,1,0:T(8,128)(2,1)}, bf16[2,2,2,8,1536]{4,3,2,1,0:T(8,128)(2,1)S(1)}, u32[]{:S(2)}) copy-start(bf16[2,2,2,8,1536]{4,3,2,1,0:T(8,128)(2,1)S(1)} %copy.15) | copy-start | bytes 589828
  71.0 16.3 %collective-permute-start.9 = (bf16[64,1536]{1,0:T(8,128)(2,1)S(1)}, bf16[64,1536]{1,0:T(8,128)(2,1)S(1)}, u32[]{:S(2)}, u32[]{:S(2)}) collective-permute-start(bf16[64,1536]{1,0:T(8,128)(2,1)S(1)} %bitcast.76), channel_id=1, source_target_pairs={{0,16},{16,0},{32,48},{48,32},{1,17},{17,1},{33,49},{49,33},{2,18}... | collective-permute-start | bytes 589832 | tf_op jit(solution)/shard_map/ppermute | solution.py:45
  88.3 16.2 %all-to-all-start.2 = ((bf16[4,2,128,384]{3,2,1,0:T(8,128)(2,1)}), bf16[4,2,128,384]{3,2,1,0:T(8,128)(2,1)S(1)}, u32[]{:S(2)}, u32[]{:S(2)}) async-start(bf16[4,2,128,384]{3,2,1,0:T(8,128)(2,1)} %broadcast_in_dim.5), calls=%async_computation.2 | async-start | bytes 1572864 | tf_op jit(solution)/shard_map/all_to_all | solution.py:27
  92.6 24.0 %collective-permute-start.15 = (bf16[128,1536]{1,0:T(8,128)(2,1)}, bf16[128,1536]{1,0:T(8,128)(2,1)}, u32[]{:S(2)}, u32[]{:S(2)}) collective-permute-start(bf16[128,1536]{1,0:T(8,128)(2,1)} %pad_maximum_fusion.2), channel_id=1, source_target_pairs={{0,32},{16,48},{32,0},{48,16},{1,33},{17,49},{33,1},{49,17},{2,34}... | collective-permute-start | bytes 1179656 | tf_op jit(solution)/shard_map/ppermute | solution.py:45
  95.8 22.8 %copy-start.3 = (bf16[2,2,2,8,1536]{4,3,2,1,0:T(8,128)(2,1)S(1)}, bf16[2,2,2,8,1536]{4,3,2,1,0:T(8,128)(2,1)}, u32[]{:S(2)}) copy-start(bf16[2,2,2,8,1536]{4,3,2,1,0:T(8,128)(2,1)} %copy-done.2) | copy-start | bytes 589828
  95.8 22.8 %copy-start.5 = (bf16[64,1536]{1,0:T(8,128)(2,1)S(1)}, bf16[64,1536]{1,0:T(8,128)(2,1)}, u32[]{:S(2)}) copy-start(bf16[64,1536]{1,0:T(8,128)(2,1)} %copy-done.4) | copy-start | bytes 589828
  95.8 34.6 %collective-permute-start.17 = (bf16[256,1536]{1,0:T(8,128)(2,1)S(1)}, bf16[256,1536]{1,0:T(8,128)(2,1)}, u32[]{:S(2)}, u32[]{:S(2)}) collective-permute-start(bf16[256,1536]{1,0:T(8,128)(2,1)S(1)} %pad_maximum_fusion.1.grad_own), channel_id=1, source_target_pairs={{0,8},{8,0},{1,9},{9,1},{2,10},{10,2},{3,11},{11,3},{4,12},{12,4},... | collective-permute-start | bytes 2359304 | tf_op jit(solution)/shard_map/ppermute | solution.py:31
  106.8 12.9 %collective-permute-start.13 = (bf16[64,1536]{1,0:T(8,128)(2,1)S(1)}, bf16[64,1536]{1,0:T(8,128)(2,1)S(1)}, u32[]{:S(2)}, u32[]{:S(2)}) collective-permute-start(bf16[64,1536]{1,0:T(8,128)(2,1)S(1)} %get-tuple-element.37), channel_id=1, source_target_pairs={{0,48},{16,32},{32,16},{48,0},{1,49},{17,33},{33,17},{49,1},{2,50}... | collective-permute-start | bytes 589832 | tf_op jit(solution)/shard_map/ppermute | solution.py:45
  110.0 11.1 %collective-permute-start.12 = (bf16[64,1536]{1,0:T(8,128)(2,1)S(1)}, bf16[64,1536]{1,0:T(8,128)(2,1)S(1)}, u32[]{:S(2)}, u32[]{:S(2)}) collective-permute-start(bf16[64,1536]{1,0:T(8,128)(2,1)S(1)} %get-tuple-element.36), channel_id=1, source_target_pairs={{0,32},{16,48},{32,0},{48,16},{1,33},{17,49},{33,1},{49,17},{2,34}... | collective-permute-start | bytes 589832 | tf_op jit(solution)/shard_map/ppermute | solution.py:45
  113.6 9.0 %collective-permute-start.11 = (bf16[64,1536]{1,0:T(8,128)(2,1)S(1)}, bf16[64,1536]{1,0:T(8,128)(2,1)S(1)}, u32[]{:S(2)}, u32[]{:S(2)}) collective-permute-start(bf16[64,1536]{1,0:T(8,128)(2,1)S(1)} %get-tuple-element.35), channel_id=1, source_target_pairs={{0,16},{16,0},{32,48},{48,32},{1,17},{17,1},{33,49},{49,33},{2,18}... | collective-permute-start | bytes 589832 | tf_op jit(solution)/shard_map/ppermute | solution.py:45
  116.7 6.7 %collective-permute-start.14 = (bf16[2,256,384]{2,1,0:T(8,128)(2,1)S(1)}, bf16[2,256,384]{2,1,0:T(8,128)(2,1)S(1)}, u32[]{:S(2)}, u32[]{:S(2)}) collective-permute-start(bf16[2,256,384]{2,1,0:T(8,128)(2,1)S(1)} %get-tuple-element.38), channel_id=1, source_target_pairs={{0,8},{8,0},{1,9},{9,1},{2,10},{10,2},{3,11},{11,3},{4,12},{12,4},... | collective-permute-start | bytes 1179656 | tf_op jit(solution)/shard_map/ppermute | solution.py:31
  123.4 10.0 %collective-permute-start.16 = (bf16[256,1536]{1,0:T(8,128)(2,1)S(1)}, bf16[256,1536]{1,0:T(8,128)(2,1)S(1)}, u32[]{:S(2)}, u32[]{:S(2)}) collective-permute-start(bf16[256,1536]{1,0:T(8,128)(2,1)S(1)} %pad_maximum_fusion.block_own), channel_id=1, source_target_pairs={{0,8},{8,0},{1,9},{9,1},{2,10},{10,2},{3,11},{11,3},{4,12},{12,4},... | collective-permute-start | bytes 2359304 | tf_op jit(solution)/shard_map/ppermute | solution.py:31
  125.3 19.5 %all-to-all-start.3 = ((bf16[8,8,1536]{2,1,0:T(8,128)(2,1)}), bf16[8,8,1536]{2,1,0:T(8,128)(2,1)}, u32[]{:S(2)}, u32[]{:S(2)}) async-start(bf16[8,8,1536]{2,1,0:T(8,128)(2,1)} %bitcast.79), calls=%async_computation.3 | async-start | bytes 393216 | tf_op jit(solution)/shard_map/all_to_all | solution.py:183
  (4 other events, 24.7 us)

commit v4 on v3

--- a/solution.py
+++ b/solution.py
@@ -69,7 +69,7 @@
         out_shape=out_shape,
         in_specs=[pl.BlockSpec(memory_space=pltpu.VMEM)] * len(operands),
         out_specs=[pl.BlockSpec(memory_space=pltpu.VMEM)] * len(out_shape),
-        compiler_params=pltpu.CompilerParams(vmem_limit_bytes=40 * 1024 * 1024),
+        compiler_params=pltpu.CompilerParams(vmem_limit_bytes=16 * 1024 * 1024),
         cost_estimate=pl.CostEstimate(flops=flops, bytes_accessed=size, transcendentals=0),
     )(*operands)
 
@@ -179,7 +179,7 @@
     far = swap(far, "c")
     sums = [flip(v, "x", k).astype(f32) for k, v in ((1, send_1), (2, send_2), (3, send_3))]
     own, far = lax.optimization_barrier((own + sums[0] + sums[1] + sums[2], far))
-    block_sib = swap(after(block, own), "c")
+    block_sib = swap(block, "c")
     by_z = lax.all_to_all(own.astype(bf16).reshape(8, 8, D), "z", 0, 0)
     (grad_w_out,) = call(
         grad_out_kernel, [jax.ShapeDtypeStruct((F, D), bf16)], 2 * 512 * D * F, cols, far, grad_own, grad_sib

time: 148 us -> 145 us (0.980)
  waiting for transfers between devices: 38.1 us -> 34.7 us
    ppermute x11, waiting for transfers between devices: 5.8 us -> 3.37 us  [flip(): return lax.ppermute(value, axis, [(i, i ^ bit) for i in range(size)])]
  transfers between devices with their start and end apart: 22 -> 22, of which waited for: 8 -> 7; matrix products, arithmetic and copies ran while one was open for 6% -> 6% of each run, Pallas kernels for 5% -> 5%
where the time goes in v4:
time: 145 us; the launch traced here: 143 us
  starting transfers between devices  86.8 us (60%)
  waiting for transfers between devices  34.7 us (24%)
  Pallas kernels  9.04 us (6%)
  other arithmetic  8.38 us (6%)
  local copies, waits for them, and re-layouts  3.39 us (2%)
    ppermute x11, starting transfers between devices, flip(): return lax.ppermute(value, axis, [(i, i ^ bit) for i in range(size)])  40.1 us
    ppermute x7, starting transfers between devices, swap(): return lax.ppermute(value, axis, [(0, 1), (1, 0)])  20.8 us
    ppermute x7, waiting for transfers between devices, swap(): return lax.ppermute(value, axis, [(0, 1), (1, 0)])  13.3 us
    all_to_all x1, starting transfers between devices, on_device(): grad_z = lax.all_to_all(copies, 'z', 0, 0).reshape(64, D)  12.6 us
    pallas_call x4, Pallas kernels, call(): pl.pallas_call(kernel, out_shape=out_shape, in_specs=[pl.BlockSpec(memory...  9.04 us
    all_to_all x1, waiting for transfers between devices, on_device(): by_z = lax.all_to_all(own.astype(bf16).reshape(8, 8, D), 'z', 0, 0)  8.42 us
    all_to_all x1, waiting for transfers between devices, spread(): return lax.all_to_all(copies, axis, 0, 0)  6.62 us
    all_to_all x1, starting transfers between devices, on_device(): by_z = lax.all_to_all(own.astype(bf16).reshape(8, 8, D), 'z', 0, 0)  5.11 us
  transfers between devices with their start and end apart: 22, of which 7 were waited for; matrix products, arithmetic and copies ran while one was open for 6% of the time, Pallas kernels for 5%

profile of v4, /device:TPU:32, one launch (start us, length us, event | category | flops | bytes accessed | tf_op | source)
XLA Modules:
  0.0 143.5 jit_solution(10295869321148107138)
XLA Ops:
  2.2 12.6 %all-to-all-start = ((bf16[8,8,1536]{2,1,0:T(8,128)(2,1)}), bf16[8,8,1536]{2,1,0:T(8,128)(2,1)S(1)}, u32[]{:S(2)}, u32[]{:S(2)}) async-start(bf16[8,8,1536]{2,1,0:T(8,128)(2,1)} %broadcast_in_dim.4), calls=%async_computation | async-start | bytes 393216 | tf_op jit(solution)/shard_map/all_to_all | solution.py:131
  14.8 1.9 %collective-permute-start.3 = (bf16[384,1536]{1,0:T(8,128)(2,1)}, bf16[384,1536]{1,0:T(8,128)(2,1)S(1)}, u32[]{:S(2)}, u32[]{:S(2)}) collective-permute-start(bf16[384,1536]{1,0:T(8,128)(2,1)} %w_own.2), channel_id=1, source_target_pairs={{0,8},{8,0},{1,9},{9,1},{2,10},{10,2},{3,11},{11,3},{4,12},{12,4},... | collective-permute-start | bytes 3538952 | tf_op jit(solution)/shard_map/ppermute | solution.py:31
  19.3 2.4 %collective-permute-start.4 = (bf16[4,8,384]{2,1,0:T(8,128)(2,1)S(1)}, bf16[4,8,384]{2,1,0:T(8,128)(2,1)S(1)}, u32[]{:S(2)}, u32[]{:S(2)}) collective-permute-start(bf16[4,8,384]{2,1,0:T(8,128)(2,1)S(1)} %fusion.8), channel_id=1, source_target_pairs={{0,8},{8,0},{1,9},{9,1},{2,10},{10,2},{3,11},{11,3},{4,12},{12,4},... | collective-permute-start | bytes 73736 | tf_op jit(solution)/shard_map/ppermute | solution.py:31
  21.7 7.3 %collective-permute-start.6 = (bf16[8,1536]{1,0:T(8,128)(2,1)S(1)}, bf16[8,1536]{1,0:T(8,128)(2,1)S(1)}, u32[]{:S(2)}, u32[]{:S(2)}) collective-permute-start(bf16[8,1536]{1,0:T(8,128)(2,1)S(1)} %copy-done.13), channel_id=1, source_target_pairs={{0,256},{64,320},{128,384},{192,448},{256,0},{320,64},{384,128},{4... | collective-permute-start | bytes 73736 | tf_op jit(solution)/shard_map/ppermute | solution.py:45
  29.6 2.6 %collective-permute-start = (bf16[64,1536]{1,0:T(8,128)(2,1)S(1)}, bf16[64,1536]{1,0:T(8,128)(2,1)S(1)}, u32[]{:S(2)}, u32[]{:S(2)}) collective-permute-start(bf16[64,1536]{1,0:T(8,128)(2,1)S(1)} %bitcast.71), channel_id=1, source_target_pairs={{0,16},{16,0},{32,48},{48,32},{1,17},{17,1},{33,49},{49,33},{2,18}... | collective-permute-start | bytes 589832 | tf_op jit(solution)/shard_map/ppermute | solution.py:45
  32.2 4.6 %collective-permute-start.1 = (bf16[64,1536]{1,0:T(8,128)(2,1)S(1)}, bf16[64,1536]{1,0:T(8,128)(2,1)S(1)}, u32[]{:S(2)}, u32[]{:S(2)}) collective-permute-start(bf16[64,1536]{1,0:T(8,128)(2,1)S(1)} %bitcast.72), channel_id=1, source_target_pairs={{0,32},{16,48},{32,0},{48,16},{1,33},{17,49},{33,1},{49,17},{2,34}... | collective-permute-start | bytes 589832 | tf_op jit(solution)/shard_map/ppermute | solution.py:45
  36.9 3.2 %collective-permute-start.2 = (bf16[64,1536]{1,0:T(8,128)(2,1)S(1)}, bf16[64,1536]{1,0:T(8,128)(2,1)S(1)}, u32[]{:S(2)}, u32[]{:S(2)}) collective-permute-start(bf16[64,1536]{1,0:T(8,128)(2,1)S(1)} %bitcast.73), channel_id=1, source_target_pairs={{0,48},{16,32},{32,16},{48,0},{1,49},{17,33},{33,17},{49,1},{2,50}... | collective-permute-start | bytes 589832 | tf_op jit(solution)/shard_map/ppermute | solution.py:45
  40.1 4.3 %collective-permute-start.7 = (bf16[2,8,1536]{2,1,0:T(8,128)(2,1)S(1)}, bf16[2,8,1536]{2,1,0:T(8,128)(2,1)S(1)}, u32[]{:S(2)}, u32[]{:S(2)}) collective-permute-start(bf16[2,8,1536]{2,1,0:T(8,128)(2,1)S(1)} %pad_maximum_fusion.9), channel_id=1, source_target_pairs={{0,128},{64,192},{128,0},{192,64},{256,384},{320,448},{384,256},{4... | collective-permute-start | bytes 147464 | tf_op jit(solution)/shard_map/ppermute | solution.py:45
  45.0 2.0 %collective-permute-done.7 = bf16[2,8,1536]{2,1,0:T(8,128)(2,1)S(1)} collective-permute-done((bf16[2,8,1536]{2,1,0:T(8,128)(2,1)S(1)}, bf16[2,8,1536]{2,1,0:T(8,128)(2,1)S(1)}, u32[]{:S(2)}, u32[]{:S(2)}) %collective-permute-start.7) | collective-permute-done | bytes 49184 | tf_op jit(solution)/shard_map/ppermute | solution.py:45
  47.9 1.7 %shard_map.76 = bf16[4,128,384]{2,1,0:T(8,128)(2,1)} custom-call(bf16[64,1536]{1,0:T(8,128)(2,1)S(1)} %bitcast.74, bf16[64,1536]{1,0:T(8,128)(2,1)S(1)} %collective-permute-done.x1, bf16[64,1536]{1,0:T(8,128)(2,1)S(1)} %collective-permute-done.1.x2, bf16[64,1536]{1,0:T(8,128)(2,1)S(1)} %collective-permute-done.2.x3, bf16[384,1536]{1,0:T(8,128)(2,1)S(1)} %copy-done, ...), custom_call_target="tpu_custom_call" | custom-call | flops 603979776 | bytes 3538944 | tf_op jit(solution)/shard_map/pallas_call | solution.py:67
  49.7 4.6 %all-to-all-start.1 = ((bf16[4,128,384]{2,1,0:T(8,128)(2,1)}), bf16[4,128,384]{2,1,0:T(8,128)(2,1)S(1)}, u32[]{:S(2)}, u32[]{:S(2)}) async-start(bf16[4,128,384]{2,1,0:T(8,128)(2,1)} %shard_map.76), calls=%async_computation.1 | async-start | bytes 786432 | tf_op jit(solution)/shard_map/all_to_all | solution.py:147
  55.1 2.5 %collective-permute-start.8 = (bf16[2,2,8,1536]{3,2,0,1:T(8,128)(2,1)S(1)}, bf16[2,2,8,1536]{3,2,0,1:T(8,128)(2,1)S(1)}, u32[]{:S(2)}, u32[]{:S(2)}) collective-permute-start(bf16[2,2,8,1536]{3,2,0,1:T(8,128)(2,1)S(1)} %pad_maximum_fusion.6), channel_id=1, source_target_pairs={{0,64},{64,0},{128,192},{192,128},{256,320},{320,256},{384,448},{4... | collective-permute-start | bytes 294920 | tf_op jit(solution)/shard_map/ppermute | solution.py:45
  57.6 1.9 %collective-permute-start.10 = (bf16[1536,384]{1,0:T(8,128)(2,1)S(1)}, bf16[1536,384]{1,0:T(8,128)(2,1)}, u32[]{:S(2)}, u32[]{:S(2)}) collective-permute-start(bf16[1536,384]{1,0:T(8,128)(2,1)S(1)} %copy-done.1), channel_id=1, source_target_pairs={{0,8},{8,0},{1,9},{9,1},{2,10},{10,2},{3,11},{11,3},{4,12},{12,4},... | collective-permute-start | bytes 3538952 | tf_op jit(solution)/shard_map/ppermute | solution.py:31
  59.6 3.0 %all-to-all-done.1 = bf16[4,128,384]{2,1,0:T(8,128)(2,1)S(1)} async-done(((bf16[4,128,384]{2,1,0:T(8,128)(2,1)}), bf16[4,128,384]{2,1,0:T(8,128)(2,1)S(1)}, u32[]{:S(2)}, u32[]{:S(2)}) %all-to-all-start.1) | async-done | bytes 393248 | tf_op jit(solution)/shard_map/all_to_all | solution.py:147
  62.6 8.2 %collective-permute-start.5 = (bf16[192,384]{1,0:T(8,128)(2,1)S(1)}, bf16[192,384]{1,0:T(8,128)(2,1)S(1)}, u32[]{:S(2)}, u32[]{:S(2)}) collective-permute-start(bf16[192,384]{1,0:T(8,128)(2,1)S(1)} %pad_maximum_fusion.5), channel_id=1, source_target_pairs={{0,4},{4,0},{1,5},{5,1},{2,6},{6,2},{3,7},{7,3},{8,12},{12,8},{9,1... | collective-permute-start | bytes 442376 | tf_op jit(solution)/shard_map/ppermute | solution.py:31
  71.0 2.7 %collective-permute-start.9 = (bf16[64,1536]{1,0:T(8,128)(2,1)S(1)}, bf16[64,1536]{1,0:T(8,128)(2,1)S(1)}, u32[]{:S(2)}, u32[]{:S(2)}) collective-permute-start(bf16[64,1536]{1,0:T(8,128)(2,1)S(1)} %bitcast.76), channel_id=1, source_target_pairs={{0,16},{16,0},{32,48},{48,32},{1,17},{17,1},{33,49},{49,33},{2,18}... | collective-permute-start | bytes 589832 | tf_op jit(solution)/shard_map/ppermute | solution.py:45
  73.7 13.3 %collective-permute-done.5 = bf16[192,384]{1,0:T(8,128)(2,1)S(1)} collective-permute-done((bf16[192,384]{1,0:T(8,128)(2,1)S(1)}, bf16[192,384]{1,0:T(8,128)(2,1)S(1)}, u32[]{:S(2)}, u32[]{:S(2)}) %collective-permute-start.5) | collective-permute-done | bytes 147488 | tf_op jit(solution)/shard_map/ppermute | solution.py:31
  88.3 3.6 %all-to-all-start.2 = ((bf16[4,2,128,384]{3,2,1,0:T(8,128)(2,1)}), bf16[4,2,128,384]{3,2,1,0:T(8,128)(2,1)S(1)}, u32[]{:S(2)}, u32[]{:S(2)}) async-start(bf16[4,2,128,384]{3,2,1,0:T(8,128)(2,1)} %broadcast_in_dim.5), calls=%async_computation.2 | async-start | bytes 1572864 | tf_op jit(solution)/shard_map/all_to_all | solution.py:27
  92.6 3.1 %collective-permute-start.15 = (bf16[128,1536]{1,0:T(8,128)(2,1)}, bf16[128,1536]{1,0:T(8,128)(2,1)}, u32[]{:S(2)}, u32[]{:S(2)}) collective-permute-start(bf16[128,1536]{1,0:T(8,128)(2,1)} %pad_maximum_fusion.2), channel_id=1, source_target_pairs={{0,32},{16,48},{32,0},{48,16},{1,33},{17,49},{33,1},{49,17},{2,34}... | collective-permute-start | bytes 1179656 | tf_op jit(solution)/shard_map/ppermute | solution.py:45
  95.8 2.1 %collective-permute-start.17 = (bf16[256,1536]{1,0:T(8,128)(2,1)S(1)}, bf16[256,1536]{1,0:T(8,128)(2,1)}, u32[]{:S(2)}, u32[]{:S(2)}) collective-permute-start(bf16[256,1536]{1,0:T(8,128)(2,1)S(1)} %pad_maximum_fusion.1.grad_own), channel_id=1, source_target_pairs={{0,8},{8,0},{1,9},{9,1},{2,10},{10,2},{3,11},{11,3},{4,12},{12,4},... | collective-permute-start | bytes 2359304 | tf_op jit(solution)/shard_map/ppermute | solution.py:31
  97.9 6.6 %all-to-all-done.2.cols = bf16[4,2,128,384]{3,2,1,0:T(8,128)(2,1)S(1)} async-done(((bf16[4,2,128,384]{3,2,1,0:T(8,128)(2,1)}), bf16[4,2,128,384]{3,2,1,0:T(8,128)(2,1)S(1)}, u32[]{:S(2)}, u32[]{:S(2)}) %all-to-all-start.2) | async-done | bytes 786464 | tf_op jit(solution)/shard_map/all_to_all | solution.py:27
  104.5 2.3 %shard_map.77 = (f32[64,1536]{1,0:T(8,128)S(1)}, bf16[64,1536]{1,0:T(8,128)(2,1)S(1)}, bf16[64,1536]{1,0:T(8,128)(2,1)S(1)}, bf16[64,1536]{1,0:T(8,128)(2,1)S(1)}, bf16[2,256,384]{2,1,0:T(8,128)(2,1)S(1)}) custom-call(bf16[4,2,128,384]{3,2,1,0:T(8,128)(2,1)S(1)} %all-to-all-done.2.cols, bf16[1536,384]{1,0:T(8,128)(2,1)S(1)} %copy-done.1, ...), custom_call_target="tpu_custom_call" | custom-call | flops 603979776 | bytes 4521984 | tf_op jit(solution)/shard_map/pallas_call | solution.py:67
  106.8 3.1 %collective-permute-start.13 = (bf16[64,1536]{1,0:T(8,128)(2,1)S(1)}, bf16[64,1536]{1,0:T(8,128)(2,1)S(1)}, u32[]{:S(2)}, u32[]{:S(2)}) collective-permute-start(bf16[64,1536]{1,0:T(8,128)(2,1)S(1)} %get-tuple-element.36), channel_id=1, source_target_pairs={{0,48},{16,32},{32,16},{48,0},{1,49},{17,33},{33,17},{49,1},{2,50}... | collective-permute-start | bytes 589832 | tf_op jit(solution)/shard_map/ppermute | solution.py:45
  110.0 3.6 %collective-permute-start.12 = (bf16[64,1536]{1,0:T(8,128)(2,1)S(1)}, bf16[64,1536]{1,0:T(8,128)(2,1)S(1)}, u32[]{:S(2)}, u32[]{:S(2)}) collective-permute-start(bf16[64,1536]{1,0:T(8,128)(2,1)S(1)} %get-tuple-element.35), channel_id=1, source_target_pairs={{0,32},{16,48},{32,0},{48,16},{1,33},{17,49},{33,1},{49,17},{2,34}... | collective-permute-start | bytes 589832 | tf_op jit(solution)/shard_map/ppermute | solution.py:45
  113.6 3.1 %collective-permute-start.11 = (bf16[64,1536]{1,0:T(8,128)(2,1)S(1)}, bf16[64,1536]{1,0:T(8,128)(2,1)S(1)}, u32[]{:S(2)}, u32[]{:S(2)}) collective-permute-start(bf16[64,1536]{1,0:T(8,128)(2,1)S(1)} %get-tuple-element.34), channel_id=1, source_target_pairs={{0,16},{16,0},{32,48},{48,32},{1,17},{17,1},{33,49},{49,33},{2,18}... | collective-permute-start | bytes 589832 | tf_op jit(solution)/shard_map/ppermute | solution.py:45
  116.7 1.9 %collective-permute-start.14 = (bf16[2,256,384]{2,1,0:T(8,128)(2,1)S(1)}, bf16[2,256,384]{2,1,0:T(8,128)(2,1)S(1)}, u32[]{:S(2)}, u32[]{:S(2)}) collective-permute-start(bf16[2,256,384]{2,1,0:T(8,128)(2,1)S(1)} %get-tuple-element.37), channel_id=1, source_target_pairs={{0,8},{8,0},{1,9},{9,1},{2,10},{10,2},{3,11},{11,3},{4,12},{12,4},... | collective-permute-start | bytes 1179656 | tf_op jit(solution)/shard_map/ppermute | solution.py:31
  119.7 2.4 %collective-permute-start.16 = (bf16[256,1536]{1,0:T(8,128)(2,1)S(1)}, bf16[256,1536]{1,0:T(8,128)(2,1)S(1)}, u32[]{:S(2)}, u32[]{:S(2)}) collective-permute-start(bf16[256,1536]{1,0:T(8,128)(2,1)S(1)} %pad_maximum_fusion.block_own), channel_id=1, source_target_pairs={{0,8},{8,0},{1,9},{9,1},{2,10},{10,2},{3,11},{11,3},{4,12},{12,4},... | collective-permute-start | bytes 2359304 | tf_op jit(solution)/shard_map/ppermute | solution.py:31
  123.4 5.1 %all-to-all-start.3 = ((bf16[8,8,1536]{2,1,0:T(8,128)(2,1)}), bf16[8,8,1536]{2,1,0:T(8,128)(2,1)}, u32[]{:S(2)}, u32[]{:S(2)}) async-start(bf16[8,8,1536]{2,1,0:T(8,128)(2,1)} %bitcast.79), calls=%async_computation.3 | async-start | bytes 393216 | tf_op jit(solution)/shard_map/all_to_all | solution.py:183
  128.5 3.0 %shard_map.79 = bf16[384,1536]{1,0:T(8,128)(2,1)} custom-call(bf16[4,2,128,384]{3,2,1,0:T(8,128)(2,1)S(1)} %all-to-all-done.2.cols, bf16[2,256,384]{2,1,0:T(8,128)(2,1)S(1)} %collective-permute-done.14.far, bf16[256,1536]{1,0:T(8,128)(2,1)S(1)} %pad_maximum_fusion.1.grad_own, bf16[256,1536]{1,0:T(8,128)(2,1)} %collective-permute-done.17.grad_sib), custom_call_target="tpu_custom_call" | custom-call | flops 603979776 | bytes 3932160 | tf_op jit(solution)/shard_map/pallas_call | solution.py:67
  131.5 2.0 %shard_map.78 = bf16[1536,384]{1,0:T(8,128)(2,1)} custom-call(bf16[4,2,128,384]{3,2,1,0:T(8,128)(2,1)S(1)} %all-to-all-done.2.cols, bf16[2,256,384]{2,1,0:T(8,128)(2,1)S(1)} %collective-permute-done.14.far, bf16[256,1536]{1,0:T(8,128)(2,1)S(1)} %pad_maximum_fusion.block_own, bf16[256,1536]{1,0:T(8,128)(2,1)S(1)} %collective-permute-done.16.block_sib), custom_call_target="tpu_custom_call" | custom-call | flops 603979776 | bytes 3932160 | tf_op jit(solution)/shard_map/pallas_call | solution.py:67
  133.5 8.4 %all-to-all-done.3 = bf16[8,8,1536]{2,1,0:T(8,128)(2,1)} async-done(((bf16[8,8,1536]{2,1,0:T(8,128)(2,1)}), bf16[8,8,1536]{2,1,0:T(8,128)(2,1)}, u32[]{:S(2)}, u32[]{:S(2)}) %all-to-all-start.3) | async-done | bytes 196640 | tf_op jit(solution)/shard_map/all_to_all | solution.py:183
  141.9 1.6 %reduce_sum.22 = bf16[8,1536]{1,0:T(8,128)(2,1)} reduce(bf16[8,8,1536]{2,1,0:T(8,128)(2,1)} %all-to-all-done.3, bf16[]{:T(256)} %constant.40.clone.1), dimensions={0}, to_apply=%region_1.2 | reduce | flops 86016 | bytes 221186 | tf_op jit(solution)/shard_map/reduce_sum | solution.py:191
  (74 shorter events, 11.6 us)
Async XLA Ops:
  0.6 47.3 %copy-start = (bf16[384,1536]{1,0:T(8,128)(2,1)S(1)}, bf16[384,1536]{1,0:T(8,128)(2,1)}, u32[]{:S(2)}) copy-start(bf16[384,1536]{1,0:T(8,128)(2,1)} %w_own.2) | copy-start | bytes 3538948
  0.6 21.1 %copy-start.13 = (bf16[8,1536]{1,0:T(8,128)(2,1)S(1)}, bf16[8,1536]{1,0:T(8,128)(2,1)}, u32[]{:S(2)}) copy-start(bf16[8,1536]{1,0:T(8,128)(2,1)} %param.5) | copy-start | bytes 73732
  2.2 27.4 %all-to-all-start = ((bf16[8,8,1536]{2,1,0:T(8,128)(2,1)}), bf16[8,8,1536]{2,1,0:T(8,128)(2,1)S(1)}, u32[]{:S(2)}, u32[]{:S(2)}) async-start(bf16[8,8,1536]{2,1,0:T(8,128)(2,1)} %broadcast_in_dim.4), calls=%async_computation | async-start | bytes 393216 | tf_op jit(solution)/shard_map/all_to_all | solution.py:131
  14.8 33.1 %collective-permute-start.3 = (bf16[384,1536]{1,0:T(8,128)(2,1)}, bf16[384,1536]{1,0:T(8,128)(2,1)S(1)}, u32[]{:S(2)}, u32[]{:S(2)}) collective-permute-start(bf16[384,1536]{1,0:T(8,128)(2,1)} %w_own.2), channel_id=1, source_target_pairs={{0,8},{8,0},{1,9},{9,1},{2,10},{10,2},{3,11},{11,3},{4,12},{12,4},... | collective-permute-start | bytes 3538952 | tf_op jit(solution)/shard_map/ppermute | solution.py:31
  19.3 20.8 %collective-permute-start.4 = (bf16[4,8,384]{2,1,0:T(8,128)(2,1)S(1)}, bf16[4,8,384]{2,1,0:T(8,128)(2,1)S(1)}, u32[]{:S(2)}, u32[]{:S(2)}) collective-permute-start(bf16[4,8,384]{2,1,0:T(8,128)(2,1)S(1)} %fusion.8), channel_id=1, source_target_pairs={{0,8},{8,0},{1,9},{9,1},{2,10},{10,2},{3,11},{11,3},{4,12},{12,4},... | collective-permute-start | bytes 73736 | tf_op jit(solution)/shard_map/ppermute | solution.py:31
  21.7 15.2 %collective-permute-start.6 = (bf16[8,1536]{1,0:T(8,128)(2,1)S(1)}, bf16[8,1536]{1,0:T(8,128)(2,1)S(1)}, u32[]{:S(2)}, u32[]{:S(2)}) collective-permute-start(bf16[8,1536]{1,0:T(8,128)(2,1)S(1)} %copy-done.13), channel_id=1, source_target_pairs={{0,256},{64,320},{128,384},{192,448},{256,0},{320,64},{384,128},{4... | collective-permute-start | bytes 73736 | tf_op jit(solution)/shard_map/ppermute | solution.py:45
  29.6 18.3 %collective-permute-start = (bf16[64,1536]{1,0:T(8,128)(2,1)S(1)}, bf16[64,1536]{1,0:T(8,128)(2,1)S(1)}, u32[]{:S(2)}, u32[]{:S(2)}) collective-permute-start(bf16[64,1536]{1,0:T(8,128)(2,1)S(1)} %bitcast.71), channel_id=1, source_target_pairs={{0,16},{16,0},{32,48},{48,32},{1,17},{17,1},{33,49},{49,33},{2,18}... | collective-permute-start | bytes 589832 | tf_op jit(solution)/shard_map/ppermute | solution.py:45
  32.2 15.7 %collective-permute-start.1 = (bf16[64,1536]{1,0:T(8,128)(2,1)S(1)}, bf16[64,1536]{1,0:T(8,128)(2,1)S(1)}, u32[]{:S(2)}, u32[]{:S(2)}) collective-permute-start(bf16[64,1536]{1,0:T(8,128)(2,1)S(1)} %bitcast.72), channel_id=1, source_target_pairs={{0,32},{16,48},{32,0},{48,16},{1,33},{17,49},{33,1},{49,17},{2,34}... | collective-permute-start | bytes 589832 | tf_op jit(solution)/shard_map/ppermute | solution.py:45
  36.9 11.0 %collective-permute-start.2 = (bf16[64,1536]{1,0:T(8,128)(2,1)S(1)}, bf16[64,1536]{1,0:T(8,128)(2,1)S(1)}, u32[]{:S(2)}, u32[]{:S(2)}) collective-permute-start(bf16[64,1536]{1,0:T(8,128)(2,1)S(1)} %bitcast.73), channel_id=1, source_target_pairs={{0,48},{16,32},{32,16},{48,0},{1,49},{17,33},{33,17},{49,1},{2,50}... | collective-permute-start | bytes 589832 | tf_op jit(solution)/shard_map/ppermute | solution.py:45
  40.1 9.6 %copy-start.6 = (bf16[1,8,1536]{2,1,0:T(8,128)(2,1)}, bf16[1,8,1536]{2,1,0:T(8,128)(2,1)S(1)}, u32[]{:S(2)}) copy-start(bf16[1,8,1536]{2,1,0:T(8,128)(2,1)S(1)} %get-tuple-element.53) | copy-start | bytes 73732
  40.1 9.6 %copy-start.7 = (bf16[1,8,1536]{2,1,0:T(8,128)(2,1)}, bf16[1,8,1536]{2,1,0:T(8,128)(2,1)S(1)}, u32[]{:S(2)}) copy-start(bf16[1,8,1536]{2,1,0:T(8,128)(2,1)S(1)} %get-tuple-element.54) | copy-start | bytes 73732
  40.1 6.9 %collective-permute-start.7 = (bf16[2,8,1536]{2,1,0:T(8,128)(2,1)S(1)}, bf16[2,8,1536]{2,1,0:T(8,128)(2,1)S(1)}, u32[]{:S(2)}, u32[]{:S(2)}) collective-permute-start(bf16[2,8,1536]{2,1,0:T(8,128)(2,1)S(1)} %pad_maximum_fusion.9), channel_id=1, source_target_pairs={{0,128},{64,192},{128,0},{192,64},{256,384},{320,448},{384,256},{4... | collective-permute-start | bytes 147464 | tf_op jit(solution)/shard_map/ppermute | solution.py:45
  49.6 13.0 %copy-start.8 = (bf16[2,4,8,384]{3,2,1,0:T(8,128)(2,1)S(1)}, bf16[2,4,8,384]{3,2,1,0:T(8,128)(2,1)}, u32[]{:S(2)}) copy-start(bf16[2,4,8,384]{3,2,1,0:T(8,128)(2,1)} %pad_maximum_fusion.7) | copy-start | bytes 147460
  49.7 12.9 %all-to-all-start.1 = ((bf16[4,128,384]{2,1,0:T(8,128)(2,1)}), bf16[4,128,384]{2,1,0:T(8,128)(2,1)S(1)}, u32[]{:S(2)}, u32[]{:S(2)}) async-start(bf16[4,128,384]{2,1,0:T(8,128)(2,1)} %shard_map.76), calls=%async_computation.1 | async-start | bytes 786432 | tf_op jit(solution)/shard_map/all_to_all | solution.py:147
  55.1 31.9 %copy-start.10 = (bf16[4,8,384]{2,1,0:T(8,128)(2,1)S(1)}, bf16[4,8,384]{2,1,0:T(8,128)(2,1)}, u32[]{:S(2)}) copy-start(bf16[4,8,384]{2,1,0:T(8,128)(2,1)} %copy-done.9) | copy-start | bytes 73732
  55.1 31.9 %copy-start.11 = (bf16[1,1,32,384]{3,2,0,1:T(8,128)(2,1)S(1)}, bf16[1,1,32,384]{3,2,0,1:T(8,128)(2,1)}, u32[]{:S(2)}) copy-start(bf16[1,1,32,384]{3,2,0,1:T(8,128)(2,1)} %get-tuple-element.55) | copy-start | bytes 73732
  55.1 15.7 %collective-permute-start.8 = (bf16[2,2,8,1536]{3,2,0,1:T(8,128)(2,1)S(1)}, bf16[2,2,8,1536]{3,2,0,1:T(8,128)(2,1)S(1)}, u32[]{:S(2)}, u32[]{:S(2)}) collective-permute-start(bf16[2,2,8,1536]{3,2,0,1:T(8,128)(2,1)S(1)} %pad_maximum_fusion.6), channel_id=1, source_target_pairs={{0,64},{64,0},{128,192},{192,128},{256,320},{320,256},{384,448},{4... | collective-permute-start | bytes 294920 | tf_op jit(solution)/shard_map/ppermute | solution.py:45
  57.6 40.2 %collective-permute-start.10 = (bf16[1536,384]{1,0:T(8,128)(2,1)S(1)}, bf16[1536,384]{1,0:T(8,128)(2,1)}, u32[]{:S(2)}, u32[]{:S(2)}) collective-permute-start(bf16[1536,384]{1,0:T(8,128)(2,1)S(1)} %copy-done.1), channel_id=1, source_target_pairs={{0,8},{8,0},{1,9},{9,1},{2,10},{10,2},{3,11},{11,3},{4,12},{12,4},... | collective-permute-start | bytes 3538952 | tf_op jit(solution)/shard_map/ppermute | solution.py:31
  62.6 24.4 %collective-permute-start.5 = (bf16[192,384]{1,0:T(8,128)(2,1)S(1)}, bf16[192,384]{1,0:T(8,128)(2,1)S(1)}, u32[]{:S(2)}, u32[]{:S(2)}) collective-permute-start(bf16[192,384]{1,0:T(8,128)(2,1)S(1)} %pad_maximum_fusion.5), channel_id=1, source_target_pairs={{0,4},{4,0},{1,5},{5,1},{2,6},{6,2},{3,7},{7,3},{8,12},{12,8},{9,1... | collective-permute-start | bytes 442376 | tf_op jit(solution)/shard_map/ppermute | solution.py:31
  71.0 20.9 %copy-start.2 = (bf16[2,2,2,8,1536]{4,3,2,1,0:T(8,128)(2,1)}, bf16[2,2,2,8,1536]{4,3,2,1,0:T(8,128)(2,1)S(1)}, u32[]{:S(2)}) copy-start(bf16[2,2,2,8,1536]{4,3,2,1,0:T(8,128)(2,1)S(1)} %copy.15) | copy-start | bytes 589828
  71.0 16.3 %collective-permute-start.9 = (bf16[64,1536]{1,0:T(8,128)(2,1)S(1)}, bf16[64,1536]{1,0:T(8,128)(2,1)S(1)}, u32[]{:S(2)}, u32[]{:S(2)}) collective-permute-start(bf16[64,1536]{1,0:T(8,128)(2,1)S(1)} %bitcast.76), channel_id=1, source_target_pairs={{0,16},{16,0},{32,48},{48,32},{1,17},{17,1},{33,49},{49,33},{2,18}... | collective-permute-start | bytes 589832 | tf_op jit(solution)/shard_map/ppermute | solution.py:45
  88.3 16.2 %all-to-all-start.2 = ((bf16[4,2,128,384]{3,2,1,0:T(8,128)(2,1)}), bf16[4,2,128,384]{3,2,1,0:T(8,128)(2,1)S(1)}, u32[]{:S(2)}, u32[]{:S(2)}) async-start(bf16[4,2,128,384]{3,2,1,0:T(8,128)(2,1)} %broadcast_in_dim.5), calls=%async_computation.2 | async-start | bytes 1572864 | tf_op jit(solution)/shard_map/all_to_all | solution.py:27
  92.6 24.0 %collective-permute-start.15 = (bf16[128,1536]{1,0:T(8,128)(2,1)}, bf16[128,1536]{1,0:T(8,128)(2,1)}, u32[]{:S(2)}, u32[]{:S(2)}) collective-permute-start(bf16[128,1536]{1,0:T(8,128)(2,1)} %pad_maximum_fusion.2), channel_id=1, source_target_pairs={{0,32},{16,48},{32,0},{48,16},{1,33},{17,49},{33,1},{49,17},{2,34}... | collective-permute-start | bytes 1179656 | tf_op jit(solution)/shard_map/ppermute | solution.py:45
  95.8 22.8 %copy-start.3 = (bf16[2,2,2,8,1536]{4,3,2,1,0:T(8,128)(2,1)S(1)}, bf16[2,2,2,8,1536]{4,3,2,1,0:T(8,128)(2,1)}, u32[]{:S(2)}) copy-start(bf16[2,2,2,8,1536]{4,3,2,1,0:T(8,128)(2,1)} %copy-done.2) | copy-start | bytes 589828
  95.8 22.8 %copy-start.5 = (bf16[64,1536]{1,0:T(8,128)(2,1)S(1)}, bf16[64,1536]{1,0:T(8,128)(2,1)}, u32[]{:S(2)}) copy-start(bf16[64,1536]{1,0:T(8,128)(2,1)} %copy-done.4) | copy-start | bytes 589828
  95.8 32.7 %collective-permute-start.17 = (bf16[256,1536]{1,0:T(8,128)(2,1)S(1)}, bf16[256,1536]{1,0:T(8,128)(2,1)}, u32[]{:S(2)}, u32[]{:S(2)}) collective-permute-start(bf16[256,1536]{1,0:T(8,128)(2,1)S(1)} %pad_maximum_fusion.1.grad_own), channel_id=1, source_target_pairs={{0,8},{8,0},{1,9},{9,1},{2,10},{10,2},{3,11},{11,3},{4,12},{12,4},... | collective-permute-start | bytes 2359304 | tf_op jit(solution)/shard_map/ppermute | solution.py:31
  106.8 12.9 %collective-permute-start.13 = (bf16[64,1536]{1,0:T(8,128)(2,1)S(1)}, bf16[64,1536]{1,0:T(8,128)(2,1)S(1)}, u32[]{:S(2)}, u32[]{:S(2)}) collective-permute-start(bf16[64,1536]{1,0:T(8,128)(2,1)S(1)} %get-tuple-element.36), channel_id=1, source_target_pairs={{0,48},{16,32},{32,16},{48,0},{1,49},{17,33},{33,17},{49,1},{2,50}... | collective-permute-start | bytes 589832 | tf_op jit(solution)/shard_map/ppermute | solution.py:45
  110.0 12.1 %collective-permute-start.12 = (bf16[64,1536]{1,0:T(8,128)(2,1)S(1)}, bf16[64,1536]{1,0:T(8,128)(2,1)S(1)}, u32[]{:S(2)}, u32[]{:S(2)}) collective-permute-start(bf16[64,1536]{1,0:T(8,128)(2,1)S(1)} %get-tuple-element.35), channel_id=1, source_target_pairs={{0,32},{16,48},{32,0},{48,16},{1,33},{17,49},{33,1},{49,17},{2,34}... | collective-permute-start | bytes 589832 | tf_op jit(solution)/shard_map/ppermute | solution.py:45
  113.6 9.0 %collective-permute-start.11 = (bf16[64,1536]{1,0:T(8,128)(2,1)S(1)}, bf16[64,1536]{1,0:T(8,128)(2,1)S(1)}, u32[]{:S(2)}, u32[]{:S(2)}) collective-permute-start(bf16[64,1536]{1,0:T(8,128)(2,1)S(1)} %get-tuple-element.34), channel_id=1, source_target_pairs={{0,16},{16,0},{32,48},{48,32},{1,17},{17,1},{33,49},{49,33},{2,18}... | collective-permute-start | bytes 589832 | tf_op jit(solution)/shard_map/ppermute | solution.py:45
  116.7 6.7 %collective-permute-start.14 = (bf16[2,256,384]{2,1,0:T(8,128)(2,1)S(1)}, bf16[2,256,384]{2,1,0:T(8,128)(2,1)S(1)}, u32[]{:S(2)}, u32[]{:S(2)}) collective-permute-start(bf16[2,256,384]{2,1,0:T(8,128)(2,1)S(1)} %get-tuple-element.37), channel_id=1, source_target_pairs={{0,8},{8,0},{1,9},{9,1},{2,10},{10,2},{3,11},{11,3},{4,12},{12,4},... | collective-permute-start | bytes 1179656 | tf_op jit(solution)/shard_map/ppermute | solution.py:31
  119.7 11.8 %collective-permute-start.16 = (bf16[256,1536]{1,0:T(8,128)(2,1)S(1)}, bf16[256,1536]{1,0:T(8,128)(2,1)S(1)}, u32[]{:S(2)}, u32[]{:S(2)}) collective-permute-start(bf16[256,1536]{1,0:T(8,128)(2,1)S(1)} %pad_maximum_fusion.block_own), channel_id=1, source_target_pairs={{0,8},{8,0},{1,9},{9,1},{2,10},{10,2},{3,11},{11,3},{4,12},{12,4},... | collective-permute-start | bytes 2359304 | tf_op jit(solution)/shard_map/ppermute | solution.py:31
  123.4 18.5 %all-to-all-start.3 = ((bf16[8,8,1536]{2,1,0:T(8,128)(2,1)}), bf16[8,8,1536]{2,1,0:T(8,128)(2,1)}, u32[]{:S(2)}, u32[]{:S(2)}) async-start(bf16[8,8,1536]{2,1,0:T(8,128)(2,1)} %bitcast.79), calls=%async_computation.3 | async-start | bytes 393216 | tf_op jit(solution)/shard_map/all_to_all | solution.py:183
  (4 other events, 24.7 us)

commit v5 on v4

--- a/solution.py
+++ b/solution.py
@@ -132,8 +132,16 @@
     other = after(flip(inputs, "z", 4), grad_z)
     block = join(inputs, other, "z", 4, 0)
     pre_parts = pre_act.reshape(4, 2, 8, F)
-    pre_parts = jnp.where((place & 1) != 0, pre_parts.reshape(2, 2, 2, 8, F)[:, ::-1].reshape(4, 2, 8, F), pre_parts)
-    pre_parts = jnp.where((place & 2) != 0, pre_parts.reshape(2, 2, 2, 8, F)[::-1].reshape(4, 2, 8, F), pre_parts)
+    pre_parts = jnp.stack(
+        [
+            jnp.where(
+                place < 2,
+                jnp.where(place == 0, pre_parts[k], pre_parts[k ^ 1]),
+                jnp.where(place == 2, pre_parts[k ^ 2], pre_parts[k ^ 3]),
+            )
+            for k in range(4)
+        ]
+    )
     w_out_sib = swap(w_out, "c")
     pre_mine = jnp.where(core == 0, pre_parts[:, 0], pre_parts[:, 1])
     pre_give = jnp.where(core == 0, pre_parts[:, 1], pre_parts[:, 0])

time: 145 us -> 144 us (level)
    all_to_all x1, starting transfers between devices: 3.57 us -> 5.3 us  [spread(): return lax.all_to_all(copies, axis, 0, 0)]
  transfers between devices with their start and end apart: 22 -> 22, of which waited for: 7 -> 8; matrix products, arithmetic and copies ran while one was open for 6% -> 5% of each run, Pallas kernels for 5% -> 5%
where the time goes in v5:
time: 144 us; the launch traced here: 143 us
  starting transfers between devices  88.2 us (61%)
  waiting for transfers between devices  33.5 us (23%)
  Pallas kernels  9.04 us (6%)
  other arithmetic  8.2 us (6%)
  local copies, waits for them, and re-layouts  2.56 us (2%)
    ppermute x11, starting transfers between devices, flip(): return lax.ppermute(value, axis, [(i, i ^ bit) for i in range(size)])  38.9 us
    ppermute x7, starting transfers between devices, swap(): return lax.ppermute(value, axis, [(0, 1), (1, 0)])  20.8 us
    ppermute x7, waiting for transfers between devices, swap(): return lax.ppermute(value, axis, [(0, 1), (1, 0)])  12.9 us
    all_to_all x1, starting transfers between devices, on_device(): grad_z = lax.all_to_all(copies, 'z', 0, 0).reshape(64, D)  12.6 us
    pallas_call x4, Pallas kernels, call(): pl.pallas_call(kernel, out_shape=out_shape, in_specs=[pl.BlockSpec(memory...  9.04 us
    all_to_all x1, waiting for transfers between devices, on_device(): by_z = lax.all_to_all(own.astype(bf16).reshape(8, 8, D), 'z', 0, 0)  8.42 us
    all_to_all x1, waiting for transfers between devices, spread(): return lax.all_to_all(copies, axis, 0, 0)  6.12 us
    all_to_all x1, starting transfers between devices, on_device(): by_z = lax.all_to_all(own.astype(bf16).reshape(8, 8, D), 'z', 0, 0)  5.86 us
  transfers between devices with their start and end apart: 22, of which 8 were waited for; matrix products, arithmetic and copies ran while one was open for 5% of the time, Pallas kernels for 5%

profile of v5, /device:TPU:32, one launch (start us, length us, event | category | flops | bytes accessed | tf_op | source)
XLA Modules:
  0.0 142.6 jit_solution(17996141425859317771)
XLA Ops:
  2.2 12.6 %all-to-all-start = ((bf16[8,8,1536]{2,1,0:T(8,128)(2,1)}), bf16[8,8,1536]{2,1,0:T(8,128)(2,1)S(1)}, u32[]{:S(2)}, u32[]{:S(2)}) async-start(bf16[8,8,1536]{2,1,0:T(8,128)(2,1)} %broadcast_in_dim.4), calls=%async_computation | async-start | bytes 393216 | tf_op jit(solution)/shard_map/all_to_all | solution.py:131
  14.8 1.9 %collective-permute-start.3 = (bf16[384,1536]{1,0:T(8,128)(2,1)}, bf16[384,1536]{1,0:T(8,128)(2,1)S(1)}, u32[]{:S(2)}, u32[]{:S(2)}) collective-permute-start(bf16[384,1536]{1,0:T(8,128)(2,1)} %w_own.2), channel_id=1, source_target_pairs={{0,8},{8,0},{1,9},{9,1},{2,10},{10,2},{3,11},{11,3},{4,12},{12,4},... | collective-permute-start | bytes 3538952 | tf_op jit(solution)/shard_map/ppermute | solution.py:31
  17.5 2.4 %collective-permute-start.4 = (bf16[4,8,384]{2,1,0:T(8,128)(2,1)S(1)}, bf16[4,8,384]{2,1,0:T(8,128)(2,1)S(1)}, u32[]{:S(2)}, u32[]{:S(2)}) collective-permute-start(bf16[4,8,384]{2,1,0:T(8,128)(2,1)S(1)} %fusion.7), channel_id=1, source_target_pairs={{0,8},{8,0},{1,9},{9,1},{2,10},{10,2},{3,11},{11,3},{4,12},{12,4},... | collective-permute-start | bytes 73736 | tf_op jit(solution)/shard_map/ppermute | solution.py:31
  20.0 7.3 %collective-permute-start.6 = (bf16[8,1536]{1,0:T(8,128)(2,1)}, bf16[8,1536]{1,0:T(8,128)(2,1)S(1)}, u32[]{:S(2)}, u32[]{:S(2)}) collective-permute-start(bf16[8,1536]{1,0:T(8,128)(2,1)} %param.5), channel_id=1, source_target_pairs={{0,256},{64,320},{128,384},{192,448},{256,0},{320,64},{384,128},{4... | collective-permute-start | bytes 73736 | tf_op jit(solution)/shard_map/ppermute | solution.py:45
  28.4 3.4 %collective-permute-start = (bf16[64,1536]{1,0:T(8,128)(2,1)S(1)}, bf16[64,1536]{1,0:T(8,128)(2,1)S(1)}, u32[]{:S(2)}, u32[]{:S(2)}) collective-permute-start(bf16[64,1536]{1,0:T(8,128)(2,1)S(1)} %bitcast.71), channel_id=1, source_target_pairs={{0,16},{16,0},{32,48},{48,32},{1,17},{17,1},{33,49},{49,33},{2,18}... | collective-permute-start | bytes 589832 | tf_op jit(solution)/shard_map/ppermute | solution.py:45
  31.8 4.6 %collective-permute-start.1 = (bf16[64,1536]{1,0:T(8,128)(2,1)S(1)}, bf16[64,1536]{1,0:T(8,128)(2,1)S(1)}, u32[]{:S(2)}, u32[]{:S(2)}) collective-permute-start(bf16[64,1536]{1,0:T(8,128)(2,1)S(1)} %bitcast.72), channel_id=1, source_target_pairs={{0,32},{16,48},{32,0},{48,16},{1,33},{17,49},{33,1},{49,17},{2,34}... | collective-permute-start | bytes 589832 | tf_op jit(solution)/shard_map/ppermute | solution.py:45
  36.4 2.4 %collective-permute-start.2 = (bf16[64,1536]{1,0:T(8,128)(2,1)S(1)}, bf16[64,1536]{1,0:T(8,128)(2,1)S(1)}, u32[]{:S(2)}, u32[]{:S(2)}) collective-permute-start(bf16[64,1536]{1,0:T(8,128)(2,1)S(1)} %bitcast.73), channel_id=1, source_target_pairs={{0,48},{16,32},{32,16},{48,0},{1,49},{17,33},{33,17},{49,1},{2,50}... | collective-permute-start | bytes 589832 | tf_op jit(solution)/shard_map/ppermute | solution.py:45
  39.6 3.7 %collective-permute-start.7 = (bf16[2,8,1536]{2,1,0:T(8,128)(2,1)S(1)}, bf16[2,8,1536]{2,1,0:T(8,128)(2,1)S(1)}, u32[]{:S(2)}, u32[]{:S(2)}) collective-permute-start(bf16[2,8,1536]{2,1,0:T(8,128)(2,1)S(1)} %pad_maximum_fusion.10), channel_id=1, source_target_pairs={{0,128},{64,192},{128,0},{192,64},{256,384},{320,448},{384,256},{4... | collective-permute-start | bytes 147464 | tf_op jit(solution)/shard_map/ppermute | solution.py:45
  44.0 2.5 %collective-permute-done.7 = bf16[2,8,1536]{2,1,0:T(8,128)(2,1)S(1)} collective-permute-done((bf16[2,8,1536]{2,1,0:T(8,128)(2,1)S(1)}, bf16[2,8,1536]{2,1,0:T(8,128)(2,1)S(1)}, u32[]{:S(2)}, u32[]{:S(2)}) %collective-permute-start.7) | collective-permute-done | bytes 49184 | tf_op jit(solution)/shard_map/ppermute | solution.py:45
  46.9 1.7 %shard_map.76 = bf16[4,128,384]{2,1,0:T(8,128)(2,1)} custom-call(bf16[64,1536]{1,0:T(8,128)(2,1)S(1)} %bitcast.74, bf16[64,1536]{1,0:T(8,128)(2,1)S(1)} %collective-permute-done.x1, bf16[64,1536]{1,0:T(8,128)(2,1)S(1)} %collective-permute-done.1.x2, bf16[64,1536]{1,0:T(8,128)(2,1)S(1)} %collective-permute-done.2.x3, bf16[384,1536]{1,0:T(8,128)(2,1)S(1)} %copy-done, ...), custom_call_target="tpu_custom_call" | custom-call | flops 603979776 | bytes 3538944 | tf_op jit(solution)/shard_map/pallas_call | solution.py:67
  48.7 4.6 %all-to-all-start.1 = ((bf16[4,128,384]{2,1,0:T(8,128)(2,1)}), bf16[4,128,384]{2,1,0:T(8,128)(2,1)S(1)}, u32[]{:S(2)}, u32[]{:S(2)}) async-start(bf16[4,128,384]{2,1,0:T(8,128)(2,1)} %shard_map.76), calls=%async_computation.1 | async-start | bytes 786432 | tf_op jit(solution)/shard_map/all_to_all | solution.py:155
  54.2 2.5 %collective-permute-start.8 = (bf16[2,2,8,1536]{3,2,0,1:T(8,128)(2,1)S(1)}, bf16[2,2,8,1536]{3,2,0,1:T(8,128)(2,1)S(1)}, u32[]{:S(2)}, u32[]{:S(2)}) collective-permute-start(bf16[2,2,8,1536]{3,2,0,1:T(8,128)(2,1)S(1)} %pad_maximum_fusion.6), channel_id=1, source_target_pairs={{0,64},{64,0},{128,192},{192,128},{256,320},{320,256},{384,448},{4... | collective-permute-start | bytes 294920 | tf_op jit(solution)/shard_map/ppermute | solution.py:45
  56.7 1.9 %collective-permute-start.10 = (bf16[1536,384]{1,0:T(8,128)(2,1)S(1)}, bf16[1536,384]{1,0:T(8,128)(2,1)}, u32[]{:S(2)}, u32[]{:S(2)}) collective-permute-start(bf16[1536,384]{1,0:T(8,128)(2,1)S(1)} %copy-done.1), channel_id=1, source_target_pairs={{0,8},{8,0},{1,9},{9,1},{2,10},{10,2},{3,11},{11,3},{4,12},{12,4},... | collective-permute-start | bytes 3538952 | tf_op jit(solution)/shard_map/ppermute | solution.py:31
  58.6 2.6 %all-to-all-done.1 = bf16[4,128,384]{2,1,0:T(8,128)(2,1)S(1)} async-done(((bf16[4,128,384]{2,1,0:T(8,128)(2,1)}), bf16[4,128,384]{2,1,0:T(8,128)(2,1)S(1)}, u32[]{:S(2)}, u32[]{:S(2)}) %all-to-all-start.1) | async-done | bytes 393248 | tf_op jit(solution)/shard_map/all_to_all | solution.py:155
  61.3 8.2 %collective-permute-start.5 = (bf16[192,384]{1,0:T(8,128)(2,1)S(1)}, bf16[192,384]{1,0:T(8,128)(2,1)S(1)}, u32[]{:S(2)}, u32[]{:S(2)}) collective-permute-start(bf16[192,384]{1,0:T(8,128)(2,1)S(1)} %pad_maximum_fusion.5), channel_id=1, source_target_pairs={{0,4},{4,0},{1,5},{5,1},{2,6},{6,2},{3,7},{7,3},{8,12},{12,8},{9,1... | collective-permute-start | bytes 442376 | tf_op jit(solution)/shard_map/ppermute | solution.py:31
  69.6 2.1 %collective-permute-start.9 = (bf16[64,1536]{1,0:T(8,128)(2,1)S(1)}, bf16[64,1536]{1,0:T(8,128)(2,1)S(1)}, u32[]{:S(2)}, u32[]{:S(2)}) collective-permute-start(bf16[64,1536]{1,0:T(8,128)(2,1)S(1)} %bitcast.76), channel_id=1, source_target_pairs={{0,16},{16,0},{32,48},{48,32},{1,17},{17,1},{33,49},{49,33},{2,18}... | collective-permute-start | bytes 589832 | tf_op jit(solution)/shard_map/ppermute | solution.py:45
  71.8 12.8 %collective-permute-done.5 = bf16[192,384]{1,0:T(8,128)(2,1)S(1)} collective-permute-done((bf16[192,384]{1,0:T(8,128)(2,1)S(1)}, bf16[192,384]{1,0:T(8,128)(2,1)S(1)}, u32[]{:S(2)}, u32[]{:S(2)}) %collective-permute-start.5) | collective-permute-done | bytes 147488 | tf_op jit(solution)/shard_map/ppermute | solution.py:31
  85.9 5.3 %all-to-all-start.2 = ((bf16[4,2,128,384]{3,2,1,0:T(8,128)(2,1)}), bf16[4,2,128,384]{3,2,1,0:T(8,128)(2,1)S(1)}, u32[]{:S(2)}, u32[]{:S(2)}) async-start(bf16[4,2,128,384]{3,2,1,0:T(8,128)(2,1)} %broadcast_in_dim.5), calls=%async_computation.2 | async-start | bytes 1572864 | tf_op jit(solution)/shard_map/all_to_all | solution.py:27
  91.9 3.1 %collective-permute-start.15 = (bf16[128,1536]{1,0:T(8,128)(2,1)}, bf16[128,1536]{1,0:T(8,128)(2,1)}, u32[]{:S(2)}, u32[]{:S(2)}) collective-permute-start(bf16[128,1536]{1,0:T(8,128)(2,1)} %pad_maximum_fusion.2), channel_id=1, source_target_pairs={{0,32},{16,48},{32,0},{48,16},{1,33},{17,49},{33,1},{49,17},{2,34}... | collective-permute-start | bytes 1179656 | tf_op jit(solution)/shard_map/ppermute | solution.py:45
  95.1 2.1 %collective-permute-start.17 = (bf16[256,1536]{1,0:T(8,128)(2,1)S(1)}, bf16[256,1536]{1,0:T(8,128)(2,1)}, u32[]{:S(2)}, u32[]{:S(2)}) collective-permute-start(bf16[256,1536]{1,0:T(8,128)(2,1)S(1)} %pad_maximum_fusion.1.grad_own), channel_id=1, source_target_pairs={{0,8},{8,0},{1,9},{9,1},{2,10},{10,2},{3,11},{11,3},{4,12},{12,4},... | collective-permute-start | bytes 2359304 | tf_op jit(solution)/shard_map/ppermute | solution.py:31
  97.2 6.1 %all-to-all-done.2.cols = bf16[4,2,128,384]{3,2,1,0:T(8,128)(2,1)S(1)} async-done(((bf16[4,2,128,384]{3,2,1,0:T(8,128)(2,1)}), bf16[4,2,128,384]{3,2,1,0:T(8,128)(2,1)S(1)}, u32[]{:S(2)}, u32[]{:S(2)}) %all-to-all-start.2) | async-done | bytes 786464 | tf_op jit(solution)/shard_map/all_to_all | solution.py:27
  103.3 2.3 %shard_map.77 = (f32[64,1536]{1,0:T(8,128)S(1)}, bf16[64,1536]{1,0:T(8,128)(2,1)S(1)}, bf16[64,1536]{1,0:T(8,128)(2,1)S(1)}, bf16[64,1536]{1,0:T(8,128)(2,1)S(1)}, bf16[2,256,384]{2,1,0:T(8,128)(2,1)S(1)}) custom-call(bf16[4,2,128,384]{3,2,1,0:T(8,128)(2,1)S(1)} %all-to-all-done.2.cols, bf16[1536,384]{1,0:T(8,128)(2,1)S(1)} %copy-done.1, ...), custom_call_target="tpu_custom_call" | custom-call | flops 603979776 | bytes 4521984 | tf_op jit(solution)/shard_map/pallas_call | solution.py:67
  105.6 4.1 %collective-permute-start.13 = (bf16[64,1536]{1,0:T(8,128)(2,1)S(1)}, bf16[64,1536]{1,0:T(8,128)(2,1)S(1)}, u32[]{:S(2)}, u32[]{:S(2)}) collective-permute-start(bf16[64,1536]{1,0:T(8,128)(2,1)S(1)} %get-tuple-element.36), channel_id=1, source_target_pairs={{0,48},{16,32},{32,16},{48,0},{1,49},{17,33},{33,17},{49,1},{2,50}... | collective-permute-start | bytes 589832 | tf_op jit(solution)/shard_map/ppermute | solution.py:45
  109.8 1.9 %collective-permute-start.12 = (bf16[64,1536]{1,0:T(8,128)(2,1)S(1)}, bf16[64,1536]{1,0:T(8,128)(2,1)S(1)}, u32[]{:S(2)}, u32[]{:S(2)}) collective-permute-start(bf16[64,1536]{1,0:T(8,128)(2,1)S(1)} %get-tuple-element.35), channel_id=1, source_target_pairs={{0,32},{16,48},{32,0},{48,16},{1,33},{17,49},{33,1},{49,17},{2,34}... | collective-permute-start | bytes 589832 | tf_op jit(solution)/shard_map/ppermute | solution.py:45
  111.7 3.8 %collective-permute-start.11 = (bf16[64,1536]{1,0:T(8,128)(2,1)S(1)}, bf16[64,1536]{1,0:T(8,128)(2,1)S(1)}, u32[]{:S(2)}, u32[]{:S(2)}) collective-permute-start(bf16[64,1536]{1,0:T(8,128)(2,1)S(1)} %get-tuple-element.34), channel_id=1, source_target_pairs={{0,16},{16,0},{32,48},{48,32},{1,17},{17,1},{33,49},{49,33},{2,18}... | collective-permute-start | bytes 589832 | tf_op jit(solution)/shard_map/ppermute | solution.py:45
  115.5 1.9 %collective-permute-start.14 = (bf16[2,256,384]{2,1,0:T(8,128)(2,1)S(1)}, bf16[2,256,384]{2,1,0:T(8,128)(2,1)S(1)}, u32[]{:S(2)}, u32[]{:S(2)}) collective-permute-start(bf16[2,256,384]{2,1,0:T(8,128)(2,1)S(1)} %get-tuple-element.37), channel_id=1, source_target_pairs={{0,8},{8,0},{1,9},{9,1},{2,10},{10,2},{3,11},{11,3},{4,12},{12,4},... | collective-permute-start | bytes 1179656 | tf_op jit(solution)/shard_map/ppermute | solution.py:31
  118.5 2.4 %collective-permute-start.16 = (bf16[256,1536]{1,0:T(8,128)(2,1)S(1)}, bf16[256,1536]{1,0:T(8,128)(2,1)S(1)}, u32[]{:S(2)}, u32[]{:S(2)}) collective-permute-start(bf16[256,1536]{1,0:T(8,128)(2,1)S(1)} %pad_maximum_fusion.block_own), channel_id=1, source_target_pairs={{0,8},{8,0},{1,9},{9,1},{2,10},{10,2},{3,11},{11,3},{4,12},{12,4},... | collective-permute-start | bytes 2359304 | tf_op jit(solution)/shard_map/ppermute | solution.py:31
  121.7 5.9 %all-to-all-start.3 = ((bf16[8,8,1536]{2,1,0:T(8,128)(2,1)}), bf16[8,8,1536]{2,1,0:T(8,128)(2,1)}, u32[]{:S(2)}, u32[]{:S(2)}) async-start(bf16[8,8,1536]{2,1,0:T(8,128)(2,1)} %bitcast.79), calls=%async_computation.3 | async-start | bytes 393216 | tf_op jit(solution)/shard_map/all_to_all | solution.py:191
  127.6 2.9 %shard_map.79 = bf16[384,1536]{1,0:T(8,128)(2,1)} custom-call(bf16[4,2,128,384]{3,2,1,0:T(8,128)(2,1)S(1)} %all-to-all-done.2.cols, bf16[2,256,384]{2,1,0:T(8,128)(2,1)S(1)} %collective-permute-done.14.far, bf16[256,1536]{1,0:T(8,128)(2,1)S(1)} %pad_maximum_fusion.1.grad_own, bf16[256,1536]{1,0:T(8,128)(2,1)} %collective-permute-done.17.grad_sib), custom_call_target="tpu_custom_call" | custom-call | flops 603979776 | bytes 3932160 | tf_op jit(solution)/shard_map/pallas_call | solution.py:67
  130.5 2.0 %shard_map.78 = bf16[1536,384]{1,0:T(8,128)(2,1)} custom-call(bf16[4,2,128,384]{3,2,1,0:T(8,128)(2,1)S(1)} %all-to-all-done.2.cols, bf16[2,256,384]{2,1,0:T(8,128)(2,1)S(1)} %collective-permute-done.14.far, bf16[256,1536]{1,0:T(8,128)(2,1)S(1)} %pad_maximum_fusion.block_own, bf16[256,1536]{1,0:T(8,128)(2,1)S(1)} %collective-permute-done.16.block_sib), custom_call_target="tpu_custom_call" | custom-call | flops 603979776 | bytes 3932160 | tf_op jit(solution)/shard_map/pallas_call | solution.py:67
  132.6 8.4 %all-to-all-done.3 = bf16[8,8,1536]{2,1,0:T(8,128)(2,1)} async-done(((bf16[8,8,1536]{2,1,0:T(8,128)(2,1)}), bf16[8,8,1536]{2,1,0:T(8,128)(2,1)}, u32[]{:S(2)}, u32[]{:S(2)}) %all-to-all-start.3) | async-done | bytes 196640 | tf_op jit(solution)/shard_map/all_to_all | solution.py:191
  141.0 1.6 %reduce_sum.22 = bf16[8,1536]{1,0:T(8,128)(2,1)} reduce(bf16[8,8,1536]{2,1,0:T(8,128)(2,1)} %all-to-all-done.3, bf16[]{:T(256)} %constant.40.clone.1), dimensions={0}, to_apply=%region_1.2 | reduce | flops 86016 | bytes 221186 | tf_op jit(solution)/shard_map/reduce_sum | solution.py:199
  (70 shorter events, 10.2 us)
Async XLA Ops:
  0.6 46.3 %copy-start = (bf16[384,1536]{1,0:T(8,128)(2,1)S(1)}, bf16[384,1536]{1,0:T(8,128)(2,1)}, u32[]{:S(2)}) copy-start(bf16[384,1536]{1,0:T(8,128)(2,1)} %w_own.2) | copy-start | bytes 3538948
  2.2 26.2 %all-to-all-start = ((bf16[8,8,1536]{2,1,0:T(8,128)(2,1)}), bf16[8,8,1536]{2,1,0:T(8,128)(2,1)S(1)}, u32[]{:S(2)}, u32[]{:S(2)}) async-start(bf16[8,8,1536]{2,1,0:T(8,128)(2,1)} %broadcast_in_dim.4), calls=%async_computation | async-start | bytes 393216 | tf_op jit(solution)/shard_map/all_to_all | solution.py:131
  14.8 32.1 %collective-permute-start.3 = (bf16[384,1536]{1,0:T(8,128)(2,1)}, bf16[384,1536]{1,0:T(8,128)(2,1)S(1)}, u32[]{:S(2)}, u32[]{:S(2)}) collective-permute-start(bf16[384,1536]{1,0:T(8,128)(2,1)} %w_own.2), channel_id=1, source_target_pairs={{0,8},{8,0},{1,9},{9,1},{2,10},{10,2},{3,11},{11,3},{4,12},{12,4},... | collective-permute-start | bytes 3538952 | tf_op jit(solution)/shard_map/ppermute | solution.py:31
  17.5 22.1 %collective-permute-start.4 = (bf16[4,8,384]{2,1,0:T(8,128)(2,1)S(1)}, bf16[4,8,384]{2,1,0:T(8,128)(2,1)S(1)}, u32[]{:S(2)}, u32[]{:S(2)}) collective-permute-start(bf16[4,8,384]{2,1,0:T(8,128)(2,1)S(1)} %fusion.7), channel_id=1, source_target_pairs={{0,8},{8,0},{1,9},{9,1},{2,10},{10,2},{3,11},{11,3},{4,12},{12,4},... | collective-permute-start | bytes 73736 | tf_op jit(solution)/shard_map/ppermute | solution.py:31
  20.0 16.5 %collective-permute-start.6 = (bf16[8,1536]{1,0:T(8,128)(2,1)}, bf16[8,1536]{1,0:T(8,128)(2,1)S(1)}, u32[]{:S(2)}, u32[]{:S(2)}) collective-permute-start(bf16[8,1536]{1,0:T(8,128)(2,1)} %param.5), channel_id=1, source_target_pairs={{0,256},{64,320},{128,384},{192,448},{256,0},{320,64},{384,128},{4... | collective-permute-start | bytes 73736 | tf_op jit(solution)/shard_map/ppermute | solution.py:45
  28.4 18.5 %collective-permute-start = (bf16[64,1536]{1,0:T(8,128)(2,1)S(1)}, bf16[64,1536]{1,0:T(8,128)(2,1)S(1)}, u32[]{:S(2)}, u32[]{:S(2)}) collective-permute-start(bf16[64,1536]{1,0:T(8,128)(2,1)S(1)} %bitcast.71), channel_id=1, source_target_pairs={{0,16},{16,0},{32,48},{48,32},{1,17},{17,1},{33,49},{49,33},{2,18}... | collective-permute-start | bytes 589832 | tf_op jit(solution)/shard_map/ppermute | solution.py:45
  31.8 15.1 %collective-permute-start.1 = (bf16[64,1536]{1,0:T(8,128)(2,1)S(1)}, bf16[64,1536]{1,0:T(8,128)(2,1)S(1)}, u32[]{:S(2)}, u32[]{:S(2)}) collective-permute-start(bf16[64,1536]{1,0:T(8,128)(2,1)S(1)} %bitcast.72), channel_id=1, source_target_pairs={{0,32},{16,48},{32,0},{48,16},{1,33},{17,49},{33,1},{49,17},{2,34}... | collective-permute-start | bytes 589832 | tf_op jit(solution)/shard_map/ppermute | solution.py:45
  36.4 10.5 %collective-permute-start.2 = (bf16[64,1536]{1,0:T(8,128)(2,1)S(1)}, bf16[64,1536]{1,0:T(8,128)(2,1)S(1)}, u32[]{:S(2)}, u32[]{:S(2)}) collective-permute-start(bf16[64,1536]{1,0:T(8,128)(2,1)S(1)} %bitcast.73), channel_id=1, source_target_pairs={{0,48},{16,32},{32,16},{48,0},{1,49},{17,33},{33,17},{49,1},{2,50}... | collective-permute-start | bytes 589832 | tf_op jit(solution)/shard_map/ppermute | solution.py:45
  39.6 9.1 %copy-start.6 = (bf16[1,8,1536]{2,1,0:T(8,128)(2,1)}, bf16[1,8,1536]{2,1,0:T(8,128)(2,1)S(1)}, u32[]{:S(2)}) copy-start(bf16[1,8,1536]{2,1,0:T(8,128)(2,1)S(1)} %get-tuple-element.53) | copy-start | bytes 73732
  39.6 9.1 %copy-start.7 = (bf16[1,8,1536]{2,1,0:T(8,128)(2,1)}, bf16[1,8,1536]{2,1,0:T(8,128)(2,1)S(1)}, u32[]{:S(2)}) copy-start(bf16[1,8,1536]{2,1,0:T(8,128)(2,1)S(1)} %get-tuple-element.54) | copy-start | bytes 73732
  39.6 9.0 %copy-start.9 = (bf16[4,8,384]{2,1,0:T(8,128)(2,1)}, bf16[4,8,384]{2,1,0:T(8,128)(2,1)S(1)}, u32[]{:S(2)}) copy-start(bf16[4,8,384]{2,1,0:T(8,128)(2,1)S(1)} %collective-permute-done.4) | copy-start | bytes 73732
  39.6 6.9 %collective-permute-start.7 = (bf16[2,8,1536]{2,1,0:T(8,128)(2,1)S(1)}, bf16[2,8,1536]{2,1,0:T(8,128)(2,1)S(1)}, u32[]{:S(2)}, u32[]{:S(2)}) collective-permute-start(bf16[2,8,1536]{2,1,0:T(8,128)(2,1)S(1)} %pad_maximum_fusion.10), channel_id=1, source_target_pairs={{0,128},{64,192},{128,0},{192,64},{256,384},{320,448},{384,256},{4... | collective-permute-start | bytes 147464 | tf_op jit(solution)/shard_map/ppermute | solution.py:45
  48.7 12.6 %copy-start.8 = (bf16[2,4,8,384]{3,2,1,0:T(8,128)(2,1)S(1)}, bf16[2,4,8,384]{3,2,1,0:T(8,128)(2,1)}, u32[]{:S(2)}) copy-start(bf16[2,4,8,384]{3,2,1,0:T(8,128)(2,1)} %pad_maximum_fusion.8) | copy-start | bytes 147460
  48.7 12.5 %all-to-all-start.1 = ((bf16[4,128,384]{2,1,0:T(8,128)(2,1)}), bf16[4,128,384]{2,1,0:T(8,128)(2,1)S(1)}, u32[]{:S(2)}, u32[]{:S(2)}) async-start(bf16[4,128,384]{2,1,0:T(8,128)(2,1)} %shard_map.76), calls=%async_computation.1 | async-start | bytes 786432 | tf_op jit(solution)/shard_map/all_to_all | solution.py:155
  54.2 30.5 %copy-start.10 = (bf16[4,8,384]{2,1,0:T(8,128)(2,1)S(1)}, bf16[4,8,384]{2,1,0:T(8,128)(2,1)}, u32[]{:S(2)}) copy-start(bf16[4,8,384]{2,1,0:T(8,128)(2,1)} %copy-done.9) | copy-start | bytes 73732
  54.2 30.4 %copy-start.11 = (bf16[1,1,32,384]{3,2,0,1:T(8,128)(2,1)S(1)}, bf16[1,1,32,384]{3,2,0,1:T(8,128)(2,1)}, u32[]{:S(2)}) copy-start(bf16[1,1,32,384]{3,2,0,1:T(8,128)(2,1)} %get-tuple-element.55) | copy-start | bytes 73732
  54.2 15.3 %collective-permute-start.8 = (bf16[2,2,8,1536]{3,2,0,1:T(8,128)(2,1)S(1)}, bf16[2,2,8,1536]{3,2,0,1:T(8,128)(2,1)S(1)}, u32[]{:S(2)}, u32[]{:S(2)}) collective-permute-start(bf16[2,2,8,1536]{3,2,0,1:T(8,128)(2,1)S(1)} %pad_maximum_fusion.6), channel_id=1, source_target_pairs={{0,64},{64,0},{128,192},{192,128},{256,320},{320,256},{384,448},{4... | collective-permute-start | bytes 294920 | tf_op jit(solution)/shard_map/ppermute | solution.py:45
  56.7 40.5 %collective-permute-start.10 = (bf16[1536,384]{1,0:T(8,128)(2,1)S(1)}, bf16[1536,384]{1,0:T(8,128)(2,1)}, u32[]{:S(2)}, u32[]{:S(2)}) collective-permute-start(bf16[1536,384]{1,0:T(8,128)(2,1)S(1)} %copy-done.1), channel_id=1, source_target_pairs={{0,8},{8,0},{1,9},{9,1},{2,10},{10,2},{3,11},{11,3},{4,12},{12,4},... | collective-permute-start | bytes 3538952 | tf_op jit(solution)/shard_map/ppermute | solution.py:31
  61.3 23.3 %collective-permute-start.5 = (bf16[192,384]{1,0:T(8,128)(2,1)S(1)}, bf16[192,384]{1,0:T(8,128)(2,1)S(1)}, u32[]{:S(2)}, u32[]{:S(2)}) collective-permute-start(bf16[192,384]{1,0:T(8,128)(2,1)S(1)} %pad_maximum_fusion.5), channel_id=1, source_target_pairs={{0,4},{4,0},{1,5},{5,1},{2,6},{6,2},{3,7},{7,3},{8,12},{12,8},{9,1... | collective-permute-start | bytes 442376 | tf_op jit(solution)/shard_map/ppermute | solution.py:31
  69.6 21.6 %copy-start.2 = (bf16[2,2,2,8,1536]{4,3,2,1,0:T(8,128)(2,1)}, bf16[2,2,2,8,1536]{4,3,2,1,0:T(8,128)(2,1)S(1)}, u32[]{:S(2)}) copy-start(bf16[2,2,2,8,1536]{4,3,2,1,0:T(8,128)(2,1)S(1)} %copy.15) | copy-start | bytes 589828
  69.6 15.3 %collective-permute-start.9 = (bf16[64,1536]{1,0:T(8,128)(2,1)S(1)}, bf16[64,1536]{1,0:T(8,128)(2,1)S(1)}, u32[]{:S(2)}, u32[]{:S(2)}) collective-permute-start(bf16[64,1536]{1,0:T(8,128)(2,1)S(1)} %bitcast.76), channel_id=1, source_target_pairs={{0,16},{16,0},{32,48},{48,32},{1,17},{17,1},{33,49},{49,33},{2,18}... | collective-permute-start | bytes 589832 | tf_op jit(solution)/shard_map/ppermute | solution.py:45
  85.9 17.4 %all-to-all-start.2 = ((bf16[4,2,128,384]{3,2,1,0:T(8,128)(2,1)}), bf16[4,2,128,384]{3,2,1,0:T(8,128)(2,1)S(1)}, u32[]{:S(2)}, u32[]{:S(2)}) async-start(bf16[4,2,128,384]{3,2,1,0:T(8,128)(2,1)} %broadcast_in_dim.5), calls=%async_computation.2 | async-start | bytes 1572864 | tf_op jit(solution)/shard_map/all_to_all | solution.py:27
  91.9 23.5 %collective-permute-start.15 = (bf16[128,1536]{1,0:T(8,128)(2,1)}, bf16[128,1536]{1,0:T(8,128)(2,1)}, u32[]{:S(2)}, u32[]{:S(2)}) collective-permute-start(bf16[128,1536]{1,0:T(8,128)(2,1)} %pad_maximum_fusion.2), channel_id=1, source_target_pairs={{0,32},{16,48},{32,0},{48,16},{1,33},{17,49},{33,1},{49,17},{2,34}... | collective-permute-start | bytes 1179656 | tf_op jit(solution)/shard_map/ppermute | solution.py:45
  95.1 22.3 %copy-start.3 = (bf16[2,2,2,8,1536]{4,3,2,1,0:T(8,128)(2,1)S(1)}, bf16[2,2,2,8,1536]{4,3,2,1,0:T(8,128)(2,1)}, u32[]{:S(2)}) copy-start(bf16[2,2,2,8,1536]{4,3,2,1,0:T(8,128)(2,1)} %copy-done.2) | copy-start | bytes 589828
  95.1 22.3 %copy-start.5 = (bf16[64,1536]{1,0:T(8,128)(2,1)S(1)}, bf16[64,1536]{1,0:T(8,128)(2,1)}, u32[]{:S(2)}) copy-start(bf16[64,1536]{1,0:T(8,128)(2,1)} %copy-done.4) | copy-start | bytes 589828
  95.1 32.5 %collective-permute-start.17 = (bf16[256,1536]{1,0:T(8,128)(2,1)S(1)}, bf16[256,1536]{1,0:T(8,128)(2,1)}, u32[]{:S(2)}, u32[]{:S(2)}) collective-permute-start(bf16[256,1536]{1,0:T(8,128)(2,1)S(1)} %pad_maximum_fusion.1.grad_own), channel_id=1, source_target_pairs={{0,8},{8,0},{1,9},{9,1},{2,10},{10,2},{3,11},{11,3},{4,12},{12,4},... | collective-permute-start | bytes 2359304 | tf_op jit(solution)/shard_map/ppermute | solution.py:31
  105.6 12.9 %collective-permute-start.13 = (bf16[64,1536]{1,0:T(8,128)(2,1)S(1)}, bf16[64,1536]{1,0:T(8,128)(2,1)S(1)}, u32[]{:S(2)}, u32[]{:S(2)}) collective-permute-start(bf16[64,1536]{1,0:T(8,128)(2,1)S(1)} %get-tuple-element.36), channel_id=1, source_target_pairs={{0,48},{16,32},{32,16},{48,0},{1,49},{17,33},{33,17},{49,1},{2,50}... | collective-permute-start | bytes 589832 | tf_op jit(solution)/shard_map/ppermute | solution.py:45
  109.8 11.1 %collective-permute-start.12 = (bf16[64,1536]{1,0:T(8,128)(2,1)S(1)}, bf16[64,1536]{1,0:T(8,128)(2,1)S(1)}, u32[]{:S(2)}, u32[]{:S(2)}) collective-permute-start(bf16[64,1536]{1,0:T(8,128)(2,1)S(1)} %get-tuple-element.35), channel_id=1, source_target_pairs={{0,32},{16,48},{32,0},{48,16},{1,33},{17,49},{33,1},{49,17},{2,34}... | collective-permute-start | bytes 589832 | tf_op jit(solution)/shard_map/ppermute | solution.py:45
  111.7 9.3 %collective-permute-start.11 = (bf16[64,1536]{1,0:T(8,128)(2,1)S(1)}, bf16[64,1536]{1,0:T(8,128)(2,1)S(1)}, u32[]{:S(2)}, u32[]{:S(2)}) collective-permute-start(bf16[64,1536]{1,0:T(8,128)(2,1)S(1)} %get-tuple-element.34), channel_id=1, source_target_pairs={{0,16},{16,0},{32,48},{48,32},{1,17},{17,1},{33,49},{49,33},{2,18}... | collective-permute-start | bytes 589832 | tf_op jit(solution)/shard_map/ppermute | solution.py:45
  115.5 6.3 %collective-permute-start.14 = (bf16[2,256,384]{2,1,0:T(8,128)(2,1)S(1)}, bf16[2,256,384]{2,1,0:T(8,128)(2,1)S(1)}, u32[]{:S(2)}, u32[]{:S(2)}) collective-permute-start(bf16[2,256,384]{2,1,0:T(8,128)(2,1)S(1)} %get-tuple-element.37), channel_id=1, source_target_pairs={{0,8},{8,0},{1,9},{9,1},{2,10},{10,2},{3,11},{11,3},{4,12},{12,4},... | collective-permute-start | bytes 1179656 | tf_op jit(solution)/shard_map/ppermute | solution.py:31
  118.5 12.1 %collective-permute-start.16 = (bf16[256,1536]{1,0:T(8,128)(2,1)S(1)}, bf16[256,1536]{1,0:T(8,128)(2,1)S(1)}, u32[]{:S(2)}, u32[]{:S(2)}) collective-permute-start(bf16[256,1536]{1,0:T(8,128)(2,1)S(1)} %pad_maximum_fusion.block_own), channel_id=1, source_target_pairs={{0,8},{8,0},{1,9},{9,1},{2,10},{10,2},{3,11},{11,3},{4,12},{12,4},... | collective-permute-start | bytes 2359304 | tf_op jit(solution)/shard_map/ppermute | solution.py:31
  121.7 19.3 %all-to-all-start.3 = ((bf16[8,8,1536]{2,1,0:T(8,128)(2,1)}), bf16[8,8,1536]{2,1,0:T(8,128)(2,1)}, u32[]{:S(2)}, u32[]{:S(2)}) async-start(bf16[8,8,1536]{2,1,0:T(8,128)(2,1)} %bitcast.79), calls=%async_computation.3 | async-start | bytes 393216 | tf_op jit(solution)/shard_map/all_to_all | solution.py:191
  (3 other events, 16.5 us)
